TPU v7x, 256 devices: a whole 4x4x8 slice. The times are simulated.
256 devices in a mesh: gy: 32 (over z, x), gz: 8 (over y, core).
Axes of the slice: x: 4, y: 4, z: 8, core: 2. Of those that a mesh axis runs over, the one named last changes fastest.
Arguments:
- heat_scalar_window: float32 [512, 64, 2048], P('gy', 'gz'), may hold values from -6 to 6
- flow_speed_vector: bfloat16 [3, 512, 64, 2048], P(None, 'gy', 'gz'), may hold values from -4 to 4
Outputs:
- updated: float32 [512, 64, 2048], P('gy', 'gz')
All inputs are finite; a program needn't handle non-finite values.
Results may differ from a plain program's by a relative error of at most 0.0003.
Values sent between devices are 32-bit elements; how exact they have to be, the bound alone decides.
No kernel may reach another device: no remote copies, remote signals or barrier semaphores. Data moves between devices by JAX's collectives and lax.ppermute only.
A program may use at most 64 MiB of HBM per device.

v0:
```python
import jax
import jax.numpy as jnp
from jax import lax
from jax.sharding import PartitionSpec as P

XB = 128
RX = 1
RY = 768
RZ = 192


EXACT = lax.Precision.HIGHEST
thermal_conduction_coefficient = 0.15


def extended(cells, sides, width):
    for axis, dim in sides:
        count = lax.axis_size(axis)
        ends = count - 1
        head = lax.slice_in_dim(cells, 0, width, axis=dim)
        tail = lax.slice_in_dim(cells, cells.shape[dim] - width, cells.shape[dim], axis=dim)
        cells = jnp.concatenate(
            [
                lax.ppermute(tail, axis, [(i, (i + 1) % count) for i in range(ends)]),
                cells,
                lax.ppermute(head, axis, [((i + 1) % count, i) for i in range(ends)]),
            ],
            axis=dim,
        )
    return cells


def prefix(value, axis, join, neutral, backward):
    count, mine = (lax.axis_size(axis), lax.axis_index(axis))
    pieces = jax.tree.map(lambda part: lax.all_gather(part, axis), value)
    if backward:
        pieces = jax.tree.map(lambda part: part[::-1], pieces)
        mine = count - 1 - mine
    so_far = jax.tree.map(
        lambda part, zero: jnp.full_like(part, 0) + jnp.asarray(zero, part.dtype), value, neutral
    )

    def hop(position, so_far):
        longer = join(so_far, jax.tree.map(lambda part: part[position], pieces))
        return jax.tree.map(lambda new, old: jnp.where(position < mine, new, old), longer, so_far)

    return lax.fori_loop(0, count - 1, hop, so_far)


def line_inverse(line_count, ratio_value):
    coupling = jnp.float32(ratio_value)
    half_step = 0.5 / coupling
    decay_base = 1.0 + half_step - jnp.sqrt(half_step * (2.0 + half_step))
    places = jnp.arange(line_count, dtype=jnp.float32)
    small_index = jnp.minimum(places[:, None], places[None, :])
    large_index = jnp.maximum(places[:, None], places[None, :])
    span_value = jnp.float32(line_count)
    numer = (
        decay_base ** (large_index - small_index + 1.0)
        * (1.0 - decay_base ** (2.0 * (small_index + 1.0)))
        * (1.0 - decay_base ** (2.0 * (span_value - large_index)))
    )
    denom = (
        coupling * (1.0 - decay_base * decay_base) * (1.0 - decay_base ** (2.0 * span_value + 2.0))
    )
    return numer / denom


def product_two(left_two, right_two):
    return jnp.sum(left_two[:, :, None] * right_two[None, :, :], axis=1)


def apply_two(matrix, vector):
    return jnp.stack(
        [
            matrix[0, 0] * vector[0] + matrix[0, 1] * vector[1],
            matrix[1, 0] * vector[0] + matrix[1, 1] * vector[1],
        ]
    )


def inverse_two(matrix):
    determinant = matrix[0, 0] * matrix[1, 1] - matrix[0, 1] * matrix[1, 0]
    return (
        jnp.stack(
            [jnp.stack([matrix[1, 1], -matrix[0, 1]]), jnp.stack([-matrix[1, 0], matrix[0, 0]])]
        )
        / determinant
    )


def couplers(inverse_block, ratio_value):
    near_value = ratio_value * inverse_block[0, 0]
    far_value = ratio_value * inverse_block[0, -1]
    zero_value = jnp.zeros_like(near_value)
    lower_map = jnp.stack([jnp.stack([zero_value, near_value]), jnp.stack([zero_value, far_value])])
    upper_map = jnp.stack([jnp.stack([far_value, zero_value]), jnp.stack([near_value, zero_value])])
    return (lower_map, upper_map)


def reduced_factors(lower_map, upper_map, line_count):
    unit_two = jnp.eye(2, dtype=jnp.float32)

    def advance(earlier_value, ignored):
        following = inverse_two(
            unit_two - product_two(product_two(lower_map, earlier_value), upper_map)
        )
        return (following, following)

    final_value, remaining = lax.scan(advance, unit_two, None, length=line_count - 1)
    return jnp.concatenate([unit_two[None], remaining], axis=0)


def solve_chain(stacked, dinvs, lower_map, upper_map):

    def forward(earlier_value, inputs):
        source_value, factor_prior = inputs
        following = source_value + apply_two(product_two(lower_map, factor_prior), earlier_value)
        return (following, following)

    first_value = stacked[0]
    final_value, remaining = lax.scan(forward, first_value, (stacked[1:], dinvs[:-1]))
    swept = jnp.concatenate([first_value[None], remaining], axis=0)
    end_value = apply_two(dinvs[-1], swept[-1])

    def backward(after_value, inputs):
        swept_value, factor_here = inputs
        current = apply_two(factor_here, swept_value + apply_two(upper_map, after_value))
        return (current, current)

    unused_top, lower_values = lax.scan(backward, end_value, (swept[:-1], dinvs[:-1]), reverse=True)
    solved = jnp.concatenate([lower_values, end_value[None]], axis=0)
    blank_row = jnp.zeros_like(solved[:1, 0])
    before_value = jnp.concatenate([blank_row, solved[:-1, 1]], axis=0)
    after_value = jnp.concatenate([solved[1:, 0], blank_row], axis=0)
    return jnp.stack([before_value, after_value], axis=1)


def compose(earlier, later_map):
    return (
        product_two(later_map[0], earlier[0]),
        apply_two(later_map[0], earlier[1]) + later_map[1],
    )


def on_device(heat_scalar_window, flow_speed_vector):
    haloed_array = extended(heat_scalar_window, (("gy", 0), ("gz", 1)), 1)
    northern_adjacent = haloed_array[2:, 1:-1]
    southern_adjacent = haloed_array[:-2, 1:-1]
    ceiling_adjacent = haloed_array[1:-1, 2:]
    bottom_adjacent = haloed_array[1:-1, :-2]
    haloed_array_east = jnp.pad(heat_scalar_window, ((0, 0), (0, 0), (1, 1)))
    eastern_adjacent = haloed_array_east[:, :, 2:]
    western_adjacent = haloed_array_east[:, :, :-2]
    laplacian_contribution = (
        eastern_adjacent
        + western_adjacent
        + northern_adjacent
        + southern_adjacent
        + ceiling_adjacent
        + bottom_adjacent
        - 6.0 * heat_scalar_window
    )
    retained_remainder = (
        flow_speed_vector[0].astype(jnp.float32) * (eastern_adjacent - western_adjacent)
        + flow_speed_vector[1].astype(jnp.float32) * (northern_adjacent - southern_adjacent)
        + flow_speed_vector[2].astype(jnp.float32) * (ceiling_adjacent - bottom_adjacent)
    )
    forcing_contribution = (
        heat_scalar_window
        + thermal_conduction_coefficient * laplacian_contribution
        - 0.5 * retained_remainder
    )
    northward_extent, vertical_extent, eastward_extent = heat_scalar_window.shape
    block_count = eastward_extent // XB
    unit_two = jnp.eye(2, dtype=jnp.float32)
    inverse_x = line_inverse(XB, RX)
    local_x = jnp.dot(
        forcing_contribution.reshape(northward_extent, vertical_extent, block_count, XB),
        inverse_x,
        precision=EXACT,
    )
    ends_x = jnp.stack([local_x[..., 0], local_x[..., -1]])
    lower_x, upper_x = couplers(inverse_x, RX)
    chained = solve_chain(
        jnp.moveaxis(ends_x, 3, 0), reduced_factors(lower_x, upper_x, block_count), lower_x, upper_x
    )
    before_x = jnp.moveaxis(chained[:, 0], 0, 2)
    after_x = jnp.moveaxis(chained[:, 1], 0, 2)
    along_x = (
        local_x
        + RX * inverse_x[:, 0] * before_x[..., None]
        + RX * inverse_x[:, -1] * after_x[..., None]
    )
    along_x = along_x.reshape(northward_extent, vertical_extent, eastward_extent)
    inverse_y = line_inverse(northward_extent, RY)
    local_y = jnp.einsum("ab,bzx->azx", inverse_y, along_x, precision=EXACT)
    ends_y = jnp.stack([local_y[0], local_y[-1]])
    lower_y, upper_y = couplers(inverse_y, RY)
    dinvs_y = reduced_factors(lower_y, upper_y, lax.axis_size("gy"))
    position = lax.axis_index("gy")
    active = (position > 0).astype(jnp.float32)
    factor_here = dinvs_y[position]
    factor_prior = dinvs_y[jnp.maximum(position - 1, 0)]
    carry_map = product_two(lower_y, factor_prior) * active
    blank_pair = jnp.zeros_like(ends_y)
    prior_value = prefix((carry_map, ends_y), "gy", compose, (unit_two, blank_pair), False)[1]
    swept = ends_y + apply_two(carry_map, prior_value)
    step_back = product_two(factor_here, upper_y)
    offset = apply_two(factor_here, swept)
    after_pair = prefix((step_back, offset), "gy", compose, (unit_two, blank_pair), True)[1]
    own_pair = apply_two(step_back, after_pair) + offset
    before_y = apply_two(factor_prior, prior_value + apply_two(upper_y, own_pair))[1] * active
    after_y = after_pair[0]
    along_y = (
        local_y
        + (RY * inverse_y[:, 0])[:, None, None] * before_y[None]
        + (RY * inverse_y[:, -1])[:, None, None] * after_y[None]
    )
    inverse_z = line_inverse(vertical_extent, RZ)
    local_z = jnp.einsum("ab,ybx->yax", inverse_z, along_y, precision=EXACT)
    ends_z = jnp.stack([local_z[:, 0], local_z[:, -1]])
    lower_z, upper_z = couplers(inverse_z, RZ)
    dinvs_z = reduced_factors(lower_z, upper_z, lax.axis_size("gz"))
    position_z = lax.axis_index("gz")
    active_z = (position_z > 0).astype(jnp.float32)
    factor_here_z = dinvs_z[position_z]
    factor_prior_z = dinvs_z[jnp.maximum(position_z - 1, 0)]
    carry_map_z = product_two(lower_z, factor_prior_z) * active_z
    blank_pair_z = jnp.zeros_like(ends_z)
    prior_value_z = prefix((carry_map_z, ends_z), "gz", compose, (unit_two, blank_pair_z), False)[1]
    swept_z = ends_z + apply_two(carry_map_z, prior_value_z)
    step_back_z = product_two(factor_here_z, upper_z)
    offset_z = apply_two(factor_here_z, swept_z)
    after_pair_z = prefix((step_back_z, offset_z), "gz", compose, (unit_two, blank_pair_z), True)[1]
    own_pair_z = apply_two(step_back_z, after_pair_z) + offset_z
    before_z = (
        apply_two(factor_prior_z, prior_value_z + apply_two(upper_z, own_pair_z))[1] * active_z
    )
    after_z = after_pair_z[0]
    updated = (
        local_z
        + (RZ * inverse_z[:, 0])[None, :, None] * before_z[:, None, :]
        + (RZ * inverse_z[:, -1])[None, :, None] * after_z[:, None, :]
    )
    return updated


def solution(mesh):
    in_specs = (P("gy", "gz", None), P(None, "gy", "gz", None))
    out_specs = P("gy", "gz", None)
    return jax.shard_map(
        on_device, mesh=mesh, in_specs=in_specs, out_specs=out_specs, check_vma=False
    )
```

profile of v0, /device:TPU:1, one launch (start us, length us, event | category | flops | bytes accessed | tf_op | source)
XLA Modules:
  0.0 1106.8 jit_solution(13264224382091304224)
XLA Ops:
  7.4 3.9 collective-permute-start.1
  16.1 106.8 %while.125 = (s32[]{:T(128)}, f32[2,2]{1,0:T(2,128)S(1)}, f32[15,2,2]{2,1,0:T(2,128)S(1)}, f32[2,2]{1,0:T(2,128)S(1)}, f32[2,2]{1,0:T(2,128)S(1)}, /*index=5*/s32[]{:T(128)}) while((s32[]{:T(128)}, f32[2,2]{1,0:T(2,128)S(1)}, f32[15,2,2]{2,1,0:T(2,128)S(1)}, f32[2,2]{1,0:T(2,128)S(1)}, f32[2,2]{1,0:T(2,128)S(1)}, ...), condition=%wide.region_3.4_spmd.clone, body=%wide.region_0.3_spmd.clone.sunk | while | flops 67 | bytes 2437 | solution.py:110
  125.0 220.6 %while.126 = (s32[]{:T(128)}, f32[2,2]{1,0:T(2,128)S(1)}, f32[31,2,2]{2,1,0:T(2,128)S(1)}, f32[2,2]{1,0:T(2,128)S(1)}, f32[2,2]{1,0:T(2,128)S(1)}, /*index=5*/s32[]{:T(128)}) while((s32[]{:T(128)}, f32[2,2]{1,0:T(2,128)S(1)}, f32[31,2,2]{2,1,0:T(2,128)S(1)}, f32[2,2]{1,0:T(2,128)S(1)}, f32[2,2]{1,0:T(2,128)S(1)}, ...), condition=%wide.region_12.13_spmd.clone, body=%wide.region_9.12_spmd.clone.sunk | while | flops 67 | bytes 2437 | solution.py:110
  349.1 2.9 collective-permute-start.2
  352.0 3.1 collective-permute-start.3
  357.2 2.5 fusion.29
  362.2 48.9 %while.123 = (s32[]{:T(128)}, f32[2,16,8]{1,2,0:T(8,128)S(1)}, f32[15,2,16,8]{2,3,1,0:T(8,128)S(1)}, f32[15,2,16,8]{2,3,1,0:T(8,128)S(1)}, f32[2,2]{1,0:T(2,128)S(1)}, /*index=5*/f32[15,2,2]{2,1,0:T(2,128)S(1)}, s32[]{:T(128)}) while((s32[]{:T(128)}, f32[2,16,8]{1,2,0:T(8,128)S(1)}, f32[15,2,16,8]{2,3,1,0:T(8,128)S(1)}, ...), condition=%wide.region_6.7_spmd, body=%wide.region_4.6_spmd.sunk | while | flops 1806 | bytes 29913 | solution.py:122
  413.6 94.8 %while.124 = (s32[]{:T(128)}, f32[2,16,8]{1,2,0:T(8,128)S(1)}, f32[15,2,16,8]{2,3,1,0:T(8,128)S(1)}, f32[15,2,2]{2,1,0:T(2,128)S(1)}, f32[15,2,16,8]{2,3,1,0:T(8...) while((s32[]{:T(128)}, f32[2,16,8]{1,2,0:T(8,128)S(1)}, ...), condition=%wide.region_8.9_spmd, body=%wide.region_7.8_spmd.sunk | while | flops 2307 | bytes 31989 | solution.py:131
  512.2 51.7 %while.127 = (s32[]{:T(128)}, f32[2,2]{1,0:T(2,128)S(1)}, f32[7,2,2]{2,1,0:T(2,128)S(1)}, f32[2,2]{1,0:T(2,128)S(1)}, f32[2,2]{1,0:T(2,128)S(1)}, /*index=5*/s32[]{:T(128)}) while((s32[]{:T(128)}, f32[2,2]{1,0:T(2,128)S(1)}, f32[7,2,2]{2,1,0:T(2,128)S(1)}, f32[2,2]{1,0:T(2,128)S(1)}, f32[2,2]{1,0:T(2,128)S(1)}, ...), condition=%wide.region_22.23_spmd.clone, body=%wide.region_19.22_spmd.clone.sunk | while | flops 67 | bytes 2437 | solution.py:110
  564.4 42.8 %all-gather.8 = f32[32,2,2]{2,1,0:T(2,128)S(1)} all-gather(f32[1,2,2]{2,1,0:T(2,128)S(1)} %fusion.152), channel_id=2, replica_groups=mesh['gy'=32,'gz'=8] {'gy'}, dimensions={0}, use_global_device_ids=true | all-gather | bytes 528 | tf_op jit(solution)/shard_map/all_gather | solution.py:35
  608.5 127.7 %while.128 = (s32[]{:T(128)}, f32[2,8,2048]{2,1,0:T(8,128)S(1)}, s32[]{:T(128)}, f32[32,2,2]{2,1,0:T(2,128)S(1)}, f32[32,2,8,2048]{3,2,1,0:T(8,128)}, /*index=5*/s32[]{:T(128)}, s32[]{:T(128)}) while((s32[]{:T(128)}, f32[2,8,2048]{2,1,0:T(8,128)S(1)}, s32[]{:T(128)}, f32[32,2,2]{2,1,0:T(2,128)S(1)}, ...), condition=%wide.region_15.16_spmd.clone, body=%wide.region_14.15_spmd.clone.sunk | while | flops 262148 | bytes 1048762 | solution.py:47
  736.3 2.7 multiply_add_fusion.32
  739.3 2.6 multiply_add_fusion.30
  742.9 31.4 %all-gather.9 = f32[32,2,2]{2,1,0:T(2,128)S(1)} all-gather(f32[1,2,2]{2,1,0:T(2,128)S(1)} %bitcast.391), channel_id=4, replica_groups=mesh['gy'=32,'gz'=8] {'gy'}, dimensions={0}, use_global_device_ids=true | all-gather | bytes 528 | tf_op jit(solution)/shard_map/all_gather | solution.py:35
  776.8 50.3 %all-gather.19.cloned.1.call-done = f32[64,8,2048]{2,1,0:T(8,128)} async-done(((f32[2,8,2048]{2,1,0:T(8,128)}), f32[64,8,2048]{2,1,0:T(8,128)}) %all-gather.19.cloned.1.call-update) | async-done | bytes 4194320 | tf_op jit(solution)/shard_map/all_gather | solution.py:35
  827.1 4.7 rev.13
  831.8 130.4 %while.129 = (s32[]{:T(128)}, f32[2,8,2048]{2,1,0:T(8,128)S(1)}, s32[]{:T(128)}, f32[32,2,2]{2,1,0:T(2,128)S(1)}, f32[32,2,8,2048]{3,2,1,0:T(8,128)}, /*index=5*/s32[]{:T(128)}, s32[]{:T(128)}) while((s32[]{:T(128)}, f32[2,8,2048]{2,1,0:T(8,128)S(1)}, s32[]{:T(128)}, f32[32,2,2]{2,1,0:T(2,128)S(1)}, ...), condition=%wide.region_18.19_spmd.clone, body=%wide.region_17.18_spmd.clone.sunk | while | flops 262148 | bytes 1048762 | solution.py:47
  832.5 2.5 multiply_add_fusion.44
  836.7 2.5 multiply_add_fusion.44
  840.9 2.5 multiply_add_fusion.44
  845.1 2.5 multiply_add_fusion.44
  849.3 2.5 multiply_add_fusion.44
  853.5 2.5 multiply_add_fusion.44
  857.7 2.5 multiply_add_fusion.44
  861.9 2.5 multiply_add_fusion.44
  866.1 2.5 multiply_add_fusion.44
  870.3 2.5 multiply_add_fusion.44
  874.5 2.5 multiply_add_fusion.44
  878.7 2.5 multiply_add_fusion.44
  882.9 2.5 multiply_add_fusion.44
  887.1 2.5 multiply_add_fusion.44
  891.4 2.5 multiply_add_fusion.44
  895.6 2.5 multiply_add_fusion.44
  899.8 2.5 multiply_add_fusion.44
  904.0 2.5 multiply_add_fusion.44
  908.2 2.5 multiply_add_fusion.44
  912.4 2.5 multiply_add_fusion.44
  916.6 2.5 multiply_add_fusion.44
  920.8 2.5 multiply_add_fusion.44
  925.0 2.5 multiply_add_fusion.44
  929.2 2.5 multiply_add_fusion.44
  933.4 2.5 multiply_add_fusion.44
  937.6 2.5 multiply_add_fusion.44
  941.8 2.5 multiply_add_fusion.44
  946.0 2.5 multiply_add_fusion.44
  950.3 2.5 multiply_add_fusion.44
  954.5 2.5 multiply_add_fusion.44
  958.7 2.5 multiply_add_fusion.44
  962.3 2.6 multiply_add_fusion.28
  973.6 13.6 %all-gather.10 = f32[8,2,2]{2,1,0:T(2,128)S(1)} all-gather(f32[1,2,2]{2,1,0:T(2,128)S(1)} %fusion.151), channel_id=6, replica_groups=mesh['gy'=32,'gz'=8] {'gz'}, dimensions={0}, use_global_device_ids=true | all-gather | bytes 144 | tf_op jit(solution)/shard_map/all_gather | solution.py:35
  988.6 13.2 %all-gather.21.cloned.1.call-done = f32[16,16,2048]{2,1,0:T(8,128)} async-done(((f32[2,16,2048]{2,1,0:T(8,128)}), f32[16,16,2048]{2,1,0:T(8,128)}) %all-gather.21.cloned.1.call-update) | async-done | bytes 2097168 | tf_op jit(solution)/shard_map/all_gather | solution.py:35
  1001.7 28.6 %while.130 = (s32[]{:T(128)}, f32[2,16,2048]{2,1,0:T(8,128)S(1)}, s32[]{:T(128)}, f32[8,2,2]{2,1,0:T(2,128)S(1)}, f32[8,2,16,2048]{3,2,1,0:T(8,128)}, /*index=5*/s32[]{:T(128)}, s32[]{:T(128)}) while((s32[]{:T(128)}, f32[2,16,2048]{2,1,0:T(8,128)S(1)}, s32[]{:T(128)}, f32[8,2,2]{2,1,0:T(2,128)S(1)}, ...), condition=%wide.region_25.26_spmd.clone, body=%wide.region_24.25_spmd.clone.sunk | while | flops 524292 | bytes 2097338 | solution.py:47
  1030.6 2.9 multiply_add_fusion.24
  1033.9 2.7 multiply_add_fusion.22
  1037.9 9.6 all-gather.11
  1050.0 15.9 %all-gather.23.cloned.1.call-done = f32[16,16,2048]{2,1,0:T(8,128)} async-done(((f32[2,16,2048]{2,1,0:T(8,128)}), f32[16,16,2048]{2,1,0:T(8,128)}) %all-gather.23.cloned.1.call-update) | async-done | bytes 2097168 | tf_op jit(solution)/shard_map/all_gather | solution.py:35
  1067.7 23.1 %while.131 = (s32[]{:T(128)}, f32[2,16,2048]{2,1,0:T(8,128)S(1)}, s32[]{:T(128)}, f32[8,2,2]{2,1,0:T(2,128)S(1)}, f32[8,2,16,2048]{3,2,1,0:T(8,128)S(1)}, /*index=5*/s32[]{:T(128)}, s32[]{:T(128)}) while((s32[]{:T(128)}, f32[2,16,2048]{2,1,0:T(8,128)S(1)}, s32[]{:T(128)}, f32[8,2,2]{2,1,0:T(2,128)S(1)}, ...), condition=%wide.region_28.29_spmd.clone, body=%wide.region_27.28_spmd.clone.sunk | while | flops 524292 | bytes 2097338 | solution.py:47
  1068.4 2.5 multiply_add_fusion.46
  1071.7 2.5 multiply_add_fusion.46
  1075.0 2.5 multiply_add_fusion.46
  1078.3 2.5 multiply_add_fusion.46
  1081.6 2.5 multiply_add_fusion.46
  1091.0 2.8 multiply_add_fusion.20
  1094.3 2.9 multiply_add_fusion.18
  (1101 shorter events, 588.5 us)
Async XLA Ops:
  6.5 602.0 %all-gather.17.cloned.1.call-start = ((), (), s32[]{:S(2)}) async-start(), calls=%async_computation | async-start | bytes 4325376 | tf_op jit(solution)/shard_map/all_gather | solution.py:35
  7.4 340.2 %collective-permute-start.1 = (f32[1,8,2048]{2,1,0:T(8,128)S(1)}, f32[1,8,2048]{2,1,0:T(8,128)S(1)}, u32[]{:S(2)}, u32[]{:S(2)}) collective-permute-start(f32[1,8,2048]{2,1,0:T(8,128)S(1)} %get-tuple-element.1035), channel_id=1, source_target_pairs={{0,8},{8,16},{16,24},{24,32},{32,40},{40,48},{48,56},{56,64},{64,7... | collective-permute-start | bytes 196616 | tf_op jit(solution)/shard_map/ppermute | solution.py:24
  11.4 337.5 %collective-permute-start = (f32[1,8,2048]{2,1,0:T(8,128)S(1)}, f32[1,8,2048]{2,1,0:T(8,128)S(1)}, u32[]{:S(2)}, u32[]{:S(2)}) collective-permute-start(f32[1,8,2048]{2,1,0:T(8,128)S(1)} %get-tuple-element.1034), channel_id=1, source_target_pairs={{8,0},{16,8},{24,16},{32,24},{40,32},{48,40},{56,48},{64,56},{72,6... | collective-permute-start | bytes 196616 | tf_op jit(solution)/shard_map/ppermute | solution.py:26
  345.7 11.5 %copy-start.2 = (f32[16,8,2048]{2,1,0:T(8,128)S(1)}, f32[16,8,2048]{2,1,0:T(8,128)}, u32[]{:S(2)}) copy-start(f32[16,8,2048]{2,1,0:T(8,128)} %param.20) | copy-start | bytes 3145732
  349.1 6.9 collective-permute-start.2
  352.0 5.2 collective-permute-start.3
  512.0 315.1 %all-gather.19.cloned.1.call-start = ((), (), s32[]{:S(2)}) async-start(), calls=%async_computation.1 | async-start | bytes 4325376 | tf_op jit(solution)/shard_map/all_gather | solution.py:35
  742.7 259.0 %all-gather.21.cloned.1.call-start = ((), (), s32[]{:S(2)}) async-start(), calls=%async_computation.2 | async-start | bytes 2359296 | tf_op jit(solution)/shard_map/all_gather | solution.py:35
  971.1 1.0 copy-start
  973.4 92.5 %all-gather.23.cloned.1.call-start = ((), (), s32[]{:S(2)}) async-start(), calls=%async_computation.3 | async-start | bytes 2359296 | tf_op jit(solution)/shard_map/all_gather | solution.py:35
  1093.8 5.2 copy-start.1
Sparse Core Ops, SparseCore 0:
  512.1 84.8 all-gather.16
  742.9 84.1 all-gather.18
  973.5 28.1 all-gather.20
  1037.9 28.0 all-gather.22
where the time goes:
time: 1120 us; the launch traced here: 1110 us
  other arithmetic  560 us (50%)
  loops' own time  198 us (18%)
  local copies, waits for them, and re-layouts  139 us (12%)
  blocking collectives  97.5 us (9%)
  waiting for transfers between devices  80.7 us (7%)
  between operations  16.4 us (1%)
  starting transfers between devices  11.3 us (1%)
    add x130, other arithmetic, apply_two(): matrix[0, 0] * vector[0] + matrix[0, 1] * vector[1]  324 us
    another operation x3, loops' own time, reduced_factors(): lax.scan(advance, unit_two, None, length=line_count - 1)  193 us
    another operation x106, other arithmetic, inverse_two(): jnp.stack([jnp.stack([matrix[1, 1], -matrix[0, 1]]), jnp.stack([-matrix[1...  141 us
    all_gather x4, blocking collectives, prefix(): pieces = jax.tree.map(lambda part: lax.all_gather(part, axis), value)  97.5 us
    slice x130, local copies, waits for them, and re-layouts, apply_two(): matrix[0, 0] * vector[0] + matrix[0, 1] * vector[1]  84.6 us
    all_gather x4, waiting for transfers between devices, prefix(): pieces = jax.tree.map(lambda part: lax.all_gather(part, axis), value)  79.4 us
    select_n x76, other arithmetic, hop(): jnp.where(position < mine, new, old)  66.8 us
    slice x53, local copies, waits for them, and re-layouts, inverse_two(): matrix[1, 1]  33.3 us
  transfers between devices with their start and end apart: 8, of which 5 were waited for; matrix products, arithmetic and copies ran while one was open for 18% of the time, Pallas kernels for 0%

commit v1 on v0

v1 whole, which is shorter than its diff:
```python
import jax
import jax.numpy as jnp
import numpy as np
from jax import lax
from jax.experimental import pallas as pl
from jax.experimental.pallas import tpu as pltpu
from jax.sharding import PartitionSpec as P

NX, NY, NZ = 2048, 512, 64
RX, RY, RZ = 1, 768, 192
DY, DZ = 32, 8
LY, LZ = NY // DY, NZ // DZ
XB = 256
NB = NX // XB
KAPPA = 0.15
F32, BF16 = jnp.float32, jnp.bfloat16


def decay(ratio):
    half = 0.5 / ratio
    return 1.0 + half - np.sqrt(half * (2.0 + half))


def line_factors(count, ratio):
    q = decay(ratio)
    i = np.arange(count)
    low = 1.0 - q ** (2.0 * (i + 1))
    high = 1.0 - q ** (2.0 * (count - i))
    denom = ratio * (1.0 - q * q) * (1.0 - q ** (2.0 * count + 2))
    return q, low, high, denom


def split_line(count, ratio, parts):
    q, low, high, denom = line_factors(count, ratio)
    size = count // parts
    low, high = low.reshape(parts, size), high.reshape(parts, size)
    m = np.arange(size)
    small = np.minimum(m[:, None], m[None])
    large = np.maximum(m[:, None], m[None])
    block = q ** (large - small + 1.0) * low[:, small] * high[:, large] / denom
    up = q ** (size - 1.0 - m) * low
    down = q ** (1.0 * m) * high
    from_low = q ** (m + 2.0) * high / denom
    from_high = q ** (size + 1.0 - m) * low / denom
    return block, up, down, from_low, from_high, q**size


def tables():
    block_y, up_y, down_y, gl_y, gh_y, step_y = split_line(NY, RY, DY)
    block_z, up_z, down_z, gl_z, gh_z, step_z = split_line(NZ, RZ, DZ)
    ty = np.zeros((DY, 24, 128))
    ty[:, :LY] = np.repeat(block_y, LZ, axis=2)
    ty[:, LY] = np.repeat(up_y, LZ, axis=1)
    ty[:, LY + 1] = np.repeat(down_y, LZ, axis=1)
    tz = np.zeros((DZ, 24, 128))
    tz[:, :LZ] = np.tile(block_z, (1, 1, LY))
    tz[:, LZ : 2 * LZ] = np.tile(np.eye(LZ), (1, LY))[None]
    tz[:, 16] = np.tile(up_z, (1, LY))
    tz[:, 17] = np.tile(down_z, (1, LY))
    tm = np.zeros((DZ, 16, 128))
    tm[:, :8, :8] = block_z
    for e in range(DZ):
        for p in range(DZ):
            if p > e:
                tm[e, 8 + p, :8] = up_z[e] * step_z ** (p - e - 1)
            if p < e:
                tm[e, 8 + p, :8] = down_z[e] * step_z ** (e - p - 1)
    tm[:, :8, 8] = gl_z
    tm[:, :8, 9] = gh_z
    tg = np.zeros((DY, 16, 128))
    tg[:, :, 0] = gl_y
    tg[:, :, 1] = gh_y
    sy = np.zeros((DY, 128))
    sy[:, :16] = gl_y
    sy[:, 16:32] = gh_y
    sz = np.zeros((DZ, 128))
    for e in range(DZ):
        for p in range(DZ):
            if p < e:
                sz[e, p] = step_z ** (e - p - 1)
            if p > e:
                sz[e, 8 + p] = step_z ** (p - e - 1)
    f32 = lambda a: a.astype(np.float32)
    return f32(ty), f32(tz), f32(tm), f32(tg), f32(sy), f32(sz), float(step_y)


TY, TZ, TM, TG, SY, SZ, STEP_Y = tables()
QX = decay(RX)


def x_weights():
    c = np.arange(XB)
    w = (QX ** (np.abs(c[:, None] - c[None]) + 1.0) / (RX * (1 - QX * QX))).astype(np.float32)
    high = w.astype(jnp.bfloat16)
    low = (w - high.astype(np.float32)).astype(jnp.bfloat16)
    edge = np.zeros((8, 128), np.float32)
    edge[0] = QX ** (np.arange(128) + 1.0)
    edge[1] = QX ** (128.0 - np.arange(128))
    return np.stack([high, low]), edge


WX, EDGE = x_weights()


def halves(value):
    high = value.astype(BF16)
    return high, (value - high.astype(F32)).astype(BF16)


def mm(a, b):
    return jnp.dot(a, b, preferred_element_type=F32)


def local_kernel(t_ref, v_ref, y1_ref, y2_ref, z1_ref, z2_ref, ty_ref, tz_ref, wx_ref, edge_ref,
                 loc_ref, a_ref, c_ref, fh, fl, g, ghl):
    d, e = lax.axis_index("gy"), lax.axis_index("gz")
    odd_y, odd_z = (d % 2) == 1, (e % 2) == 1
    zi = lax.broadcasted_iota(jnp.int32, (LZ, NX), 0)
    xi = lax.broadcasted_iota(jnp.int32, (LZ, NX), 1)
    north_halo = jnp.where(odd_y, y2_ref[...], y1_ref[...])
    south_halo = jnp.where(odd_y, y1_ref[...], y2_ref[...])
    for y in range(LY):
        t = t_ref[y]
        north = t_ref[y + 1] if y < LY - 1 else north_halo
        south = t_ref[y - 1] if y > 0 else south_halo
        h1, h2 = z1_ref[y : y + 1, :], z2_ref[y : y + 1, :]
        above = jnp.where(odd_z, h2, h1)
        below = jnp.where(odd_z, h1, h2)
        ceil = jnp.where(zi == LZ - 1, above, pltpu.roll(t, LZ - 1, 0))
        floor = jnp.where(zi == 0, below, pltpu.roll(t, 1, 0))
        east = jnp.where(xi == NX - 1, 0.0, pltpu.roll(t, NX - 1, 1))
        west = jnp.where(xi == 0, 0.0, pltpu.roll(t, 1, 1))
        lap = ((east + west) + (north + south)) + (ceil + floor) - 6.0 * t
        adv = (v_ref[0, y].astype(F32) * (east - west) + v_ref[1, y].astype(F32) * (north - south)
               + v_ref[2, y].astype(F32) * (ceil - floor))
        f = t + KAPPA * lap - 0.5 * adv
        high, low = f.astype(BF16).astype(F32), None
        for b in range(NB):
            part = f[:, b * XB : (b + 1) * XB]
            g[b, y * LZ : (y + 1) * LZ, :] = part
    for b in range(NB):
        high, low = halves(g[b])
        fh[b] = high
        fl[b] = low
    wh, wl = wx_ref[0], wx_ref[1]
    rows = LY * LZ
    xh = fh[...].reshape(NB * rows, XB)
    xl = fl[...].reshape(NB * rows, XB)
    g[...] = (mm(xh, wh) + (mm(xh, wl) + mm(xl, wh))).reshape(NB, rows, XB)
    left, right = edge_ref[0:1, :], edge_ref[1:2, :]
    for b in range(NB):
        before = g[b - 1, :, XB - 1 :] if b > 0 else g[0, :, :1] * (-QX)
        after = g[b + 1, :, :1] if b < NB - 1 else g[NB - 1, :, XB - 1 :] * (-QX)
        lo = g[b, :, :128] + before * left
        hi = g[b, :, 128:] + after * right
        for k, part in ((0, lo), (1, hi)):
            high, low = halves(part)
            at = b * XB + k * 128
            ghl[:rows, at : at + 128] = high
            ghl[rows:, at : at + 128] = low
    my = ty_ref[d]
    mz = tz_ref[e]
    own = (my[:LY][:, None, :] * mz[:LZ][None]).reshape(rows, 128)
    a_rows = jnp.concatenate([my[LY : LY + 1] * mz[8:16], my[LY + 1 : LY + 2] * mz[8:16]], axis=0)
    c_rows = jnp.concatenate([my[:LY] * mz[16:17], my[:LY] * mz[17:18]], axis=0)
    m = jnp.concatenate([own, a_rows, c_rows], axis=0)
    mh, ml = halves(m)
    first = jnp.concatenate([mh, mh], axis=1)
    for b in range(NB):
        cols = slice(b * XB, (b + 1) * XB)
        out = mm(first, ghl[:, cols]) + mm(ml, ghl[:rows, cols])
        loc_ref[:, :, cols] = out[:rows].reshape(LY, LZ, XB)
        c_ref[0, :, cols] = out[rows + 16 : rows + 32]
        c_ref[1, :, cols] = out[rows + 32 :]
        for k in range(2):
            for h in range(2):
                t = b * 2 + h
                tile = out[rows + 8 * k : rows + 8 * k + 8, h * 128 : (h + 1) * 128]
                a_ref[pl.ds((t // 4) * 8 + k * 4 + t % 4, 8, stride=32), :] = tile


def scan_kernel(r_ref, o_ref):
    low_half = lax.broadcasted_iota(jnp.int32, (8, 128), 0) < 4
    state = jnp.zeros((8, 128), F32)
    ahead = []
    for d in range(DY):
        ahead.append(state)
        state = state * STEP_Y + r_ref[d]
    state = jnp.zeros((8, 128), F32)
    for d in range(DY - 1, -1, -1):
        o_ref[d] = jnp.where(low_half, ahead[d], state)
        state = state * STEP_Y + r_ref[d]


def mixed_kernel(p_ref, tm_ref, dz_ref, s_ref):
    e = lax.axis_index("gz")
    tm = tm_ref[e]
    own = [jnp.broadcast_to(tm[:8, w : w + 1], (8, 128)) for w in range(8)]
    out = [jnp.broadcast_to(tm[8:, w : w + 1], (8, 128)) for w in range(8)]
    for k in range(2):
        for t in range(16):
            p = p_ref[pl.ds((t // 4) * 8 + k * 4 + t % 4, 8, stride=32), :]
            one = own[0] * p[0:1]
            two = out[0] * p[0:1]
            for w in range(1, 8):
                one += own[w] * p[w : w + 1]
                two += out[w] * p[w : w + 1]
            dz_ref[k, :, t * 128 : (t + 1) * 128] = one
            s_ref[pl.ds(k * 16 + t, 8, stride=32), :] = two


CH = 512


def final_kernel(loc_ref, dz_ref, cg_ref, r_ref, tm_ref, tg_ref, sy_ref, sz_ref, o_ref, cl, ch):
    d, e = lax.axis_index("gy"), lax.axis_index("gz")
    j = pl.program_id(0)
    tg = tg_ref[d]
    ga = jnp.broadcast_to(tg[:, 0:1], (16, 128))
    gb = jnp.broadcast_to(tg[:, 1:2], (16, 128))
    for i in range(CH // 128):
        cols = slice(i * 128, (i + 1) * 128)
        t = j * (CH // 128) + i
        low = jnp.zeros((16, 128), F32)
        high = jnp.zeros((16, 128), F32)
        for p in range(DZ):
            low += sz_ref[e, p] * cg_ref[p, 0, :, cols]
            high += sz_ref[e, 8 + p] * cg_ref[p, 1, :, cols]
        rows = []
        for k in range(2):
            lo = jnp.zeros((1, 128), F32)
            hi = jnp.zeros((1, 128), F32)
            for p in range(DZ):
                row = r_ref[pl.ds(p * 32 + k * 16 + t, 1), :]
                lo += jnp.where(p < e, row, 0.0)
                hi += jnp.where(p > e, row, 0.0)
            rows.append((lo, hi))
        cl[:, cols] = low + ga * rows[0][0] + gb * rows[1][0]
        ch[:, cols] = high + ga * rows[0][1] + gb * rows[1][1]
    tm = tm_ref[e]
    hl = jnp.broadcast_to(tm[:8, 8:9], (8, CH))
    hh = jnp.broadcast_to(tm[:8, 9:10], (8, CH))
    for l in range(LY):
        o_ref[l] = (loc_ref[l] + sy_ref[d, l] * dz_ref[0] + sy_ref[d, 16 + l] * dz_ref[1]
                    + (hl * cl[l : l + 1, :] + hh * ch[l : l + 1, :]))


VMEM = pl.BlockSpec(memory_space=pltpu.VMEM)
SMEM = pl.BlockSpec(memory_space=pltpu.SMEM)


def params(mib):
    return pltpu.CompilerParams(vmem_limit_bytes=mib * 2**20)


def pairs(count, odd):
    out = []
    for i in range(count):
        j = i + 1 if (i % 2 == 1) == odd else i - 1
        if 0 <= j < count:
            out.append((i, j))
    return out


def on_device(temp, vel):
    d, e = lax.axis_index("gy"), lax.axis_index("gz")
    odd_y, odd_z = d % 2, e % 2
    face_y = lambda last: lax.dynamic_slice_in_dim(temp, last * (LY - 1), 1, 0)[0]
    face_z = lambda last: jnp.where(last == 1, temp[:, LZ - 1], temp[:, 0])
    y1 = lax.ppermute(face_y(1 - odd_y), "gy", pairs(DY, False))
    y2 = lax.ppermute(face_y(odd_y), "gy", pairs(DY, True))
    z1 = lax.ppermute(face_z(1 - odd_z), "gz", pairs(DZ, False))
    z2 = lax.ppermute(face_z(odd_z), "gz", pairs(DZ, True))
    rows = LY * LZ
    loc, a, c = pl.pallas_call(
        local_kernel,
        out_shape=(
            jax.ShapeDtypeStruct((LY, LZ, NX), F32),
            jax.ShapeDtypeStruct((256, 128), F32),
            jax.ShapeDtypeStruct((2, LY, NX), F32),
        ),
        in_specs=[VMEM] * 10,
        out_specs=(VMEM, VMEM, VMEM),
        scratch_shapes=[
            pltpu.VMEM((NB, rows, XB), BF16),
            pltpu.VMEM((NB, rows, XB), BF16),
            pltpu.VMEM((NB, rows, XB), F32),
            pltpu.VMEM((2 * rows, NX), BF16),
        ],
        compiler_params=params(40),
        name="local",
    )(temp, vel, y1, y2, z1, z2, TY, TZ, WX, EDGE)
    cg = lax.all_gather(c, "gz")
    r1 = lax.all_to_all(a.reshape(DY, 8, 128), "gy", 0, 0)
    scanned = pl.pallas_call(
        scan_kernel,
        out_shape=jax.ShapeDtypeStruct((DY, 8, 128), F32),
        in_specs=[VMEM],
        out_specs=VMEM,
        name="scan",
    )(r1)
    r2 = lax.all_to_all(scanned, "gy", 0, 0)
    dz, s = pl.pallas_call(
        mixed_kernel,
        out_shape=(
            jax.ShapeDtypeStruct((2, LZ, NX), F32),
            jax.ShapeDtypeStruct((256, 128), F32),
        ),
        in_specs=[VMEM] * 2,
        out_specs=(VMEM, VMEM),
        name="mixed",
    )(r2.reshape(256, 128), TM)
    r3 = lax.all_to_all(s.reshape(DZ, 32, 128), "gz", 0, 0)
    return pl.pallas_call(
        final_kernel,
        grid=(NX // CH,),
        out_shape=jax.ShapeDtypeStruct((LY, LZ, NX), F32),
        in_specs=[
            pl.BlockSpec((LY, LZ, CH), lambda j: (0, 0, j)),
            pl.BlockSpec((2, LZ, CH), lambda j: (0, 0, j)),
            pl.BlockSpec((DZ, 2, LY, CH), lambda j: (0, 0, 0, j)),
            VMEM, VMEM, VMEM, SMEM, SMEM,
        ],
        out_specs=pl.BlockSpec((LY, LZ, CH), lambda j: (0, 0, j)),
        scratch_shapes=[pltpu.VMEM((LY, CH), F32)] * 2,
        compiler_params=params(24),
        name="final",
    )(loc, dz, cg, r3.reshape(256, 128), TM, TG, SY, SZ)


def solution(mesh):
    return jax.shard_map(
        on_device,
        mesh=mesh,
        in_specs=(P("gy", "gz", None), P(None, "gy", "gz", None)),
        out_specs=P("gy", "gz", None),
        check_vma=False,
    )
```

time: 1120 us -> 93.9 us (0.08); the launches traced: 1110 us -> 93.3 us
  other arithmetic: 560 us -> 0.09 us
  loops' own time: 198 us -> 0 us
  local copies, waits for them, and re-layouts: 139 us -> 10.4 us
  waiting for transfers between devices: 80.7 us -> 1.68 us
  blocking collectives: 97.5 us -> 48.7 us
    add x169 -> x0, other arithmetic: 328 us -> none  [the longest x130 324 us: apply_two(): matrix[0, 0] * vector[0] + matrix[0, 1] * vector[1]]
    another operation x9 -> x0, loops' own time: 198 us -> none  [the longest x3 193 us: reduced_factors(): lax.scan(advance, unit_two, None, length=line_count - 1)]
    another operation x124 -> x0, other arithmetic: 145 us -> none  [the longest x106 141 us: inverse_two(): jnp.stack([jnp.stack([matrix[1, 1], -matrix[0, 1]]), jnp.stack([-matrix[1...]
    slice x196 -> x1, local copies, waits for them, and re-layouts: 124 us -> 2.07 us  [on_device(): face_z = lambda last: jnp.where(last == 1, temp[:, LZ - 1], temp[:, 0])]
    all_gather x4 -> x0, blocking collectives: 97.5 us -> none  [prefix(): pieces = jax.tree.map(lambda part: lax.all_gather(part, axis), value)]
    all_gather x4 -> x1, waiting for transfers between devices: 79.4 us -> 0.01 us  [on_device(): cg = lax.all_gather(c, 'gz')]
    select_n x76 -> x1, other arithmetic: 66.8 us -> 0.09 us  [on_device(): face_z = lambda last: jnp.where(last == 1, temp[:, LZ - 1], temp[:, 0])]
    all_to_all x0 -> x3, blocking collectives: none -> 48.7 us  [the longest x1 21.1 us: on_device(): r1 = lax.all_to_all(a.reshape(DY, 8, 128), 'gy', 0, 0)]
  transfers between devices with their start and end apart: 8 -> 5, of which waited for: 5 -> 1; matrix products, arithmetic and copies ran while one was open for 18% -> 1% of each run, Pallas kernels for 0% -> 4%
where the time goes in v1:
time: 93.9 us; the launch traced here: 93.3 us
  blocking collectives  48.7 us (52%)
  between operations  13.5 us (14%)
  local copies, waits for them, and re-layouts  10.4 us (11%)
  Pallas kernels  9.76 us (10%)
  starting transfers between devices  9.11 us (10%)
  waiting for transfers between devices  1.68 us (2%)
    all_to_all x1, blocking collectives, on_device(): r1 = lax.all_to_all(a.reshape(DY, 8, 128), 'gy', 0, 0)  21.1 us
    all_to_all x1, blocking collectives, on_device(): r2 = lax.all_to_all(scanned, 'gy', 0, 0)  14 us
    all_to_all x1, blocking collectives, on_device(): r3 = lax.all_to_all(s.reshape(DZ, 32, 128), 'gz', 0, 0)  13.7 us
    unnamed x24, local copies, waits for them, and re-layouts  7.44 us
    ppermute x1, starting transfers between devices, on_device(): z2 = lax.ppermute(face_z(odd_z), 'gz', pairs(DZ, True))  4.59 us
    ppermute x1, starting transfers between devices, on_device(): y1 = lax.ppermute(face_y(1 - odd_y), 'gy', pairs(DY, False))  3.75 us
    pallas_call x1, Pallas kernels, on_device(): pl.pallas_call(local_kernel, out_shape=(jax.ShapeDtypeStruct((LY, LZ, NX)...  3.23 us
    pallas_call x1, Pallas kernels, on_device(): pl.pallas_call(final_kernel, grid=(NX // CH,), out_shape=jax.ShapeDtypeSt...  3.01 us
  transfers between devices with their start and end apart: 5, of which 1 were waited for; matrix products, arithmetic and copies ran while one was open for 1% of the time, Pallas kernels for 4%

profile of v1, /device:TPU:1, one launch (start us, length us, event | category | flops | bytes accessed | tf_op | source)
XLA Modules:
  0.0 93.3 jit_solution(11538487943695566153)
XLA Ops:
  6.5 0.0 copy-start.1
  6.5 0.0 all-gather.3.cloned.1.call-start
  6.5 2.1 %fusion = (f32[16,1,2048]{2,1,0:T(1,128)S(1)}, f32[16,1,2048]{2,1,0:T(1,128)S(1)}) fusion(f32[16,8,2048]{2,1,0:T(8,128)} %t_ref.1), kind=kLoop, calls=%fused_computation.4 | loop fusion | bytes 524288 | tf_op jit(solution)/shard_map/slice | solution.py:269
  8.6 0.1 select_bitcast_fusion
  8.7 4.6 %collective-permute-start.3 = (f32[16,2048]{1,0:T(8,128)S(1)}, f32[16,2048]{1,0:T(8,128)S(1)}, u32[]{:S(2)}, u32[]{:S(2)}) collective-permute-start(f32[16,2048]{1,0:T(8,128)S(1)} %get-tuple-element.19), channel_id=1, source_target_pairs={{1,2},{2,1},{3,4},{4,3},{5,6},{6,5},{9,10},{10,9},{11,12},{12,11},... | collective-permute-start | bytes 393224 | tf_op jit(solution)/shard_map/ppermute | solution.py:273
  13.3 0.1 collective-permute-start.2
  13.4 0.0 copy-start.4
  13.5 0.0 copy-start.9
  13.5 0.0 copy-start.10
  13.5 0.9 dynamic-slice_bitcast_fusion
  14.4 0.7 collective-permute-start.1
  15.1 3.8 %collective-permute-start = (f32[8,2048]{1,0:T(8,128)S(1)}, f32[8,2048]{1,0:T(8,128)S(1)}, u32[]{:S(2)}, u32[]{:S(2)}) collective-permute-start(f32[8,2048]{1,0:T(8,128)S(1)} %get-tuple-element.18), channel_id=1, source_target_pairs={{0,8},{8,0},{16,24},{24,16},{32,40},{40,32},{48,56},{56,48},{64,72... | collective-permute-start | bytes 196616 | tf_op jit(solution)/shard_map/ppermute | solution.py:270
  18.8 0.0 collective-permute-done.1.y2_ref
  18.8 1.7 %collective-permute-done.y1_ref = f32[8,2048]{1,0:T(8,128)S(1)} collective-permute-done((f32[8,2048]{1,0:T(8,128)S(1)}, f32[8,2048]{1,0:T(8,128)S(1)}, u32[]{:S(2)}, u32[]{:S(2)}) %collective-permute-start) | collective-permute-done | bytes 65568 | tf_op jit(solution)/shard_map/ppermute | solution.py:270
  20.5 0.0 collective-permute-done.3.z2_ref
  20.5 0.0 collective-permute-done.2.z1_ref
  20.5 0.0 copy-done.1
  20.5 0.0 copy-start.2
  20.5 1.4 %copy-done.2 = bf16[3,16,8,2048]{3,2,1,0:T(8,128)(2,1)S(1)} copy-done((bf16[3,16,8,2048]{3,2,1,0:T(8,128)(2,1)S(1)}, bf16[3,16,8,2048]{3,2,1,0:T(8,128)(2,1)}, u32[]{:S(2)}) %copy-start.2) | copy-done | bytes 1572888
  21.9 0.0 copy-start.3
  21.9 1.0 %copy-done.3 = f32[32,24,128]{2,1,0:T(8,128)S(1)} copy-done((f32[32,24,128]{2,1,0:T(8,128)S(1)}, f32[32,24,128]{2,1,0:T(8,128)}, u32[]{:S(2)}) %copy-start.3) | copy-done | bytes 393240
  22.9 0.0 copy-start.6
  22.9 0.9 %copy-done.6 = bf16[2,256,256]{2,1,0:T(8,128)(2,1)S(1)} copy-done((bf16[2,256,256]{2,1,0:T(8,128)(2,1)S(1)}, bf16[2,256,256]{2,1,0:T(8,128)(2,1)}, u32[]{:S(2)}) %copy-start.6) | copy-done | bytes 262168
  23.8 0.0 copy-start.8
  23.8 0.9 copy-done.8
  24.7 0.0 copy-start.11
  24.7 0.7 copy-done.11
  25.4 0.0 copy-start.5
  25.4 3.2 %local.1 = (f32[16,8,2048]{2,1,0:T(8,128)S(1)}, f32[256,128]{1,0:T(8,128)S(1)}, f32[2,16,2048]{2,1,0:T(8,128)}) custom-call(f32[16,8,2048]{2,1,0:T(8,128)S(1)} %copy-done.1, bf16[3,16,8,2048]{3,2,1,0:T(8,128)(2,1)S(1)} %copy-done.2, f32[8,2048]{1,0:T(8,128)S(1)} %collective-permute-done.y1_ref, f32[8,2048]{1,0:T(8,128)S(1)} %collective-permute-done.1.y2_ref, ...), custom_call_target="tpu_custom_call" | custom-call | tf_op jit(solution)/shard_map/local/pallas_call | solution.py:275
  28.7 0.0 all-gather.3.cloned.1.call-update
  28.7 21.1 %all_to_all.15.r_ref = f32[32,8,128]{2,1,0:T(8,128)} all-to-all(f32[32,8,128]{2,1,0:T(8,128)S(1)} %bitcast.15), channel_id=1, replica_groups=mesh['gy'=32,'gz'=8] {'gy'}, dimensions={0} | all-to-all | bytes 262144 | tf_op jit(solution)/shard_map/all_to_all | solution.py:294
  49.8 1.6 %scan.1 = f32[32,8,128]{2,1,0:T(8,128)} custom-call(f32[32,8,128]{2,1,0:T(8,128)} %all_to_all.15.r_ref), custom_call_target="tpu_custom_call" | custom-call | tf_op jit(solution)/shard_map/scan/pallas_call | solution.py:295
  51.4 14.0 %all_to_all.16 = f32[32,8,128]{2,1,0:T(8,128)} all-to-all(f32[32,8,128]{2,1,0:T(8,128)} %scan.1), channel_id=1, replica_groups=mesh['gy'=32,'gz'=8] {'gy'}, dimensions={0} | all-to-all | bytes 262144 | tf_op jit(solution)/shard_map/all_to_all | solution.py:302
  65.3 1.9 %mixed.1 = (f32[2,8,2048]{2,1,0:T(8,128)}, f32[256,128]{1,0:T(8,128)}) custom-call(f32[256,128]{1,0:T(8,128)} %bitcast.16, f32[8,16,128]{2,1,0:T(8,128)} %constant.52.clone.tm_ref), custom_call_target="tpu_custom_call" | custom-call | tf_op jit(solution)/shard_map/mixed/pallas_call | solution.py:303
  67.2 13.7 %all_to_all.17 = f32[8,32,128]{2,1,0:T(8,128)S(1)} all-to-all(f32[8,32,128]{2,1,0:T(8,128)} %bitcast.17), channel_id=1, replica_groups=mesh['gy'=32,'gz'=8] {'gz'}, dimensions={0} | all-to-all | bytes 262144 | tf_op jit(solution)/shard_map/all_to_all | solution.py:313
  80.9 0.0 all-gather.3.cloned.1.call-done
  80.9 0.0 copy-done.4
  80.9 0.0 copy-done.9
  80.9 0.0 copy-done.10
  80.9 0.0 copy-done.5
  80.9 0.0 copy-start
  80.9 1.6 %copy-done = f32[16,16,2048]{2,1,0:T(8,128)S(1)} copy-done((f32[16,16,2048]{2,1,0:T(8,128)S(1)}, f32[16,16,2048]{2,1,0:T(8,128)}, u32[]{:S(2)}) %copy-start) | copy-done | bytes 2097176
  82.5 0.0 copy-start.7
  82.5 0.9 copy-done.7
  83.4 3.0 %final.1 = f32[16,8,2048]{2,1,0:T(8,128)} custom-call(f32[16,8,2048]{2,1,0:T(8,128)S(1)} %get-tuple-element.10.loc_ref, f32[2,8,2048]{2,1,0:T(8,128)S(1)} %copy-done.7, f32[8,2,16,2048]{3,2,1,0:T(8,128)S(1)} %bitcast.13, f32[256,128]{1,0:T(8,128)S(1)} %bitcast.14, f32[8,16,128]{2,1,0:T(8,128)S(1)} %copy-done.4, f32[32,16,128]{2,1,0:T(8,128)S(1)} %copy-done.5, ...), custom_call_target="tpu_custom_call" | custom-call | tf_op jit(solution)/shard_map/final/pallas_call | solution.py:314
Async XLA Ops:
  6.5 13.9 %copy-start.1 = (f32[16,8,2048]{2,1,0:T(8,128)S(1)}, f32[16,8,2048]{2,1,0:T(8,128)}, u32[]{:S(2)}) copy-start(f32[16,8,2048]{2,1,0:T(8,128)} %t_ref.1) | copy-start | bytes 3145732
  6.5 74.4 %all-gather.3.cloned.1.call-start = ((), (), s32[]{:S(2)}) async-start(), calls=%async_computation.3 | async-start | bytes 2359296 | tf_op jit(solution)/shard_map/all_gather | solution.py:293
  8.7 11.8 %collective-permute-start.3 = (f32[16,2048]{1,0:T(8,128)S(1)}, f32[16,2048]{1,0:T(8,128)S(1)}, u32[]{:S(2)}, u32[]{:S(2)}) collective-permute-start(f32[16,2048]{1,0:T(8,128)S(1)} %get-tuple-element.19), channel_id=1, source_target_pairs={{1,2},{2,1},{3,4},{4,3},{5,6},{6,5},{9,10},{10,9},{11,12},{12,11},... | collective-permute-start | bytes 393224 | tf_op jit(solution)/shard_map/ppermute | solution.py:273
  13.3 7.2 %collective-permute-start.2 = (f32[16,2048]{1,0:T(8,128)S(1)}, f32[16,2048]{1,0:T(8,128)S(1)}, u32[]{:S(2)}, u32[]{:S(2)}) collective-permute-start(f32[16,2048]{1,0:T(8,128)S(1)} %get-tuple-element.20), channel_id=1, source_target_pairs={{0,1},{1,0},{2,3},{3,2},{4,5},{5,4},{6,7},{7,6},{8,9},{9,8},{10,11... | collective-permute-start | bytes 393224 | tf_op jit(solution)/shard_map/ppermute | solution.py:272
  13.4 67.5 %copy-start.4 = (f32[8,16,128]{2,1,0:T(8,128)S(1)}, f32[8,16,128]{2,1,0:T(8,128)}, u32[]{:S(2)}) copy-start(f32[8,16,128]{2,1,0:T(8,128)} %constant.52.clone.tm_ref) | copy-start | bytes 196612
  13.5 67.5 %copy-start.9 = (f32[32,128]{1,0:T(8,128)S(1)}, f32[32,128]{1,0:T(8,128)}, u32[]{:S(2)}) copy-start(f32[32,128]{1,0:T(8,128)} %constant.54.clone.sy_ref) | copy-start | bytes 49156
  13.5 67.5 %copy-start.10 = (f32[8,128]{1,0:T(8,128)S(1)}, f32[8,128]{1,0:T(8,128)}, u32[]{:S(2)}) copy-start(f32[8,128]{1,0:T(8,128)} %constant.55.clone.sz_ref) | copy-start | bytes 12292
  14.4 4.4 %collective-permute-start.1 = (f32[8,2048]{1,0:T(8,128)S(1)}, f32[8,2048]{1,0:T(8,128)S(1)}, u32[]{:S(2)}, u32[]{:S(2)}) collective-permute-start(f32[8,2048]{1,0:T(8,128)S(1)} %get-tuple-element.17), channel_id=1, source_target_pairs={{8,16},{16,8},{24,32},{32,24},{40,48},{48,40},{56,64},{64,56},{72,... | collective-permute-start | bytes 196616 | tf_op jit(solution)/shard_map/ppermute | solution.py:271
  15.1 5.4 %collective-permute-start = (f32[8,2048]{1,0:T(8,128)S(1)}, f32[8,2048]{1,0:T(8,128)S(1)}, u32[]{:S(2)}, u32[]{:S(2)}) collective-permute-start(f32[8,2048]{1,0:T(8,128)S(1)} %get-tuple-element.18), channel_id=1, source_target_pairs={{0,8},{8,0},{16,24},{24,16},{32,40},{40,32},{48,56},{56,48},{64,72... | collective-permute-start | bytes 196616 | tf_op jit(solution)/shard_map/ppermute | solution.py:270
  20.5 1.4 %copy-start.2 = (bf16[3,16,8,2048]{3,2,1,0:T(8,128)(2,1)S(1)}, bf16[3,16,8,2048]{3,2,1,0:T(8,128)(2,1)}, u32[]{:S(2)}) copy-start(bf16[3,16,8,2048]{3,2,1,0:T(8,128)(2,1)} %v_ref.1) | copy-start | bytes 4718596
  21.9 1.0 %copy-start.3 = (f32[32,24,128]{2,1,0:T(8,128)S(1)}, f32[32,24,128]{2,1,0:T(8,128)}, u32[]{:S(2)}) copy-start(f32[32,24,128]{2,1,0:T(8,128)} %constant.48.clone.ty_ref) | copy-start | bytes 1179652
  22.9 0.9 %copy-start.6 = (bf16[2,256,256]{2,1,0:T(8,128)(2,1)S(1)}, bf16[2,256,256]{2,1,0:T(8,128)(2,1)}, u32[]{:S(2)}) copy-start(bf16[2,256,256]{2,1,0:T(8,128)(2,1)} %constant.50.clone.wx_ref) | copy-start | bytes 786436
  23.8 0.9 copy-start.8
  24.7 0.7 copy-start.11
  25.4 55.5 %copy-start.5 = (f32[32,16,128]{2,1,0:T(8,128)S(1)}, f32[32,16,128]{2,1,0:T(8,128)}, u32[]{:S(2)}) copy-start(f32[32,16,128]{2,1,0:T(8,128)} %constant.53.clone.tg_ref) | copy-start | bytes 786436
  80.9 1.6 %copy-start = (f32[16,16,2048]{2,1,0:T(8,128)S(1)}, f32[16,16,2048]{2,1,0:T(8,128)}, u32[]{:S(2)}) copy-start(f32[16,16,2048]{2,1,0:T(8,128)} %all-gather.3.cloned.1.call-done) | copy-start | bytes 6291460
  82.5 0.9 copy-start.7
Sparse Core Ops, SparseCore 0:
  28.8 32.5 all-gather.2

commit v2 on v1

v2 whole, which is shorter than its diff:
```python
import jax
import jax.numpy as jnp
import numpy as np
from jax import lax
from jax.experimental import pallas as pl
from jax.experimental.pallas import tpu as pltpu
from jax.sharding import PartitionSpec as P

NX, NY, NZ = 2048, 512, 64
RX, RY, RZ = 1, 768, 192
DY, DZ = 32, 8
LY, LZ = NY // DY, NZ // DZ
XB = 256
NB = NX // XB
KAPPA = 0.15
F32, BF16 = jnp.float32, jnp.bfloat16


def decay(ratio):
    half = 0.5 / ratio
    return 1.0 + half - np.sqrt(half * (2.0 + half))


def line_factors(count, ratio):
    q = decay(ratio)
    i = np.arange(count)
    low = 1.0 - q ** (2.0 * (i + 1))
    high = 1.0 - q ** (2.0 * (count - i))
    denom = ratio * (1.0 - q * q) * (1.0 - q ** (2.0 * count + 2))
    return q, low, high, denom


def split_line(count, ratio, parts):
    q, low, high, denom = line_factors(count, ratio)
    size = count // parts
    low, high = low.reshape(parts, size), high.reshape(parts, size)
    m = np.arange(size)
    small = np.minimum(m[:, None], m[None])
    large = np.maximum(m[:, None], m[None])
    block = q ** (large - small + 1.0) * low[:, small] * high[:, large] / denom
    up = q ** (size - 1.0 - m) * low
    down = q ** (1.0 * m) * high
    from_low = q ** (m + 2.0) * high / denom
    from_high = q ** (size + 1.0 - m) * low / denom
    return block, up, down, from_low, from_high, q**size


def tables():
    block_y, up_y, down_y, gl_y, gh_y, step_y = split_line(NY, RY, DY)
    block_z, up_z, down_z, gl_z, gh_z, step_z = split_line(NZ, RZ, DZ)
    lines = np.zeros((DY + DZ, 24, 128))
    ty, tz = lines[:DY], lines[DY:]
    ty[:, :LY] = np.repeat(block_y, LZ, axis=2)
    ty[:, LY] = np.repeat(up_y, LZ, axis=1)
    ty[:, LY + 1] = np.repeat(down_y, LZ, axis=1)
    tz[:, :LZ] = np.tile(block_z, (1, 1, LY))
    tz[:, LZ : 2 * LZ] = np.tile(np.eye(LZ), (1, LY))[None]
    tz[:, 16] = np.tile(up_z, (1, LY))
    tz[:, 17] = np.tile(down_z, (1, LY))
    tz[:, 18] = QX ** (np.arange(128) + 1.0)
    tz[:, 19] = QX ** (128.0 - np.arange(128))
    sums = np.zeros((DY + DZ, 16, 128))
    tm = sums[DY:]
    tm[:, :8, :8] = block_z
    for e in range(DZ):
        for p in range(DZ):
            if p > e:
                tm[e, 8 + p, :8] = up_z[e] * step_z ** (p - e - 1)
            if p < e:
                tm[e, 8 + p, :8] = down_z[e] * step_z ** (e - p - 1)
    tm[:, :8, 8] = gl_z
    tm[:, :8, 9] = gh_z
    sums[:DY, :, 0] = gl_y
    sums[:DY, :, 1] = gh_y
    scal = np.zeros((DY, 128))
    scal[:, :16] = gl_y
    scal[:, 16:32] = gh_y
    f32 = lambda a: a.astype(np.float32)
    return f32(lines), f32(sums), f32(scal), float(step_y), float(step_z)


QX = decay(RX)
LINES, SUMS, SCAL, STEP_Y, STEP_Z = tables()


def x_weights():
    c = np.arange(XB)
    w = (QX ** (np.abs(c[:, None] - c[None]) + 1.0) / (RX * (1 - QX * QX))).astype(np.float32)
    high = w.astype(jnp.bfloat16)
    low = (w - high.astype(np.float32)).astype(jnp.bfloat16)
    return np.stack([high, low])


WX = x_weights()


def halves(value):
    high = value.astype(BF16)
    return high, (value - high.astype(F32)).astype(BF16)


def mm(a, b):
    return jnp.dot(a, b, preferred_element_type=F32)


def start(*pairs_and_sem):
    copies = [pltpu.make_async_copy(*p) for p in pairs_and_sem]
    for c in copies:
        c.start()
    return copies


def faces_kernel(t_hbm, t_ref, y1_ref, y2_ref, z1_ref, z2_ref, sem):
    d, e = lax.axis_index("gy"), lax.axis_index("gz")
    odd_y, odd_z = (d % 2) == 1, (e % 2) == 1
    load = pltpu.make_async_copy(t_hbm, t_ref, sem)
    load.start()
    load.wait()
    first, last = t_ref[0], t_ref[LY - 1]
    y1_ref[...] = jnp.where(odd_y, first, last)
    y2_ref[...] = jnp.where(odd_y, last, first)
    for y in range(LY):
        bottom, top = t_ref[y, 0:1, :], t_ref[y, LZ - 1 : LZ, :]
        z1_ref[y : y + 1, :] = jnp.where(odd_z, bottom, top)
        z2_ref[y : y + 1, :] = jnp.where(odd_z, top, bottom)


def local_kernel(t_ref, v_hbm, y1_ref, y2_ref, z1_ref, z2_ref, lines_hbm, wx_hbm,
                 loc_ref, a_ref, c_ref, fh, fl, g, ghl, v_ref, ty_ref, tz_ref, wx_ref, sems):
    d, e = lax.axis_index("gy"), lax.axis_index("gz")
    loads = start((v_hbm, v_ref, sems.at[0]), (wx_hbm, wx_ref, sems.at[1]),
                  (lines_hbm.at[d], ty_ref, sems.at[2]), (lines_hbm.at[DY + e], tz_ref, sems.at[3]))
    odd_y, odd_z = (d % 2) == 1, (e % 2) == 1
    zi = lax.broadcasted_iota(jnp.int32, (LZ, NX), 0)
    xi = lax.broadcasted_iota(jnp.int32, (LZ, NX), 1)
    north_halo = jnp.where(odd_y, y2_ref[...], y1_ref[...])
    south_halo = jnp.where(odd_y, y1_ref[...], y2_ref[...])
    loads[0].wait()
    for y in range(LY):
        t = t_ref[y]
        north = t_ref[y + 1] if y < LY - 1 else north_halo
        south = t_ref[y - 1] if y > 0 else south_halo
        h1, h2 = z1_ref[y : y + 1, :], z2_ref[y : y + 1, :]
        above = jnp.where(odd_z, h2, h1)
        below = jnp.where(odd_z, h1, h2)
        ceil = jnp.where(zi == LZ - 1, above, pltpu.roll(t, LZ - 1, 0))
        floor = jnp.where(zi == 0, below, pltpu.roll(t, 1, 0))
        east = jnp.where(xi == NX - 1, 0.0, pltpu.roll(t, NX - 1, 1))
        west = jnp.where(xi == 0, 0.0, pltpu.roll(t, 1, 1))
        lap = ((east + west) + (north + south)) + (ceil + floor) - 6.0 * t
        adv = (v_ref[0, y].astype(F32) * (east - west) + v_ref[1, y].astype(F32) * (north - south)
               + v_ref[2, y].astype(F32) * (ceil - floor))
        f = t + KAPPA * lap - 0.5 * adv
        for b in range(NB):
            part = f[:, b * XB : (b + 1) * XB]
            g[b, y * LZ : (y + 1) * LZ, :] = part
    for b in range(NB):
        high, low = halves(g[b])
        fh[b] = high
        fl[b] = low
    for load in loads[1:]:
        load.wait()
    wh, wl = wx_ref[0], wx_ref[1]
    rows = LY * LZ
    xh = fh[...].reshape(NB * rows, XB)
    xl = fl[...].reshape(NB * rows, XB)
    g[...] = (mm(xh, wh) + (mm(xh, wl) + mm(xl, wh))).reshape(NB, rows, XB)
    left, right = tz_ref[18:19, :], tz_ref[19:20, :]
    for b in range(NB):
        before = g[b - 1, :, XB - 1 :] if b > 0 else g[0, :, :1] * (-QX)
        after = g[b + 1, :, :1] if b < NB - 1 else g[NB - 1, :, XB - 1 :] * (-QX)
        lo = g[b, :, :128] + before * left
        hi = g[b, :, 128:] + after * right
        for k, part in ((0, lo), (1, hi)):
            high, low = halves(part)
            at = b * XB + k * 128
            ghl[:rows, at : at + 128] = high
            ghl[rows:, at : at + 128] = low
    my = ty_ref[...]
    mz = tz_ref[...]
    own = (my[:LY][:, None, :] * mz[:LZ][None]).reshape(rows, 128)
    a_rows = jnp.concatenate([my[LY : LY + 1] * mz[8:16], my[LY + 1 : LY + 2] * mz[8:16]], axis=0)
    c_rows = jnp.concatenate([my[:LY] * mz[16:17], my[:LY] * mz[17:18]], axis=0)
    m = jnp.concatenate([own, a_rows, c_rows], axis=0)
    mh, ml = halves(m)
    first = jnp.concatenate([mh, mh], axis=1)
    for b in range(NB):
        cols = slice(b * XB, (b + 1) * XB)
        out = mm(first, ghl[:, cols]) + mm(ml, ghl[:rows, cols])
        loc_ref[:, :, cols] = out[:rows].reshape(LY, LZ, XB)
        c_ref[0, :, cols] = out[rows + 16 : rows + 32]
        c_ref[1, :, cols] = out[rows + 32 :]
        for k in range(2):
            for h in range(2):
                t = b * 2 + h
                tile = out[rows + 8 * k : rows + 8 * k + 8, h * 128 : (h + 1) * 128]
                a_ref[pl.ds((t // 4) * 8 + k * 4 + t % 4, 8, stride=32), :] = tile


def scan_kernel(r_ref, c_ref, x_ref, o_ref, tot_ref, pre_ref):
    low_half = lax.broadcasted_iota(jnp.int32, (8, 128), 0) < 4
    state = jnp.zeros((8, 128), F32)
    ahead = []
    for d in range(DY):
        ahead.append(state)
        state = state * STEP_Y + r_ref[d]
    state = jnp.zeros((8, 128), F32)
    for d in range(DY - 1, -1, -1):
        o_ref[d] = jnp.where(low_half, ahead[d], state)
        state = state * STEP_Y + r_ref[d]
    e = lax.axis_index("gz")
    upper = (e % 2) == 1
    near, far = jnp.where(upper, 1.0, STEP_Z), jnp.where(upper, STEP_Z, 1.0)
    tot_ref[0] = near * c_ref[0] + far * x_ref[0]
    tot_ref[1] = far * c_ref[1] + near * x_ref[1]
    pre_ref[0] = jnp.where(upper, x_ref[0], 0.0)
    pre_ref[1] = jnp.where(upper, 0.0, x_ref[1])


def mixed_kernel(p_ref, tot_ref, x_ref, pre_ref, sums_hbm, dz_ref, s_ref, send_ref, pre2_ref, tm_ref, sem):
    e = lax.axis_index("gz")
    load = pltpu.make_async_copy(sums_hbm.at[DY + e], tm_ref, sem)
    load.start()
    upper = ((e // 2) % 2) == 1
    odd = (e % 2) == 1
    two = STEP_Z * STEP_Z
    near, far = jnp.where(upper, 1.0, two), jnp.where(upper, two, 1.0)
    top = (e // 4) == 1
    send_ref[...] = jnp.where(top, far * tot_ref[1] + near * x_ref[1], near * tot_ref[0] + far * x_ref[0])
    low = jnp.where(odd, STEP_Z, 1.0)
    high = jnp.where(odd, 1.0, STEP_Z)
    pre2_ref[0] = pre_ref[0] + jnp.where(upper, low * x_ref[0], 0.0)
    pre2_ref[1] = pre_ref[1] + jnp.where(upper, 0.0, high * x_ref[1])
    load.wait()
    tm = tm_ref[...]
    own = [jnp.broadcast_to(tm[:8, w : w + 1], (8, 128)) for w in range(8)]
    out = [jnp.broadcast_to(tm[8:, w : w + 1], (8, 128)) for w in range(8)]
    for k in range(2):
        for t in range(16):
            p = p_ref[pl.ds((t // 4) * 8 + k * 4 + t % 4, 8, stride=32), :]
            one = own[0] * p[0:1]
            two = out[0] * p[0:1]
            for w in range(1, 8):
                one += own[w] * p[w : w + 1]
                two += out[w] * p[w : w + 1]
            dz_ref[k, :, t * 128 : (t + 1) * 128] = one
            s_ref[pl.ds(k * 16 + t, 8, stride=32), :] = two


def final_kernel(loc_ref, dz_ref, pre_ref, x_ref, r_ref, sums_hbm, scal_ref, o_hbm,
                 cl, ch, o_ref, tg_ref, tm_ref, sems):
    d, e = lax.axis_index("gy"), lax.axis_index("gz")
    loads = start((sums_hbm.at[d], tg_ref, sems.at[0]), (sums_hbm.at[DY + e], tm_ref, sems.at[1]))
    lo = jnp.zeros((32, 128), F32)
    hi = jnp.zeros((32, 128), F32)
    for p in range(DZ):
        part = r_ref[p * 32 : (p + 1) * 32, :]
        lo += jnp.where(p < e, part, 0.0)
        hi += jnp.where(p > e, part, 0.0)
    top = (e // 4) == 1
    at = lax.rem(e, 4)
    power = lambda k: jnp.where(k == 0, 1.0, jnp.where(k == 1, STEP_Z, jnp.where(k == 2, STEP_Z**2, STEP_Z**3)))
    up = jnp.where(top, power(at), 0.0)
    down = jnp.where(top, 0.0, power(3 - at))
    for load in loads:
        load.wait()
    tg, tm = tg_ref[...], tm_ref[...]
    ga = jnp.broadcast_to(tg[:, 0:1], (16, 128))
    gb = jnp.broadcast_to(tg[:, 1:2], (16, 128))
    for t in range(NX // 128):
        cols = slice(t * 128, (t + 1) * 128)
        cl[:, cols] = (pre_ref[0, :, cols] + up * x_ref[:, cols]) + (ga * lo[t : t + 1] + gb * lo[16 + t : 17 + t])
        ch[:, cols] = (pre_ref[1, :, cols] + down * x_ref[:, cols]) + (ga * hi[t : t + 1] + gb * hi[16 + t : 17 + t])
    hl = jnp.broadcast_to(tm[:8, 8:9], (8, NX))
    hh = jnp.broadcast_to(tm[:8, 9:10], (8, NX))
    stores = []
    for l in range(LY):
        o_ref[l] = (loc_ref[l] + scal_ref[d, l] * dz_ref[0] + scal_ref[d, 16 + l] * dz_ref[1]
                    + (hl * cl[l : l + 1, :] + hh * ch[l : l + 1, :]))
        if l % 4 == 3:
            i = l // 4
            stores += start((o_ref.at[pl.ds(l - 3, 4)], o_hbm.at[pl.ds(l - 3, 4)], sems.at[2 + i]))
    for store in stores:
        store.wait()


VMEM = pl.BlockSpec(memory_space=pltpu.VMEM)
SMEM = pl.BlockSpec(memory_space=pltpu.SMEM)
HBM = pl.BlockSpec(memory_space=pltpu.HBM)


def call(kernel, outs, ins, out_specs, scratch, mib, name):
    return pl.pallas_call(
        kernel,
        out_shape=tuple(jax.ShapeDtypeStruct(shape, F32) for shape in outs),
        in_specs=ins,
        out_specs=tuple(out_specs),
        scratch_shapes=scratch,
        compiler_params=pltpu.CompilerParams(vmem_limit_bytes=mib * 2**20),
        name=name,
    )


def pairs(count, odd):
    out = []
    for i in range(count):
        j = i + 1 if (i % 2 == 1) == odd else i - 1
        if 0 <= j < count:
            out.append((i, j))
    return out


def across(value, bit):
    return lax.ppermute(value, "gz", [(i, i ^ bit) for i in range(DZ)])


def on_device(temp, vel):
    rows = LY * LZ
    dma = pltpu.SemaphoreType.DMA
    temp, y1, y2, z1, z2 = call(
        faces_kernel, [(LY, LZ, NX), (LZ, NX), (LZ, NX), (LY, NX), (LY, NX)], [HBM], [VMEM] * 5, [dma], 8, "faces"
    )(temp)
    y1 = lax.ppermute(y1, "gy", pairs(DY, False))
    y2 = lax.ppermute(y2, "gy", pairs(DY, True))
    z1 = lax.ppermute(z1, "gz", pairs(DZ, False))
    z2 = lax.ppermute(z2, "gz", pairs(DZ, True))
    loc, a, c = call(
        local_kernel,
        [(LY, LZ, NX), (256, 128), (2, LY, NX)],
        [VMEM, HBM] + [VMEM] * 4 + [HBM] * 2,
        [VMEM] * 3,
        [
            pltpu.VMEM((NB, rows, XB), BF16),
            pltpu.VMEM((NB, rows, XB), BF16),
            pltpu.VMEM((NB, rows, XB), F32),
            pltpu.VMEM((2 * rows, NX), BF16),
            pltpu.VMEM((3, LY, LZ, NX), BF16),
            pltpu.VMEM((24, 128), F32),
            pltpu.VMEM((24, 128), F32),
            pltpu.VMEM((2, XB, XB), BF16),
            dma((4,)),
        ],
        16,
        "local",
    )(temp, vel, y1, y2, z1, z2, LINES, WX)
    x1 = across(c, 1)
    r1 = lax.all_to_all(a.reshape(DY, 8, 128), "gy", 0, 0)
    scanned, tot, pre = call(
        scan_kernel, [(DY, 8, 128), (2, LY, NX), (2, LY, NX)], [VMEM] * 3, [VMEM] * 3, [], 8, "scan"
    )(r1, c, x1)
    x2 = across(tot, 2)
    r2 = lax.all_to_all(scanned, "gy", 0, 0)
    dz, s, send, pre = call(
        mixed_kernel,
        [(2, LZ, NX), (256, 128), (LY, NX), (2, LY, NX)],
        [VMEM] * 4 + [HBM],
        [VMEM] * 4,
        [pltpu.VMEM((16, 128), F32), dma],
        8,
        "mixed",
    )(r2.reshape(256, 128), tot, x2, pre, SUMS)
    x3 = across(send, 4)
    r3 = lax.all_to_all(s.reshape(DZ, 32, 128), "gz", 0, 0)
    return call(
        final_kernel,
        [(LY, LZ, NX)],
        [VMEM] * 5 + [HBM, SMEM],
        [HBM],
        [
            pltpu.VMEM((LY, NX), F32),
            pltpu.VMEM((LY, NX), F32),
            pltpu.VMEM((LY, LZ, NX), F32),
            pltpu.VMEM((16, 128), F32),
            pltpu.VMEM((16, 128), F32),
            dma((6,)),
        ],
        16,
        "final",
    )(loc, dz, pre, x3, r3.reshape(256, 128), SUMS, SCAL)[0]


def solution(mesh):
    return jax.shard_map(
        on_device,
        mesh=mesh,
        in_specs=(P("gy", "gz", None), P(None, "gy", "gz", None)),
        out_specs=P("gy", "gz", None),
        check_vma=False,
    )
```

time: 93.9 us -> 72.8 us (0.78)
  between operations: 13.5 us -> 0.07 us
  local copies, waits for them, and re-layouts: 10.4 us -> 4.62 us
  Pallas kernels: 9.76 us -> 5.84 us
  starting transfers between devices: 9.11 us -> 12.5 us
  blocking collectives: 48.7 us -> 46.4 us
  waiting for transfers between devices: 1.68 us -> 2.95 us
    pallas_call x4 -> x5, Pallas kernels: 9.76 us -> 5.84 us  [the longest x1 3.07 us: on_device(): call(local_kernel, [(LY, LZ, NX), (256, 128), (2, LY, NX)], [VMEM, HBM] +...]
    ppermute x4 -> x7, starting transfers between devices: 9.1 us -> 12.5 us  [the longest x3 5.84 us: across(): return lax.ppermute(value, 'gz', [(i, i ^ bit) for i in range(DZ)])]
    unnamed x24 -> x12, local copies, waits for them, and re-layouts: 7.44 us -> 4.62 us
    all_to_all x1, blocking collectives: 13.7 us -> 11 us  [on_device(): r3 = lax.all_to_all(s.reshape(DZ, 32, 128), 'gz', 0, 0)]
    slice x1 -> x0, local copies, waits for them, and re-layouts: 2.07 us -> none  [on_device(): face_z = lambda last: jnp.where(last == 1, temp[:, LZ - 1], temp[:, 0])]
    all_to_all x1, blocking collectives: 21.1 us -> 22.8 us  [on_device(): r1 = lax.all_to_all(a.reshape(DY, 8, 128), 'gy', 0, 0)]
    all_to_all x1, blocking collectives: 14 us -> 12.6 us  [on_device(): r2 = lax.all_to_all(scanned, 'gy', 0, 0)]
    ppermute x4 -> x7, waiting for transfers between devices: 1.66 us -> 2.95 us  [the longest x1 1.79 us: on_device(): y1 = lax.ppermute(y1, 'gy', pairs(DY, False))]
  transfers between devices with their start and end apart: 5 -> 7, of which waited for: 1 -> 2; matrix products, arithmetic and copies ran while one was open for 1% -> 0% of each run, Pallas kernels for 4% -> 0%
where the time goes in v2:
time: 72.8 us; the launch traced here: 72.3 us
  blocking collectives  46.4 us (64%)
  starting transfers between devices  12.5 us (17%)
  Pallas kernels  5.84 us (8%)
  local copies, waits for them, and re-layouts  4.62 us (6%)
  waiting for transfers between devices  2.95 us (4%)
    all_to_all x1, blocking collectives, on_device(): r1 = lax.all_to_all(a.reshape(DY, 8, 128), 'gy', 0, 0)  22.8 us
    all_to_all x1, blocking collectives, on_device(): r2 = lax.all_to_all(scanned, 'gy', 0, 0)  12.6 us
    all_to_all x1, blocking collectives, on_device(): r3 = lax.all_to_all(s.reshape(DZ, 32, 128), 'gz', 0, 0)  11 us
    ppermute x3, starting transfers between devices, across(): return lax.ppermute(value, 'gz', [(i, i ^ bit) for i in range(DZ)])  5.84 us
    unnamed x12, local copies, waits for them, and re-layouts  4.62 us
    ppermute x1, starting transfers between devices, on_device(): z1 = lax.ppermute(z1, 'gz', pairs(DZ, False))  3.33 us
    pallas_call x1, Pallas kernels, on_device(): call(local_kernel, [(LY, LZ, NX), (256, 128), (2, LY, NX)], [VMEM, HBM] +...  3.07 us
    pallas_call x1, Pallas kernels, on_device(): call(final_kernel, [(LY, LZ, NX)], [VMEM] * 5 + [HBM, SMEM], [HBM], [pltp...  2.09 us
  transfers between devices with their start and end apart: 7, of which 2 were waited for; matrix products, arithmetic and copies ran while one was open for 0% of the time, Pallas kernels for 0%

profile of v2, /device:TPU:1, one launch (start us, length us, event | category | flops | bytes accessed | tf_op | source)
XLA Modules:
  0.0 72.3 jit_solution(10922934227524491396)
XLA Ops:
  0.0 0.0 copy-start.2
  0.0 1.2 %copy-done.2 = f32[16,8,2048]{2,1,0:T(8,128)S(1)} copy-done((f32[16,8,2048]{2,1,0:T(8,128)S(1)}, f32[16,8,2048]{2,1,0:T(8,128)}, u32[]{:S(2)}) %copy-start.2) | copy-done | bytes 1048600
  1.2 0.2 faces.1
  1.4 3.3 %collective-permute-start.2 = (f32[16,2048]{1,0:T(8,128)S(1)}, f32[16,2048]{1,0:T(8,128)S(1)}, u32[]{:S(2)}, u32[]{:S(2)}) collective-permute-start(f32[16,2048]{1,0:T(8,128)S(1)} %get-tuple-element.23), channel_id=1, source_target_pairs={{0,1},{1,0},{2,3},{3,2},{4,5},{5,4},{6,7},{7,6},{8,9},{9,8},{10,11... | collective-permute-start | bytes 393224 | tf_op jit(solution)/shard_map/ppermute | solution.py:325
  4.7 1.9 %collective-permute-start.3 = (f32[16,2048]{1,0:T(8,128)S(1)}, f32[16,2048]{1,0:T(8,128)S(1)}, u32[]{:S(2)}, u32[]{:S(2)}) collective-permute-start(f32[16,2048]{1,0:T(8,128)S(1)} %get-tuple-element.24), channel_id=1, source_target_pairs={{1,2},{2,1},{3,4},{4,3},{5,6},{6,5},{9,10},{10,9},{11,12},{12,11},... | collective-permute-start | bytes 393224 | tf_op jit(solution)/shard_map/ppermute | solution.py:326
  6.6 0.8 %collective-permute-start = (f32[8,2048]{1,0:T(8,128)S(1)}, f32[8,2048]{1,0:T(8,128)S(1)}, u32[]{:S(2)}, u32[]{:S(2)}) collective-permute-start(f32[8,2048]{1,0:T(8,128)S(1)} %get-tuple-element.21), channel_id=1, source_target_pairs={{0,8},{8,0},{16,24},{24,16},{32,40},{40,32},{48,56},{56,48},{64,72... | collective-permute-start | bytes 196616 | tf_op jit(solution)/shard_map/ppermute | solution.py:323
  7.4 0.7 collective-permute-start.1
  8.1 1.8 %collective-permute-done.y1_ref = f32[8,2048]{1,0:T(8,128)S(1)} collective-permute-done((f32[8,2048]{1,0:T(8,128)S(1)}, f32[8,2048]{1,0:T(8,128)S(1)}, u32[]{:S(2)}, u32[]{:S(2)}) %collective-permute-start) | collective-permute-done | bytes 65568 | tf_op jit(solution)/shard_map/ppermute | solution.py:323
  9.8 0.0 collective-permute-done.1.y2_ref
  9.9 0.0 collective-permute-done.2.z1_ref
  9.9 1.1 %collective-permute-done.3.z2_ref = f32[16,2048]{1,0:T(8,128)S(1)} collective-permute-done((f32[16,2048]{1,0:T(8,128)S(1)}, f32[16,2048]{1,0:T(8,128)S(1)}, u32[]{:S(2)}, u32[]{:S(2)}) %collective-permute-start.3) | collective-permute-done | bytes 131104 | tf_op jit(solution)/shard_map/ppermute | solution.py:326
  11.0 0.0 copy-start
  11.0 1.4 %copy-done = bf16[3,16,8,2048]{3,2,1,0:T(8,128)(2,1)S(1)} copy-done((bf16[3,16,8,2048]{3,2,1,0:T(8,128)(2,1)S(1)}, bf16[3,16,8,2048]{3,2,1,0:T(8,128)(2,1)}, u32[]{:S(2)}) %copy-start) | copy-done | bytes 1572888
  12.4 0.0 copy-start.3
  12.4 1.0 %copy-done.3 = f32[40,24,128]{2,1,0:T(8,128)S(1)} copy-done((f32[40,24,128]{2,1,0:T(8,128)S(1)}, f32[40,24,128]{2,1,0:T(8,128)}, u32[]{:S(2)}) %copy-start.3) | copy-done | bytes 491544
  13.4 0.0 copy-start.4
  13.4 0.9 %copy-done.4 = bf16[2,256,256]{2,1,0:T(8,128)(2,1)S(1)} copy-done((bf16[2,256,256]{2,1,0:T(8,128)(2,1)S(1)}, bf16[2,256,256]{2,1,0:T(8,128)(2,1)}, u32[]{:S(2)}) %copy-start.4) | copy-done | bytes 262168
  14.4 0.0 copy-start.1
  14.4 3.1 %local.1 = (f32[16,8,2048]{2,1,0:T(8,128)S(1)}, f32[256,128]{1,0:T(8,128)S(1)}, f32[2,16,2048]{2,1,0:T(8,128)S(1)}) custom-call(f32[16,8,2048]{2,1,0:T(8,128)S(1)} %get-tuple-element.20.t_ref, bf16[3,16,8,2048]{3,2,1,0:T(8,128)(2,1)S(1)} %copy-done, f32[8,2048]{1,0:T(8,128)S(1)} %collective-permute-done.y1_ref, f32[8,2048]{1,0:T(8,128)S(1)} %collective-permute-done.1.y2_ref, ...), custom_call_target="tpu_custom_call" | custom-call | tf_op jit(solution)/shard_map/local/pallas_call | solution.py:327
  17.5 0.0 copy-start.5
  17.5 0.1 collective-permute-start.4
  17.6 22.8 %all_to_all.15.r_ref = f32[32,8,128]{2,1,0:T(8,128)S(1)} all-to-all(f32[32,8,128]{2,1,0:T(8,128)S(1)} %bitcast.6), channel_id=1, replica_groups=mesh['gy'=32,'gz'=8] {'gy'}, dimensions={0} | all-to-all | bytes 262144 | tf_op jit(solution)/shard_map/all_to_all | solution.py:347
  40.4 0.0 collective-permute-done.4.x_ref
  40.4 0.1 scan.1
  40.4 3.4 %collective-permute-start.5 = (f32[2,16,2048]{2,1,0:T(8,128)S(1)}, f32[2,16,2048]{2,1,0:T(8,128)S(1)}, u32[]{:S(2)}, u32[]{:S(2)}) collective-permute-start(f32[2,16,2048]{2,1,0:T(8,128)S(1)} %get-tuple-element.29.tot_ref), channel_id=1, source_target_pairs={{0,2},{1,3},{2,0},{3,1},{4,6},{5,7},{6,4},{7,5},{8,10},{9,11},{10,... | collective-permute-start | bytes 786440 | tf_op jit(solution)/shard_map/ppermute | solution.py:314
  43.8 12.6 %all_to_all.16 = f32[32,8,128]{2,1,0:T(8,128)S(1)} all-to-all(f32[32,8,128]{2,1,0:T(8,128)S(1)} %get-tuple-element.28), channel_id=1, replica_groups=mesh['gy'=32,'gz'=8] {'gy'}, dimensions={0} | all-to-all | bytes 262144 | tf_op jit(solution)/shard_map/all_to_all | solution.py:352
  56.4 0.0 collective-permute-done.5.x_ref
  56.4 0.0 copy-done.1
  56.4 0.4 mixed.1
  56.8 2.4 %collective-permute-start.6 = (f32[16,2048]{1,0:T(8,128)S(1)}, f32[16,2048]{1,0:T(8,128)S(1)}, u32[]{:S(2)}, u32[]{:S(2)}) collective-permute-start(f32[16,2048]{1,0:T(8,128)S(1)} %get-tuple-element.33), channel_id=1, source_target_pairs={{0,4},{1,5},{2,6},{3,7},{4,0},{5,1},{6,2},{7,3},{8,12},{9,13},{10,... | collective-permute-start | bytes 393224 | tf_op jit(solution)/shard_map/ppermute | solution.py:314
  59.2 11.0 %all_to_all.17 = f32[8,32,128]{2,1,0:T(8,128)S(1)} all-to-all(f32[8,32,128]{2,1,0:T(8,128)S(1)} %bitcast.7), channel_id=1, replica_groups=mesh['gy'=32,'gz'=8] {'gz'}, dimensions={0} | all-to-all | bytes 262144 | tf_op jit(solution)/shard_map/all_to_all | solution.py:363
  70.2 0.0 collective-permute-done.6.x_ref
  70.2 0.0 copy-done.5
  70.2 2.1 %final.1 = f32[16,8,2048]{2,1,0:T(8,128)} custom-call(f32[16,8,2048]{2,1,0:T(8,128)S(1)} %get-tuple-element.25.loc_ref, f32[2,8,2048]{2,1,0:T(8,128)S(1)} %get-tuple-element.31.dz_ref, f32[2,16,2048]{2,1,0:T(8,128)S(1)} %get-tuple-element.32.pre_ref, f32[16,2048]{1,0:T(8,128)S(1)} %collective-permute-done.6.x_ref, f32[256,128]{1,0:T(8,128)S(1)} %bitcast.4, ...), custom_call_target="tpu_custom_call" | custom-call | tf_op jit(solution)/shard_map/final/pallas_call | solution.py:364
Async XLA Ops:
  0.0 1.2 %copy-start.2 = (f32[16,8,2048]{2,1,0:T(8,128)S(1)}, f32[16,8,2048]{2,1,0:T(8,128)}, u32[]{:S(2)}) copy-start(f32[16,8,2048]{2,1,0:T(8,128)} %t_hbm.1) | copy-start | bytes 3145732
  1.4 8.5 %collective-permute-start.2 = (f32[16,2048]{1,0:T(8,128)S(1)}, f32[16,2048]{1,0:T(8,128)S(1)}, u32[]{:S(2)}, u32[]{:S(2)}) collective-permute-start(f32[16,2048]{1,0:T(8,128)S(1)} %get-tuple-element.23), channel_id=1, source_target_pairs={{0,1},{1,0},{2,3},{3,2},{4,5},{5,4},{6,7},{7,6},{8,9},{9,8},{10,11... | collective-permute-start | bytes 393224 | tf_op jit(solution)/shard_map/ppermute | solution.py:325
  4.7 6.3 %collective-permute-start.3 = (f32[16,2048]{1,0:T(8,128)S(1)}, f32[16,2048]{1,0:T(8,128)S(1)}, u32[]{:S(2)}, u32[]{:S(2)}) collective-permute-start(f32[16,2048]{1,0:T(8,128)S(1)} %get-tuple-element.24), channel_id=1, source_target_pairs={{1,2},{2,1},{3,4},{4,3},{5,6},{6,5},{9,10},{10,9},{11,12},{12,11},... | collective-permute-start | bytes 393224 | tf_op jit(solution)/shard_map/ppermute | solution.py:326
  6.6 3.2 %collective-permute-start = (f32[8,2048]{1,0:T(8,128)S(1)}, f32[8,2048]{1,0:T(8,128)S(1)}, u32[]{:S(2)}, u32[]{:S(2)}) collective-permute-start(f32[8,2048]{1,0:T(8,128)S(1)} %get-tuple-element.21), channel_id=1, source_target_pairs={{0,8},{8,0},{16,24},{24,16},{32,40},{40,32},{48,56},{56,48},{64,72... | collective-permute-start | bytes 196616 | tf_op jit(solution)/shard_map/ppermute | solution.py:323
  7.4 2.4 %collective-permute-start.1 = (f32[8,2048]{1,0:T(8,128)S(1)}, f32[8,2048]{1,0:T(8,128)S(1)}, u32[]{:S(2)}, u32[]{:S(2)}) collective-permute-start(f32[8,2048]{1,0:T(8,128)S(1)} %get-tuple-element.22), channel_id=1, source_target_pairs={{8,16},{16,8},{24,32},{32,24},{40,48},{48,40},{56,64},{64,56},{72,... | collective-permute-start | bytes 196616 | tf_op jit(solution)/shard_map/ppermute | solution.py:324
  11.0 1.4 %copy-start = (bf16[3,16,8,2048]{3,2,1,0:T(8,128)(2,1)S(1)}, bf16[3,16,8,2048]{3,2,1,0:T(8,128)(2,1)}, u32[]{:S(2)}) copy-start(bf16[3,16,8,2048]{3,2,1,0:T(8,128)(2,1)} %v_hbm.1) | copy-start | bytes 4718596
  12.4 1.0 %copy-start.3 = (f32[40,24,128]{2,1,0:T(8,128)S(1)}, f32[40,24,128]{2,1,0:T(8,128)}, u32[]{:S(2)}) copy-start(f32[40,24,128]{2,1,0:T(8,128)} %constant.8.clone.lines_hbm) | copy-start | bytes 1474564
  13.4 0.9 %copy-start.4 = (bf16[2,256,256]{2,1,0:T(8,128)(2,1)S(1)}, bf16[2,256,256]{2,1,0:T(8,128)(2,1)}, u32[]{:S(2)}) copy-start(bf16[2,256,256]{2,1,0:T(8,128)(2,1)} %constant.9.clone.wx_hbm) | copy-start | bytes 786436
  14.4 42.0 %copy-start.1 = (f32[40,16,128]{2,1,0:T(8,128)S(1)}, f32[40,16,128]{2,1,0:T(8,128)}, u32[]{:S(2)}) copy-start(f32[40,16,128]{2,1,0:T(8,128)} %constant.10.clone.sums_hbm) | copy-start | bytes 983044
  17.5 52.8 %copy-start.5 = (f32[32,128]{1,0:T(8,128)S(1)}, f32[32,128]{1,0:T(8,128)}, u32[]{:S(2)}) copy-start(f32[32,128]{1,0:T(8,128)} %constant.11.clone.scal_ref) | copy-start | bytes 49156
  17.5 22.9 %collective-permute-start.4 = (f32[2,16,2048]{2,1,0:T(8,128)S(1)}, f32[2,16,2048]{2,1,0:T(8,128)S(1)}, u32[]{:S(2)}, u32[]{:S(2)}) collective-permute-start(f32[2,16,2048]{2,1,0:T(8,128)S(1)} %get-tuple-element.27.c_ref), channel_id=1, source_target_pairs={{0,1},{1,0},{2,3},{3,2},{4,5},{5,4},{6,7},{7,6},{8,9},{9,8},{10,11... | collective-permute-start | bytes 786440 | tf_op jit(solution)/shard_map/ppermute | solution.py:314
  40.4 16.0 %collective-permute-start.5 = (f32[2,16,2048]{2,1,0:T(8,128)S(1)}, f32[2,16,2048]{2,1,0:T(8,128)S(1)}, u32[]{:S(2)}, u32[]{:S(2)}) collective-permute-start(f32[2,16,2048]{2,1,0:T(8,128)S(1)} %get-tuple-element.29.tot_ref), channel_id=1, source_target_pairs={{0,2},{1,3},{2,0},{3,1},{4,6},{5,7},{6,4},{7,5},{8,10},{9,11},{10,... | collective-permute-start | bytes 786440 | tf_op jit(solution)/shard_map/ppermute | solution.py:314
  56.8 13.4 %collective-permute-start.6 = (f32[16,2048]{1,0:T(8,128)S(1)}, f32[16,2048]{1,0:T(8,128)S(1)}, u32[]{:S(2)}, u32[]{:S(2)}) collective-permute-start(f32[16,2048]{1,0:T(8,128)S(1)} %get-tuple-element.33), channel_id=1, source_target_pairs={{0,4},{1,5},{2,6},{3,7},{4,0},{5,1},{6,2},{7,3},{8,12},{9,13},{10,... | collective-permute-start | bytes 393224 | tf_op jit(solution)/shard_map/ppermute | solution.py:314

commit v3 on v2

v3 whole, which is shorter than its diff:
```python
import jax
import jax.numpy as jnp
import numpy as np
from jax import lax
from jax.experimental import pallas as pl
from jax.experimental.pallas import tpu as pltpu
from jax.sharding import PartitionSpec as P

NX, NY, NZ = 2048, 512, 64
RX, RY, RZ = 1, 768, 192
DY, DZ = 32, 8
GX, GZ = 4, 8
Q = NX // GX
LY, LZ = NY // DY, NZ // DZ
XB = 256
NB = NX // XB
KAPPA = 0.15
F32, BF16 = jnp.float32, jnp.bfloat16


def decay(ratio):
    half = 0.5 / ratio
    return 1.0 + half - np.sqrt(half * (2.0 + half))


def line_factors(count, ratio):
    q = decay(ratio)
    i = np.arange(count)
    low = 1.0 - q ** (2.0 * (i + 1))
    high = 1.0 - q ** (2.0 * (count - i))
    denom = ratio * (1.0 - q * q) * (1.0 - q ** (2.0 * count + 2))
    return q, low, high, denom


def split_line(count, ratio, parts):
    q, low, high, denom = line_factors(count, ratio)
    size = count // parts
    low, high = low.reshape(parts, size), high.reshape(parts, size)
    m = np.arange(size)
    small = np.minimum(m[:, None], m[None])
    large = np.maximum(m[:, None], m[None])
    block = q ** (large - small + 1.0) * low[:, small] * high[:, large] / denom
    up = q ** (size - 1.0 - m) * low
    down = q ** (1.0 * m) * high
    from_low = q ** (m + 2.0) * high / denom
    from_high = q ** (size + 1.0 - m) * low / denom
    return block, up, down, from_low, from_high, q**size


QX, QY, QZ = decay(RX), decay(RY), decay(RZ)


def tables():
    block_y, up_y, down_y, gl_y, gh_y, step_y = split_line(NY, RY, DY)
    block_z, up_z, down_z, gl_z, gh_z, step_z = split_line(NZ, RZ, DZ)
    sums = np.zeros((DY + DZ, 16, 128))
    tm = sums[DY:]
    tm[:, :8, :8] = block_z
    for e in range(DZ):
        for p in range(DZ):
            if p > e:
                tm[e, 8 + p, :8] = up_z[e] * step_z ** (p - e - 1)
            if p < e:
                tm[e, 8 + p, :8] = down_z[e] * step_z ** (e - p - 1)
    tm[:, :8, 8] = gl_z
    tm[:, :8, 9] = gh_z
    sums[:DY, :, 0] = gl_y
    sums[:DY, :, 1] = gh_y
    scal = np.zeros((DY, 128))
    scal[:, :16] = gl_y
    scal[:, 16:32] = gh_y
    scal[:, 32:48] = up_y
    scal[:, 48:64] = down_y
    group = step_y**GX
    for d in range(DY):
        z, x = d // GX, d % GX
        for i in range(GX):
            xi = x ^ i
            scal[d, 64 + i] = step_y ** (GX - 1 - xi)
            scal[d, 68 + i] = step_y**xi
            for j in range(GX):
                xj = x ^ j
                if xj < xi:
                    scal[d, 80 + 4 * i + j] = step_y ** (xi - xj - 1)
                if xj > xi:
                    scal[d, 96 + 4 * i + j] = step_y ** (xj - xi - 1)
        for p in range(GZ):
            if p != z:
                scal[d, 72 + p] = group ** (abs(p - z) - 1)
    f32 = lambda a: a.astype(np.float32)
    return f32(sums), f32(scal), float(step_z)


SUMS, SCAL, STEP_Z = tables()
ROWS = LY * LZ


def halves(value):
    high = value.astype(BF16)
    return high, (value - high.astype(F32)).astype(BF16)


def mm(a, b):
    return jnp.dot(a, b, preferred_element_type=F32)


def start(*pairs_and_sem):
    copies = [pltpu.make_async_copy(*p) for p in pairs_and_sem]
    for c in copies:
        c.start()
    return copies


def power(q, k):
    return jnp.exp2(k * float(np.log2(q)))


def solve_x(high, low, wx_ref, g, put):
    lines = high.shape[1]
    wh, wl = wx_ref[0], wx_ref[1]
    xh = high[...].reshape(NB * lines, XB)
    xl = low[...].reshape(NB * lines, XB)
    g[...] = (mm(xh, wh) + (mm(xh, wl) + mm(xl, wh))).reshape(NB, lines, XB)
    lane = lax.broadcasted_iota(jnp.int32, (8, 128), 1).astype(F32)
    left, right = power(QX, lane + 1.0)[0:1], power(QX, 128.0 - lane)[0:1]
    for b in range(NB):
        before = g[b - 1, :, XB - 1 :] if b > 0 else g[0, :, :1] * (-QX)
        after = g[b + 1, :, :1] if b < NB - 1 else g[NB - 1, :, XB - 1 :] * (-QX)
        put(2 * b, g[b, :, :128] + before * left)
        put(2 * b + 1, g[b, :, 128:] + after * right)


def faces_kernel(t_ref, y1_ref, y2_ref, z1_ref, z2_ref):
    d, e = lax.axis_index("gy"), lax.axis_index("gz")
    odd_y, odd_z = (d % 2) == 1, (e % 2) == 1
    first, last = t_ref[0], t_ref[LY - 1]
    y1_ref[...] = jnp.where(odd_y, first, last)
    y2_ref[...] = jnp.where(odd_y, last, first)
    for y in range(LY):
        bottom, top = t_ref[y, 0:1, :], t_ref[y, LZ - 1 : LZ, :]
        z1_ref[y : y + 1, :] = jnp.where(odd_z, bottom, top)
        z2_ref[y : y + 1, :] = jnp.where(odd_z, top, bottom)


def inner_kernel(t_ref, v_ref, scal_ref, f_ref, mf_ref, ml_ref, wx_ref, tv_ref):
    d, e = lax.axis_index("gy"), lax.axis_index("gz")
    zi = lax.broadcasted_iota(jnp.int32, (LZ, NX), 0)
    xi = lax.broadcasted_iota(jnp.int32, (LZ, NX), 1)
    nothing = jnp.zeros((LZ, NX), F32)
    for y in range(LY):
        t = t_ref[y]
        north = t_ref[y + 1] if y < LY - 1 else nothing
        south = t_ref[y - 1] if y > 0 else nothing
        ceil = jnp.where(zi == LZ - 1, 0.0, pltpu.roll(t, LZ - 1, 0))
        floor = jnp.where(zi == 0, 0.0, pltpu.roll(t, 1, 0))
        east = jnp.where(xi == NX - 1, 0.0, pltpu.roll(t, NX - 1, 1))
        west = jnp.where(xi == 0, 0.0, pltpu.roll(t, 1, 1))
        lap = ((east + west) + (north + south)) + (ceil + floor) - 6.0 * t
        adv = (v_ref[0, y].astype(F32) * (east - west) + v_ref[1, y].astype(F32) * (north - south)
               + v_ref[2, y].astype(F32) * (ceil - floor))
        f_ref[y] = t + KAPPA * lap - 0.5 * adv
    i = lax.broadcasted_iota(jnp.int32, (XB, XB), 0)
    j = lax.broadcasted_iota(jnp.int32, (XB, XB), 1)
    w = power(QX, (jnp.abs(i - j) + 1).astype(F32)) * (1.0 / (RX * (1 - QX * QX)))
    wx_ref[0], wx_ref[1] = halves(w)
    row = scal_ref[pl.ds(d, 1), :]
    r = lax.broadcasted_iota(jnp.int32, (128, 128), 0)
    c = lax.broadcasted_iota(jnp.int32, (128, 128), 1)
    tv_ref[...] = jnp.broadcast_to(jnp.sum(jnp.where(r == c, row, 0.0), axis=1, keepdims=True), (128, 128))
    lane = lax.broadcasted_iota(jnp.int32, (16, 128), 1)
    sub = lax.broadcasted_iota(jnp.int32, (16, 128), 0)

    def block(q, ratio, count, first, own, other):
        small = (jnp.minimum(own, other) + first + 1).astype(F32)
        large = (count - first - jnp.maximum(own, other)).astype(F32)
        gap = (jnp.abs(own - other) + 1).astype(F32)
        return (power(q, gap) * (1.0 - power(q, 2.0 * small)) * (1.0 - power(q, 2.0 * large))
                * (1.0 / (ratio * (1 - q * q) * (1 - q ** (2.0 * count + 2)))))

    my = block(QY, RY, NY, d * LY, sub, lane // LZ)
    w8 = (lane % LZ)[:8]
    mz = block(QZ, RZ, NZ, e * LZ, sub[:8], w8)
    up = power(QZ, (LZ - 1 - w8).astype(F32)) * (1.0 - power(QZ, 2.0 * (w8 + e * LZ + 1).astype(F32)))
    down = power(QZ, w8.astype(F32)) * (1.0 - power(QZ, 2.0 * (NZ - e * LZ - w8).astype(F32)))
    for l in range(LY // 2):
        pair = jnp.concatenate([my[2 * l : 2 * l + 1] * mz, my[2 * l + 1 : 2 * l + 2] * mz], axis=0)
        high, low = halves(pair)
        mf_ref[16 * l : 16 * l + 16, :128] = high
        mf_ref[16 * l : 16 * l + 16, 128:] = high
        ml_ref[16 * l : 16 * l + 16] = low
    for k, part in ((0, up), (1, down)):
        high, low = halves(my * part[0:1])
        at = ROWS + 16 * k
        mf_ref[at : at + 16, :128] = high
        mf_ref[at : at + 16, 128:] = high
        ml_ref[at : at + 16] = low


def source_kernel(f0_ref, v_ref, y1_ref, y2_ref, z1_ref, z2_ref, wx_ref, tv_ref,
                  f_ref, own_ref, s1_ref, s2_ref, s3_ref, ah, al, g, a4):
    d, e = lax.axis_index("gy"), lax.axis_index("gz")
    odd_y, odd_z = (d % 2) == 1, (e % 2) == 1
    zi = lax.broadcasted_iota(jnp.int32, (LZ, XB), 0)
    for b in range(NB):
        cols = slice(b * XB, (b + 1) * XB)
        sums = [jnp.zeros((LZ, XB), F32), jnp.zeros((LZ, XB), F32)]
        for y in range(LY):
            f = f0_ref[y, :, cols]
            w = 0.5 * v_ref[2, y, :, cols].astype(F32)
            h1, h2 = z1_ref[y : y + 1, cols], z2_ref[y : y + 1, cols]
            above, below = jnp.where(odd_z, h2, h1), jnp.where(odd_z, h1, h2)
            f += jnp.where(zi == 0, (KAPPA + w) * below, jnp.where(zi == LZ - 1, (KAPPA - w) * above, 0.0))
            if y == 0:
                south = jnp.where(odd_y, y1_ref[:, cols], y2_ref[:, cols])
                f += (KAPPA + 0.5 * v_ref[1, y, :, cols].astype(F32)) * south
            if y == LY - 1:
                north = jnp.where(odd_y, y2_ref[:, cols], y1_ref[:, cols])
                f += (KAPPA - 0.5 * v_ref[1, y, :, cols].astype(F32)) * north
            f_ref[y, :, cols] = f
            for k in range(2):
                c = tv_ref[32 + 16 * k + y : 33 + 16 * k + y, :]
                sums[k] += f * jnp.concatenate([c, c], axis=1)
        high, low = halves(jnp.concatenate(sums, axis=0))
        ah[b] = high
        al[b] = low

    def put(t, part):
        for k in range(2):
            a4[t // 4, k, :, (t % 4) * 128 : (t % 4 + 1) * 128] = part[8 * k : 8 * k + 8]

    solve_x(ah, al, wx_ref, g, put)
    x = lax.rem(d, GX)
    for i, ref in enumerate((own_ref, s1_ref, s2_ref, s3_ref)):
        ref[...] = a4[lax.bitwise_xor(x, i)]


def local_kernel(f_ref, wx_ref, mf_ref, ml_ref, loc_ref, c_ref, fh, fl, g, ghl):
    for b in range(NB):
        high, low = halves(f_ref[:, :, b * XB : (b + 1) * XB].reshape(ROWS, XB))
        fh[b] = high
        fl[b] = low

    def put(t, part):
        high, low = halves(part)
        ghl[:ROWS, t * 128 : (t + 1) * 128] = high
        ghl[ROWS:, t * 128 : (t + 1) * 128] = low

    solve_x(fh, fl, wx_ref, g, put)
    for b in range(NB):
        cols = slice(b * XB, (b + 1) * XB)
        out = mm(mf_ref[...], ghl[:, cols]) + mm(ml_ref[...], ghl[:ROWS, cols])
        loc_ref[:, :, cols] = out[:ROWS].reshape(LY, LZ, XB)
        c_ref[0, :, cols] = out[ROWS : ROWS + 16]
        c_ref[1, :, cols] = out[ROWS + 16 :]


def group_kernel(a_ref, b_ref, c_ref, d_ref, tv_ref, o_ref):
    z = lax.axis_index("gy") // GX
    parts = (a_ref, b_ref, c_ref, d_ref)
    for t in range(Q // 128):
        cols = slice(t * 128, (t + 1) * 128)
        tot = []
        for k in range(2):
            base = 64 + 4 * k
            tot.append(sum(tv_ref[base + i : base + i + 1, :] * parts[i][k, :, cols] for i in range(4)))
        for p in range(GZ):
            o_ref[p, :, cols] = tv_ref[72 + p : 73 + p, :] * jnp.where(p > z, tot[0], tot[1])


def spread_kernel(a_ref, b_ref, c_ref, d_ref, r_ref, tv_ref, cs_ref, x_ref,
                  own_ref, s1_ref, s2_ref, s3_ref, tot_ref, pre_ref):
    d, e = lax.axis_index("gy"), lax.axis_index("gz")
    z = d // GX
    parts = (a_ref, b_ref, c_ref, d_ref)
    outs = (own_ref, s1_ref, s2_ref, s3_ref)
    for t in range(Q // 128):
        cols = slice(t * 128, (t + 1) * 128)
        low = jnp.zeros((8, 128), F32)
        high = jnp.zeros((8, 128), F32)
        for p in range(GZ):
            part = r_ref[p, :, cols]
            low += jnp.where(p < z, part, 0.0)
            high += jnp.where(p > z, part, 0.0)
        for k, group in ((0, low), (1, high)):
            vals = [ref[k, :, cols] for ref in parts]
            for i in range(4):
                at = 68 + i if k == 0 else 64 + i
                total = tv_ref[at : at + 1, :] * group
                for j in range(4):
                    if j != i:
                        row = 80 + 16 * k + 4 * i + j
                        total += tv_ref[row : row + 1, :] * vals[j]
                outs[i][k, :, cols] = total
    upper = (e % 2) == 1
    near, far = jnp.where(upper, 1.0, STEP_Z), jnp.where(upper, STEP_Z, 1.0)
    tot_ref[0] = near * cs_ref[0] + far * x_ref[0]
    tot_ref[1] = far * cs_ref[1] + near * x_ref[1]
    pre_ref[0] = jnp.where(upper, x_ref[0], 0.0)
    pre_ref[1] = jnp.where(upper, 0.0, x_ref[1])


def mixed_kernel(p0_ref, p1_ref, p2_ref, p3_ref, tot_ref, x_ref, pre_ref, sums_hbm,
                 dz_ref, s_ref, send_ref, pre2_ref, p4, tm_ref, sem):
    e = lax.axis_index("gz")
    load = pltpu.make_async_copy(sums_hbm.at[DY + e], tm_ref, sem)
    load.start()
    x = lax.rem(lax.axis_index("gy"), GX)
    for i, ref in enumerate((p0_ref, p1_ref, p2_ref, p3_ref)):
        p4[lax.bitwise_xor(x, i)] = ref[...]
    upper = ((e // 2) % 2) == 1
    odd = (e % 2) == 1
    two = STEP_Z * STEP_Z
    near, far = jnp.where(upper, 1.0, two), jnp.where(upper, two, 1.0)
    top = (e // 4) == 1
    send_ref[...] = jnp.where(top, far * tot_ref[1] + near * x_ref[1], near * tot_ref[0] + far * x_ref[0])
    low = jnp.where(odd, STEP_Z, 1.0)
    high = jnp.where(odd, 1.0, STEP_Z)
    pre2_ref[0] = pre_ref[0] + jnp.where(upper, low * x_ref[0], 0.0)
    pre2_ref[1] = pre_ref[1] + jnp.where(upper, 0.0, high * x_ref[1])
    load.wait()
    tm = tm_ref[...]
    own = [jnp.broadcast_to(tm[:8, w : w + 1], (8, 128)) for w in range(8)]
    out = [jnp.broadcast_to(tm[8:, w : w + 1], (8, 128)) for w in range(8)]
    for k in range(2):
        for t in range(16):
            p = p4[t // 4, k, :, (t % 4) * 128 : (t % 4 + 1) * 128]
            one = own[0] * p[0:1]
            two = out[0] * p[0:1]
            for w in range(1, 8):
                one += own[w] * p[w : w + 1]
                two += out[w] * p[w : w + 1]
            dz_ref[k, :, t * 128 : (t + 1) * 128] = one
            s_ref[pl.ds(k * 16 + t, 8, stride=32), :] = two


def final_kernel(loc_ref, dz_ref, pre_ref, x_ref, r_ref, sums_hbm, tv_ref, o_hbm,
                 cl, ch, o_ref, tg_ref, tm_ref, sems):
    d, e = lax.axis_index("gy"), lax.axis_index("gz")
    loads = start((sums_hbm.at[d], tg_ref, sems.at[0]), (sums_hbm.at[DY + e], tm_ref, sems.at[1]))
    lo = jnp.zeros((32, 128), F32)
    hi = jnp.zeros((32, 128), F32)
    for p in range(DZ):
        part = r_ref[p * 32 : (p + 1) * 32, :]
        lo += jnp.where(p < e, part, 0.0)
        hi += jnp.where(p > e, part, 0.0)
    top = (e // 4) == 1
    at = lax.rem(e, 4)
    power = lambda k: jnp.where(k == 0, 1.0, jnp.where(k == 1, STEP_Z, jnp.where(k == 2, STEP_Z**2, STEP_Z**3)))
    up = jnp.where(top, power(at), 0.0)
    down = jnp.where(top, 0.0, power(3 - at))
    for load in loads:
        load.wait()
    tg, tm = tg_ref[...], tm_ref[...]
    ga = jnp.broadcast_to(tg[:, 0:1], (16, 128))
    gb = jnp.broadcast_to(tg[:, 1:2], (16, 128))
    for t in range(NX // 128):
        cols = slice(t * 128, (t + 1) * 128)
        cl[:, cols] = (pre_ref[0, :, cols] + up * x_ref[:, cols]) + (ga * lo[t : t + 1] + gb * lo[16 + t : 17 + t])
        ch[:, cols] = (pre_ref[1, :, cols] + down * x_ref[:, cols]) + (ga * hi[t : t + 1] + gb * hi[16 + t : 17 + t])
    hl = jnp.broadcast_to(tm[:8, 8:9], (8, 128))
    hh = jnp.broadcast_to(tm[:8, 9:10], (8, 128))
    stores = []
    for l in range(LY):
        for t in range(NX // 128):
            cols = slice(t * 128, (t + 1) * 128)
            o_ref[l, :, cols] = (
                loc_ref[l, :, cols] + tv_ref[l : l + 1, :] * dz_ref[0, :, cols]
                + tv_ref[16 + l : 17 + l, :] * dz_ref[1, :, cols]
                + (hl * cl[l : l + 1, cols] + hh * ch[l : l + 1, cols]))
        if l % 4 == 3:
            i = l // 4
            stores += start((o_ref.at[pl.ds(l - 3, 4)], o_hbm.at[pl.ds(l - 3, 4)], sems.at[2 + i]))
    for store in stores:
        store.wait()


VMEM = pl.BlockSpec(memory_space=pltpu.VMEM)
HBM = pl.BlockSpec(memory_space=pltpu.HBM)
FULL, QUARTER, SUMS_Z = (LY, LZ, NX), (2, LZ, Q), (2, LY, NX)


def call(kernel, outs, ins, out_specs, scratch, mib, name, cost=None):
    if cost is not None:
        cost = pl.CostEstimate(flops=cost[0], bytes_accessed=cost[1], transcendentals=0)
    return pl.pallas_call(
        kernel,
        out_shape=tuple(o if isinstance(o, jax.ShapeDtypeStruct) else jax.ShapeDtypeStruct(o, F32) for o in outs),
        in_specs=ins,
        out_specs=tuple(out_specs),
        scratch_shapes=scratch,
        compiler_params=pltpu.CompilerParams(vmem_limit_bytes=mib * 2**20),
        cost_estimate=cost,
        name=name,
    )


def pairs(count, odd):
    out = []
    for i in range(count):
        j = i + 1 if (i % 2 == 1) == odd else i - 1
        if 0 <= j < count:
            out.append((i, j))
    return out


def across(value, axis, count, bit):
    return lax.ppermute(value, axis, [(i, i ^ bit) for i in range(count)])


COLUMN = [[z * GX + x for z in range(GZ)] for x in range(GX)]


def on_device(temp, vel):
    dma = pltpu.SemaphoreType.DMA
    bf = lambda *shape: jax.ShapeDtypeStruct(shape, BF16)
    y1, y2, z1, z2 = call(
        faces_kernel, [(LZ, NX), (LZ, NX), (LY, NX), (LY, NX)], [VMEM], [VMEM] * 4, [], 4, "faces"
    )(temp)
    y1 = lax.ppermute(y1, "gy", pairs(DY, False))
    y2 = lax.ppermute(y2, "gy", pairs(DY, True))
    z1 = lax.ppermute(z1, "gz", pairs(DZ, False))
    z2 = lax.ppermute(z2, "gz", pairs(DZ, True))
    f, mf, ml, wx, tv = call(
        inner_kernel,
        [FULL, bf(ROWS + 32, 256), bf(ROWS + 32, 128), bf(2, XB, XB), (128, 128)],
        [VMEM] * 3,
        [VMEM] * 5,
        [],
        16,
        "inner",
        (10**7, 8 * 10**6),
    )(temp, vel, SCAL)
    f, *mine = call(
        source_kernel,
        [FULL] + [QUARTER] * 4,
        [VMEM] * 8,
        [VMEM] * 5,
        [
            pltpu.VMEM((NB, 16, XB), BF16),
            pltpu.VMEM((NB, 16, XB), BF16),
            pltpu.VMEM((NB, 16, XB), F32),
            pltpu.VMEM((GX, 2, LZ, Q), F32),
        ],
        16,
        "source",
    )(f, vel, y1, y2, z1, z2, wx, tv)
    sets = [mine[0]] + [across(mine[i], "gy", DY, i) for i in (1, 2, 3)]
    loc, c = call(
        local_kernel,
        [FULL, SUMS_Z],
        [VMEM] * 4,
        [VMEM] * 2,
        [
            pltpu.VMEM((NB, ROWS, XB), BF16),
            pltpu.VMEM((NB, ROWS, XB), BF16),
            pltpu.VMEM((NB, ROWS, XB), F32),
            pltpu.VMEM((2 * ROWS, NX), BF16),
        ],
        16,
        "local",
        (2 * 10**9, 8 * 10**6),
    )(f, wx, mf, ml)
    x1 = across(c, "gz", DZ, 1)
    tots = call(group_kernel, [(GZ, LZ, Q)], [VMEM] * 5, [VMEM], [], 4, "group")(*sets, tv)[0]
    r1 = lax.all_to_all(tots, "gy", 0, 0, axis_index_groups=COLUMN)
    *mine, tot, pre = call(
        spread_kernel, [QUARTER] * 4 + [SUMS_Z] * 2, [VMEM] * 8, [VMEM] * 6, [], 8, "spread"
    )(*sets, r1, tv, c, x1)
    sets = [mine[0]] + [across(mine[i], "gy", DY, i) for i in (1, 2, 3)]
    x2 = across(tot, "gz", DZ, 2)
    dz, s, send, pre = call(
        mixed_kernel,
        [(2, LZ, NX), (256, 128), (LY, NX), SUMS_Z],
        [VMEM] * 7 + [HBM],
        [VMEM] * 4,
        [pltpu.VMEM((GX, 2, LZ, Q), F32), pltpu.VMEM((16, 128), F32), dma],
        8,
        "mixed",
    )(*sets, tot, x2, pre, SUMS)
    x3 = across(send, "gz", DZ, 4)
    r3 = lax.all_to_all(s.reshape(DZ, 32, 128), "gz", 0, 0)
    return call(
        final_kernel,
        [FULL],
        [VMEM] * 5 + [HBM, VMEM],
        [HBM],
        [
            pltpu.VMEM((LY, NX), F32),
            pltpu.VMEM((LY, NX), F32),
            pltpu.VMEM(FULL, F32),
            pltpu.VMEM((16, 128), F32),
            pltpu.VMEM((16, 128), F32),
            dma((6,)),
        ],
        16,
        "final",
    )(loc, dz, pre, x3, r3.reshape(256, 128), SUMS, tv)[0]


def solution(mesh):
    return jax.shard_map(
        on_device,
        mesh=mesh,
        in_specs=(P("gy", "gz", None), P(None, "gy", "gz", None)),
        out_specs=P("gy", "gz", None),
        check_vma=False,
    )
```

time: 72.8 us -> 66.7 us (0.916)
  blocking collectives: 46.4 us -> 13.9 us
  starting transfers between devices: 12.5 us -> 30.3 us
  waiting for transfers between devices: 2.95 us -> 12.4 us
  local copies, waits for them, and re-layouts: 4.62 us -> 3.58 us
    all_to_all x2 -> x0, blocking collectives: 35.4 us -> none  [the longest x1 22.8 us: on_device(): r1 = lax.all_to_all(a.reshape(DY, 8, 128), 'gy', 0, 0)]
    ppermute x3 -> x9, starting transfers between devices: 5.84 us -> 15.3 us  [across(): return lax.ppermute(value, axis, [(i, i ^ bit) for i in range(count)])]
    all_to_all x0 -> x1, starting transfers between devices: none -> 8.26 us  [on_device(): r1 = lax.all_to_all(tots, 'gy', 0, 0, axis_index_groups=COLUMN)]
    all_to_all x0 -> x1, waiting for transfers between devices: none -> 7.8 us  [on_device(): r1 = lax.all_to_all(tots, 'gy', 0, 0, axis_index_groups=COLUMN)]
    ppermute x3 -> x9, waiting for transfers between devices: 0.01 us -> 4.59 us  [across(): return lax.ppermute(value, axis, [(i, i ^ bit) for i in range(count)])]
    all_to_all x1, blocking collectives: 11 us -> 13.9 us  [on_device(): r3 = lax.all_to_all(s.reshape(DZ, 32, 128), 'gz', 0, 0)]
    ppermute x1, waiting for transfers between devices: 1.79 us -> 0.01 us  [on_device(): y1 = lax.ppermute(y1, 'gy', pairs(DY, False))]
    ppermute x1, waiting for transfers between devices: 1.15 us -> 0.01 us  [on_device(): z2 = lax.ppermute(z2, 'gz', pairs(DZ, True))]
  transfers between devices with their start and end apart: 7 -> 14, of which waited for: 2 -> 4; matrix products, arithmetic and copies ran while one was open for 0% -> 0% of each run, Pallas kernels for 0% -> 5%
where the time goes in v3:
time: 66.7 us; the launch traced here: 66.3 us
  starting transfers between devices  30.3 us (45%)
  blocking collectives  13.9 us (21%)
  waiting for transfers between devices  12.4 us (19%)
  Pallas kernels  6.04 us (9%)
  local copies, waits for them, and re-layouts  3.58 us (5%)
    ppermute x9, starting transfers between devices, across(): return lax.ppermute(value, axis, [(i, i ^ bit) for i in range(count)])  15.3 us
    all_to_all x1, blocking collectives, on_device(): r3 = lax.all_to_all(s.reshape(DZ, 32, 128), 'gz', 0, 0)  13.9 us
    all_to_all x1, starting transfers between devices, on_device(): r1 = lax.all_to_all(tots, 'gy', 0, 0, axis_index_groups=COLUMN)  8.26 us
    all_to_all x1, waiting for transfers between devices, on_device(): r1 = lax.all_to_all(tots, 'gy', 0, 0, axis_index_groups=COLUMN)  7.8 us
    ppermute x9, waiting for transfers between devices, across(): return lax.ppermute(value, axis, [(i, i ^ bit) for i in range(count)])  4.59 us
    unnamed x12, local copies, waits for them, and re-layouts  3.58 us
    ppermute x1, starting transfers between devices, on_device(): z1 = lax.ppermute(z1, 'gz', pairs(DZ, False))  3.33 us
    ppermute x1, starting transfers between devices, on_device(): z2 = lax.ppermute(z2, 'gz', pairs(DZ, True))  1.91 us
  transfers between devices with their start and end apart: 14, of which 4 were waited for; matrix products, arithmetic and copies ran while one was open for 0% of the time, Pallas kernels for 5%

profile of v3, /device:TPU:1, one launch (start us, length us, event | category | flops | bytes accessed | tf_op | source)
XLA Modules:
  0.0 66.3 jit_solution(18131553130864147779)
XLA Ops:
  0.0 0.0 copy-start.2
  0.0 1.2 %copy-done.2 = f32[16,8,2048]{2,1,0:T(8,128)S(1)} copy-done((f32[16,8,2048]{2,1,0:T(8,128)S(1)}, f32[16,8,2048]{2,1,0:T(8,128)}, u32[]{:S(2)}) %copy-start.2) | copy-done | bytes 1048600
  1.2 0.0 copy-start.3
  1.2 0.1 faces.1
  1.3 3.3 %collective-permute-start.2 = (f32[16,2048]{1,0:T(8,128)S(1)}, f32[16,2048]{1,0:T(8,128)S(1)}, u32[]{:S(2)}, u32[]{:S(2)}) collective-permute-start(f32[16,2048]{1,0:T(8,128)S(1)} %get-tuple-element.34), channel_id=1, source_target_pairs={{0,1},{1,0},{2,3},{3,2},{4,5},{5,4},{6,7},{7,6},{8,9},{9,8},{10,11... | collective-permute-start | bytes 393224 | tf_op jit(solution)/shard_map/ppermute | solution.py:421
  4.6 1.9 %collective-permute-start.3 = (f32[16,2048]{1,0:T(8,128)S(1)}, f32[16,2048]{1,0:T(8,128)S(1)}, u32[]{:S(2)}, u32[]{:S(2)}) collective-permute-start(f32[16,2048]{1,0:T(8,128)S(1)} %get-tuple-element.35), channel_id=1, source_target_pairs={{1,2},{2,1},{3,4},{4,3},{5,6},{6,5},{9,10},{10,9},{11,12},{12,11},... | collective-permute-start | bytes 393224 | tf_op jit(solution)/shard_map/ppermute | solution.py:422
  6.6 0.9 %collective-permute-start = (f32[8,2048]{1,0:T(8,128)S(1)}, f32[8,2048]{1,0:T(8,128)S(1)}, u32[]{:S(2)}, u32[]{:S(2)}) collective-permute-start(f32[8,2048]{1,0:T(8,128)S(1)} %get-tuple-element.32), channel_id=1, source_target_pairs={{0,8},{8,0},{16,24},{24,16},{32,40},{40,32},{48,56},{56,48},{64,72... | collective-permute-start | bytes 196616 | tf_op jit(solution)/shard_map/ppermute | solution.py:419
  7.5 0.7 collective-permute-start.1
  8.1 0.0 copy-done.3
  8.1 0.0 copy-start
  8.1 1.4 %copy-done = bf16[3,16,8,2048]{3,2,1,0:T(8,128)(2,1)S(1)} copy-done((bf16[3,16,8,2048]{3,2,1,0:T(8,128)(2,1)S(1)}, bf16[3,16,8,2048]{3,2,1,0:T(8,128)(2,1)}, u32[]{:S(2)}) %copy-start) | copy-done | bytes 1572888
  9.5 0.0 copy-start.5
  9.5 0.7 %copy-done.5 = f32[32,128]{1,0:T(8,128)S(1)} copy-done((f32[32,128]{1,0:T(8,128)S(1)}, f32[32,128]{1,0:T(8,128)}, u32[]{:S(2)}) %copy-start.5) | copy-done | bytes 16408
  10.3 0.0 copy-start.1
  10.3 1.1 %inner.1 = (f32[16,8,2048]{2,1,0:T(8,128)S(1)}, bf16[160,256]{1,0:T(8,128)(2,1)S(1)}, bf16[160,128]{1,0:T(8,128)(2,1)S(1)}, bf16[2,256,256]{2,1,0:T(8,128)(2,1)S(1)}, f32[128,128]{1,0:T(8,128)S(1)}) custom-call(f32[16,8,2048]{2,1,0:T(8,128)S(1)} %copy-done.3, bf16[3,16,8,2048]{3,2,1,0:T(8,128)(2,1)S(1)} %copy-done, f32[32,128]{1,0:T(8,128)S(1)} %copy-done.5), custom_call_target="tpu_custom_call" | custom-call | flops 10000000 | bytes 8000000 | tf_op jit(solution)/shard_map/inner/pallas_call | solution.py:423
  11.4 0.0 collective-permute-done.y1_ref
  11.4 0.0 collective-permute-done.1.y2_ref
  11.4 0.0 collective-permute-done.2.z1_ref
  11.4 0.0 collective-permute-done.3.z2_ref
  11.4 0.2 copy-done.1
  11.7 0.9 %source.1 = (f32[16,8,2048]{2,1,0:T(8,128)S(1)}, f32[2,8,512]{2,1,0:T(8,128)S(1)}, f32[2,8,512]{2,1,0:T(8,128)S(1)}, f32[2,8,512]{2,1,0:T(8,128)S(1)}, f32[2,8,512]{2,1,0:T(8,128)S(1)}) custom-call(f32[16,8,2048]{2,1,0:T(8,128)S(1)} %get-tuple-element.31.f0_ref, bf16[3,16,8,2048]{3,2,1,0:T(8,128)(2,1)S(1)} %copy-done.1, ...), custom_call_target="tpu_custom_call" | custom-call | tf_op jit(solution)/shard_map/source/pallas_call | solution.py:433
  12.5 3.5 %collective-permute-start.4 = (f32[2,8,512]{2,1,0:T(8,128)S(1)}, f32[2,8,512]{2,1,0:T(8,128)S(1)}, u32[]{:S(2)}, u32[]{:S(2)}) collective-permute-start(f32[2,8,512]{2,1,0:T(8,128)S(1)} %get-tuple-element.43), channel_id=1, source_target_pairs={{0,8},{8,0},{16,24},{24,16},{32,40},{40,32},{48,56},{56,48},{64,72... | collective-permute-start | bytes 98312 | tf_op jit(solution)/shard_map/ppermute | solution.py:407
  16.0 3.1 %collective-permute-start.5 = (f32[2,8,512]{2,1,0:T(8,128)S(1)}, f32[2,8,512]{2,1,0:T(8,128)S(1)}, u32[]{:S(2)}, u32[]{:S(2)}) collective-permute-start(f32[2,8,512]{2,1,0:T(8,128)S(1)} %get-tuple-element.44), channel_id=1, source_target_pairs={{0,16},{8,24},{16,0},{24,8},{32,48},{40,56},{48,32},{56,40},{64,80... | collective-permute-start | bytes 98312 | tf_op jit(solution)/shard_map/ppermute | solution.py:407
  19.1 0.0 collective-permute-start.6
  19.1 1.6 %local.1 = (f32[16,8,2048]{2,1,0:T(8,128)S(1)}, f32[2,16,2048]{2,1,0:T(8,128)S(1)}) custom-call(f32[16,8,2048]{2,1,0:T(8,128)S(1)} %get-tuple-element.38.f_ref, bf16[2,256,256]{2,1,0:T(8,128)(2,1)S(1)} %get-tuple-element.36.wx_ref, bf16[160,256]{1,0:T(8,128)(2,1)S(1)} %get-tuple-element.39.mf_ref, bf16[160,128]{1,0:T(8,128)(2,1)S(1)} %get-tuple-element.40.ml_ref), custom_call_target="tpu_custom_call" | custom-call | flops 2000000000 | bytes 8000000 | tf_op jit(solution)/shard_map/local/pallas_call | solution.py:448
  20.7 0.0 copy-start.4
  20.7 0.1 collective-permute-start.7
  20.8 0.0 collective-permute-done.4.b_ref
  20.8 0.0 collective-permute-done.5.c_ref
  20.8 2.2 %collective-permute-done.6.d_ref = f32[2,8,512]{2,1,0:T(8,128)S(1)} collective-permute-done((f32[2,8,512]{2,1,0:T(8,128)S(1)}, f32[2,8,512]{2,1,0:T(8,128)S(1)}, u32[]{:S(2)}, u32[]{:S(2)}) %collective-permute-start.6) | collective-permute-done | bytes 32800 | tf_op jit(solution)/shard_map/ppermute | solution.py:407
  23.1 0.7 %group.1 = f32[8,8,512]{2,1,0:T(8,128)} custom-call(f32[2,8,512]{2,1,0:T(8,128)S(1)} %get-tuple-element.42.a_ref, f32[2,8,512]{2,1,0:T(8,128)S(1)} %collective-permute-done.4.b_ref, f32[2,8,512]{2,1,0:T(8,128)S(1)} %collective-permute-done.5.c_ref, f32[2,8,512]{2,1,0:T(8,128)S(1)} %collective-permute-done.6.d_ref, f32[128,128]{1,0:T(8,128)S(1)} %get-tuple-element.37.tv_ref), custom_call_target="tpu_custom_call" | custom-call | tf_op jit(solution)/shard_map/group/pallas_call | solution.py:464
  23.7 8.3 %all-to-all-start = ((f32[8,8,512]{2,1,0:T(8,128)}), f32[8,8,512]{2,1,0:T(8,128)S(1)}, u32[]{:S(2)}, u32[]{:S(2)}) async-start(f32[8,8,512]{2,1,0:T(8,128)} %group.1), calls=%async_computation | async-start | bytes 262144 | tf_op jit(solution)/shard_map/all_to_all | solution.py:465
  32.0 0.0 collective-permute-done.7.x_ref
  32.0 7.8 %all-to-all-done.r_ref = f32[8,8,512]{2,1,0:T(8,128)S(1)} async-done(((f32[8,8,512]{2,1,0:T(8,128)}), f32[8,8,512]{2,1,0:T(8,128)S(1)}, u32[]{:S(2)}, u32[]{:S(2)}) %all-to-all-start) | async-done | bytes 131104 | tf_op jit(solution)/shard_map/all_to_all | solution.py:465
  39.8 0.1 spread.1
  39.9 3.0 %collective-permute-start.11 = (f32[2,16,2048]{2,1,0:T(8,128)S(1)}, f32[2,16,2048]{2,1,0:T(8,128)S(1)}, u32[]{:S(2)}, u32[]{:S(2)}) collective-permute-start(f32[2,16,2048]{2,1,0:T(8,128)S(1)} %get-tuple-element.51.tot_ref), channel_id=1, source_target_pairs={{0,2},{1,3},{2,0},{3,1},{4,6},{5,7},{6,4},{7,5},{8,10},{9,11},{10,... | collective-permute-start | bytes 786440 | tf_op jit(solution)/shard_map/ppermute | solution.py:407
  42.9 0.0 collective-permute-start.8
  42.9 2.2 %collective-permute-start.9 = (f32[2,8,512]{2,1,0:T(8,128)S(1)}, f32[2,8,512]{2,1,0:T(8,128)S(1)}, u32[]{:S(2)}, u32[]{:S(2)}) collective-permute-start(f32[2,8,512]{2,1,0:T(8,128)S(1)} %get-tuple-element.49), channel_id=1, source_target_pairs={{0,16},{8,24},{16,0},{24,8},{32,48},{40,56},{48,32},{56,40},{64,80... | collective-permute-start | bytes 98312 | tf_op jit(solution)/shard_map/ppermute | solution.py:407
  45.1 1.6 %collective-permute-start.10 = (f32[2,8,512]{2,1,0:T(8,128)S(1)}, f32[2,8,512]{2,1,0:T(8,128)S(1)}, u32[]{:S(2)}, u32[]{:S(2)}) collective-permute-start(f32[2,8,512]{2,1,0:T(8,128)S(1)} %get-tuple-element.50), channel_id=1, source_target_pairs={{0,24},{8,16},{16,8},{24,0},{32,56},{40,48},{48,40},{56,32},{64,88... | collective-permute-start | bytes 98312 | tf_op jit(solution)/shard_map/ppermute | solution.py:407
  46.7 0.0 collective-permute-done.8.p1_ref
  46.7 0.4 collective-permute-done.9.p2_ref
  47.2 1.9 %collective-permute-done.10.p3_ref = f32[2,8,512]{2,1,0:T(8,128)S(1)} collective-permute-done((f32[2,8,512]{2,1,0:T(8,128)S(1)}, f32[2,8,512]{2,1,0:T(8,128)S(1)}, u32[]{:S(2)}, u32[]{:S(2)}) %collective-permute-start.10) | collective-permute-done | bytes 32800 | tf_op jit(solution)/shard_map/ppermute | solution.py:407
  49.1 0.0 collective-permute-done.11.x_ref
  49.1 0.0 copy-done.4
  49.1 0.4 mixed.1
  49.5 1.8 %collective-permute-start.12 = (f32[16,2048]{1,0:T(8,128)S(1)}, f32[16,2048]{1,0:T(8,128)S(1)}, u32[]{:S(2)}, u32[]{:S(2)}) collective-permute-start(f32[16,2048]{1,0:T(8,128)S(1)} %get-tuple-element.55), channel_id=1, source_target_pairs={{0,4},{1,5},{2,6},{3,7},{4,0},{5,1},{6,2},{7,3},{8,12},{9,13},{10,... | collective-permute-start | bytes 393224 | tf_op jit(solution)/shard_map/ppermute | solution.py:407
  51.3 13.9 %all_to_all.10 = f32[8,32,128]{2,1,0:T(8,128)S(1)} all-to-all(f32[8,32,128]{2,1,0:T(8,128)S(1)} %bitcast.3), channel_id=1, replica_groups=mesh['gy'=32,'gz'=8] {'gz'}, dimensions={0} | all-to-all | bytes 262144 | tf_op jit(solution)/shard_map/all_to_all | solution.py:481
  65.1 0.0 collective-permute-done.12.x_ref
  65.1 1.2 %final.1 = f32[16,8,2048]{2,1,0:T(8,128)} custom-call(f32[16,8,2048]{2,1,0:T(8,128)S(1)} %get-tuple-element.41.loc_ref, f32[2,8,2048]{2,1,0:T(8,128)S(1)} %get-tuple-element.53.dz_ref, f32[2,16,2048]{2,1,0:T(8,128)S(1)} %get-tuple-element.54.pre_ref, f32[16,2048]{1,0:T(8,128)S(1)} %collective-permute-done.12.x_ref, f32[256,128]{1,0:T(8,128)S(1)} %bitcast.2, ...), custom_call_target="tpu_custom_call" | custom-call | tf_op jit(solution)/shard_map/final/pallas_call | solution.py:482
Async XLA Ops:
  0.0 1.2 %copy-start.2 = (f32[16,8,2048]{2,1,0:T(8,128)S(1)}, f32[16,8,2048]{2,1,0:T(8,128)}, u32[]{:S(2)}) copy-start(f32[16,8,2048]{2,1,0:T(8,128)} %t_ref.3) | copy-start | bytes 3145732
  1.2 6.9 %copy-start.3 = (f32[16,8,2048]{2,1,0:T(8,128)S(1)}, f32[16,8,2048]{2,1,0:T(8,128)}, u32[]{:S(2)}) copy-start(f32[16,8,2048]{2,1,0:T(8,128)} %t_ref.3) | copy-start | bytes 3145732
  1.3 10.1 %collective-permute-start.2 = (f32[16,2048]{1,0:T(8,128)S(1)}, f32[16,2048]{1,0:T(8,128)S(1)}, u32[]{:S(2)}, u32[]{:S(2)}) collective-permute-start(f32[16,2048]{1,0:T(8,128)S(1)} %get-tuple-element.34), channel_id=1, source_target_pairs={{0,1},{1,0},{2,3},{3,2},{4,5},{5,4},{6,7},{7,6},{8,9},{9,8},{10,11... | collective-permute-start | bytes 393224 | tf_op jit(solution)/shard_map/ppermute | solution.py:421
  4.6 6.8 %collective-permute-start.3 = (f32[16,2048]{1,0:T(8,128)S(1)}, f32[16,2048]{1,0:T(8,128)S(1)}, u32[]{:S(2)}, u32[]{:S(2)}) collective-permute-start(f32[16,2048]{1,0:T(8,128)S(1)} %get-tuple-element.35), channel_id=1, source_target_pairs={{1,2},{2,1},{3,4},{4,3},{5,6},{6,5},{9,10},{10,9},{11,12},{12,11},... | collective-permute-start | bytes 393224 | tf_op jit(solution)/shard_map/ppermute | solution.py:422
  6.6 4.8 %collective-permute-start = (f32[8,2048]{1,0:T(8,128)S(1)}, f32[8,2048]{1,0:T(8,128)S(1)}, u32[]{:S(2)}, u32[]{:S(2)}) collective-permute-start(f32[8,2048]{1,0:T(8,128)S(1)} %get-tuple-element.32), channel_id=1, source_target_pairs={{0,8},{8,0},{16,24},{24,16},{32,40},{40,32},{48,56},{56,48},{64,72... | collective-permute-start | bytes 196616 | tf_op jit(solution)/shard_map/ppermute | solution.py:419
  7.5 4.0 %collective-permute-start.1 = (f32[8,2048]{1,0:T(8,128)S(1)}, f32[8,2048]{1,0:T(8,128)S(1)}, u32[]{:S(2)}, u32[]{:S(2)}) collective-permute-start(f32[8,2048]{1,0:T(8,128)S(1)} %get-tuple-element.33), channel_id=1, source_target_pairs={{8,16},{16,8},{24,32},{32,24},{40,48},{48,40},{56,64},{64,56},{72,... | collective-permute-start | bytes 196616 | tf_op jit(solution)/shard_map/ppermute | solution.py:420
  8.1 1.4 %copy-start = (bf16[3,16,8,2048]{3,2,1,0:T(8,128)(2,1)S(1)}, bf16[3,16,8,2048]{3,2,1,0:T(8,128)(2,1)}, u32[]{:S(2)}) copy-start(bf16[3,16,8,2048]{3,2,1,0:T(8,128)(2,1)} %v_ref.3) | copy-start | bytes 4718596
  9.5 0.7 %copy-start.5 = (f32[32,128]{1,0:T(8,128)S(1)}, f32[32,128]{1,0:T(8,128)}, u32[]{:S(2)}) copy-start(f32[32,128]{1,0:T(8,128)} %constant.4.clone.scal_ref) | copy-start | bytes 49156
  10.3 1.4 %copy-start.1 = (bf16[3,16,8,2048]{3,2,1,0:T(8,128)(2,1)S(1)}, bf16[3,16,8,2048]{3,2,1,0:T(8,128)(2,1)}, u32[]{:S(2)}) copy-start(bf16[3,16,8,2048]{3,2,1,0:T(8,128)(2,1)} %v_ref.3) | copy-start | bytes 4718596
  12.5 8.3 %collective-permute-start.4 = (f32[2,8,512]{2,1,0:T(8,128)S(1)}, f32[2,8,512]{2,1,0:T(8,128)S(1)}, u32[]{:S(2)}, u32[]{:S(2)}) collective-permute-start(f32[2,8,512]{2,1,0:T(8,128)S(1)} %get-tuple-element.43), channel_id=1, source_target_pairs={{0,8},{8,0},{16,24},{24,16},{32,40},{40,32},{48,56},{56,48},{64,72... | collective-permute-start | bytes 98312 | tf_op jit(solution)/shard_map/ppermute | solution.py:407
  16.0 4.8 %collective-permute-start.5 = (f32[2,8,512]{2,1,0:T(8,128)S(1)}, f32[2,8,512]{2,1,0:T(8,128)S(1)}, u32[]{:S(2)}, u32[]{:S(2)}) collective-permute-start(f32[2,8,512]{2,1,0:T(8,128)S(1)} %get-tuple-element.44), channel_id=1, source_target_pairs={{0,16},{8,24},{16,0},{24,8},{32,48},{40,56},{48,32},{56,40},{64,80... | collective-permute-start | bytes 98312 | tf_op jit(solution)/shard_map/ppermute | solution.py:407
  19.1 4.0 %collective-permute-start.6 = (f32[2,8,512]{2,1,0:T(8,128)S(1)}, f32[2,8,512]{2,1,0:T(8,128)S(1)}, u32[]{:S(2)}, u32[]{:S(2)}) collective-permute-start(f32[2,8,512]{2,1,0:T(8,128)S(1)} %get-tuple-element.45), channel_id=1, source_target_pairs={{0,24},{8,16},{16,8},{24,0},{32,56},{40,48},{48,40},{56,32},{64,88... | collective-permute-start | bytes 98312 | tf_op jit(solution)/shard_map/ppermute | solution.py:407
  20.7 28.4 %copy-start.4 = (f32[40,16,128]{2,1,0:T(8,128)S(1)}, f32[40,16,128]{2,1,0:T(8,128)}, u32[]{:S(2)}) copy-start(f32[40,16,128]{2,1,0:T(8,128)} %constant.5.clone.sums_hbm) | copy-start | bytes 983044
  20.7 11.3 %collective-permute-start.7 = (f32[2,16,2048]{2,1,0:T(8,128)S(1)}, f32[2,16,2048]{2,1,0:T(8,128)S(1)}, u32[]{:S(2)}, u32[]{:S(2)}) collective-permute-start(f32[2,16,2048]{2,1,0:T(8,128)S(1)} %get-tuple-element.46.cs_ref), channel_id=1, source_target_pairs={{0,1},{1,0},{2,3},{3,2},{4,5},{5,4},{6,7},{7,6},{8,9},{9,8},{10,11... | collective-permute-start | bytes 786440 | tf_op jit(solution)/shard_map/ppermute | solution.py:407
  23.7 16.1 %all-to-all-start = ((f32[8,8,512]{2,1,0:T(8,128)}), f32[8,8,512]{2,1,0:T(8,128)S(1)}, u32[]{:S(2)}, u32[]{:S(2)}) async-start(f32[8,8,512]{2,1,0:T(8,128)} %group.1), calls=%async_computation | async-start | bytes 262144 | tf_op jit(solution)/shard_map/all_to_all | solution.py:465
  39.9 9.1 %collective-permute-start.11 = (f32[2,16,2048]{2,1,0:T(8,128)S(1)}, f32[2,16,2048]{2,1,0:T(8,128)S(1)}, u32[]{:S(2)}, u32[]{:S(2)}) collective-permute-start(f32[2,16,2048]{2,1,0:T(8,128)S(1)} %get-tuple-element.51.tot_ref), channel_id=1, source_target_pairs={{0,2},{1,3},{2,0},{3,1},{4,6},{5,7},{6,4},{7,5},{8,10},{9,11},{10,... | collective-permute-start | bytes 786440 | tf_op jit(solution)/shard_map/ppermute | solution.py:407
  42.9 3.9 %collective-permute-start.8 = (f32[2,8,512]{2,1,0:T(8,128)S(1)}, f32[2,8,512]{2,1,0:T(8,128)S(1)}, u32[]{:S(2)}, u32[]{:S(2)}) collective-permute-start(f32[2,8,512]{2,1,0:T(8,128)S(1)} %get-tuple-element.48), channel_id=1, source_target_pairs={{0,8},{8,0},{16,24},{24,16},{32,40},{40,32},{48,56},{56,48},{64,72... | collective-permute-start | bytes 98312 | tf_op jit(solution)/shard_map/ppermute | solution.py:407
  42.9 4.3 %collective-permute-start.9 = (f32[2,8,512]{2,1,0:T(8,128)S(1)}, f32[2,8,512]{2,1,0:T(8,128)S(1)}, u32[]{:S(2)}, u32[]{:S(2)}) collective-permute-start(f32[2,8,512]{2,1,0:T(8,128)S(1)} %get-tuple-element.49), channel_id=1, source_target_pairs={{0,16},{8,24},{16,0},{24,8},{32,48},{40,56},{48,32},{56,40},{64,80... | collective-permute-start | bytes 98312 | tf_op jit(solution)/shard_map/ppermute | solution.py:407
  45.1 4.0 %collective-permute-start.10 = (f32[2,8,512]{2,1,0:T(8,128)S(1)}, f32[2,8,512]{2,1,0:T(8,128)S(1)}, u32[]{:S(2)}, u32[]{:S(2)}) collective-permute-start(f32[2,8,512]{2,1,0:T(8,128)S(1)} %get-tuple-element.50), channel_id=1, source_target_pairs={{0,24},{8,16},{16,8},{24,0},{32,56},{40,48},{48,40},{56,32},{64,88... | collective-permute-start | bytes 98312 | tf_op jit(solution)/shard_map/ppermute | solution.py:407
  49.5 15.7 %collective-permute-start.12 = (f32[16,2048]{1,0:T(8,128)S(1)}, f32[16,2048]{1,0:T(8,128)S(1)}, u32[]{:S(2)}, u32[]{:S(2)}) collective-permute-start(f32[16,2048]{1,0:T(8,128)S(1)} %get-tuple-element.55), channel_id=1, source_target_pairs={{0,4},{1,5},{2,6},{3,7},{4,0},{5,1},{6,2},{7,3},{8,12},{9,13},{10,... | collective-permute-start | bytes 393224 | tf_op jit(solution)/shard_map/ppermute | solution.py:407

commit v4 on v3

--- a/solution.py
+++ b/solution.py
@@ -267,10 +267,22 @@
             o_ref[p, :, cols] = tv_ref[72 + p : 73 + p, :] * jnp.where(p > z, tot[0], tot[1])
 
 
-def spread_kernel(a_ref, b_ref, c_ref, d_ref, r_ref, tv_ref, cs_ref, x_ref,
-                  own_ref, s1_ref, s2_ref, s3_ref, tot_ref, pre_ref):
-    d, e = lax.axis_index("gy"), lax.axis_index("gz")
-    z = d // GX
+def weights(sums_ref, first):
+    tm = sums_ref[DY + lax.axis_index("gz")]
+    return [jnp.broadcast_to(tm[first : first + 8, w : w + 1], (8, 128)) for w in range(8)]
+
+
+def weighted(rows, p):
+    total = rows[0] * p[0:1]
+    for w in range(1, 8):
+        total += rows[w] * p[w : w + 1]
+    return total
+
+
+def spread_kernel(a_ref, b_ref, c_ref, d_ref, r_ref, tv_ref, sums_ref, own_ref, s1_ref, s2_ref, s3_ref, o_ref):
+    d = lax.axis_index("gy")
+    z, x = d // GX, lax.rem(d, GX)
+    out = weights(sums_ref, 8)
     parts = (a_ref, b_ref, c_ref, d_ref)
     outs = (own_ref, s1_ref, s2_ref, s3_ref)
     for t in range(Q // 128):
@@ -291,7 +303,11 @@
                         row = 80 + 16 * k + 4 * i + j
                         total += tv_ref[row : row + 1, :] * vals[j]
                 outs[i][k, :, cols] = total
-    upper = (e % 2) == 1
+                o_ref[lax.bitwise_xor(x, i), pl.ds(k * 4 + t, 8, stride=8), :] = weighted(out, total)
+
+
+def pair_kernel(cs_ref, x_ref, tot_ref, pre_ref):
+    upper = (lax.axis_index("gz") % 2) == 1
     near, far = jnp.where(upper, 1.0, STEP_Z), jnp.where(upper, STEP_Z, 1.0)
     tot_ref[0] = near * cs_ref[0] + far * x_ref[0]
     tot_ref[1] = far * cs_ref[1] + near * x_ref[1]
@@ -299,14 +315,8 @@
     pre_ref[1] = jnp.where(upper, 0.0, x_ref[1])
 
 
-def mixed_kernel(p0_ref, p1_ref, p2_ref, p3_ref, tot_ref, x_ref, pre_ref, sums_hbm,
-                 dz_ref, s_ref, send_ref, pre2_ref, p4, tm_ref, sem):
+def quad_kernel(tot_ref, x_ref, pre_ref, send_ref, pre2_ref):
     e = lax.axis_index("gz")
-    load = pltpu.make_async_copy(sums_hbm.at[DY + e], tm_ref, sem)
-    load.start()
-    x = lax.rem(lax.axis_index("gy"), GX)
-    for i, ref in enumerate((p0_ref, p1_ref, p2_ref, p3_ref)):
-        p4[lax.bitwise_xor(x, i)] = ref[...]
     upper = ((e // 2) % 2) == 1
     odd = (e % 2) == 1
     two = STEP_Z * STEP_Z
@@ -317,59 +327,63 @@
     high = jnp.where(odd, 1.0, STEP_Z)
     pre2_ref[0] = pre_ref[0] + jnp.where(upper, low * x_ref[0], 0.0)
     pre2_ref[1] = pre_ref[1] + jnp.where(upper, 0.0, high * x_ref[1])
-    load.wait()
-    tm = tm_ref[...]
-    own = [jnp.broadcast_to(tm[:8, w : w + 1], (8, 128)) for w in range(8)]
-    out = [jnp.broadcast_to(tm[8:, w : w + 1], (8, 128)) for w in range(8)]
+
+
+def own_kernel(p0_ref, p1_ref, p2_ref, p3_ref, sums_ref, dz_ref, p4):
+    x = lax.rem(lax.axis_index("gy"), GX)
+    for i, ref in enumerate((p0_ref, p1_ref, p2_ref, p3_ref)):
+        p4[lax.bitwise_xor(x, i)] = ref[...]
+    own = weights(sums_ref, 0)
     for k in range(2):
         for t in range(16):
             p = p4[t // 4, k, :, (t % 4) * 128 : (t % 4 + 1) * 128]
-            one = own[0] * p[0:1]
-            two = out[0] * p[0:1]
-            for w in range(1, 8):
-                one += own[w] * p[w : w + 1]
-                two += out[w] * p[w : w + 1]
-            dz_ref[k, :, t * 128 : (t + 1) * 128] = one
-            s_ref[pl.ds(k * 16 + t, 8, stride=32), :] = two
-
-
-def final_kernel(loc_ref, dz_ref, pre_ref, x_ref, r_ref, sums_hbm, tv_ref, o_hbm,
-                 cl, ch, o_ref, tg_ref, tm_ref, sems):
+            dz_ref[k, :, t * 128 : (t + 1) * 128] = weighted(own, p)
+
+
+def near_kernel(loc_ref, dz_ref, tv_ref, o_ref):
+    for l in range(LY):
+        for t in range(NX // 128):
+            cols = slice(t * 128, (t + 1) * 128)
+            o_ref[l, :, cols] = (loc_ref[l, :, cols] + tv_ref[l : l + 1, :] * dz_ref[0, :, cols]
+                                 + tv_ref[16 + l : 17 + l, :] * dz_ref[1, :, cols])
+
+
+def final_kernel(near_ref, pre_ref, x_ref, r_ref, sums_ref, o_hbm, cl, ch, o_ref, sems):
     d, e = lax.axis_index("gy"), lax.axis_index("gz")
-    loads = start((sums_hbm.at[d], tg_ref, sems.at[0]), (sums_hbm.at[DY + e], tm_ref, sems.at[1]))
-    lo = jnp.zeros((32, 128), F32)
-    hi = jnp.zeros((32, 128), F32)
-    for p in range(DZ):
-        part = r_ref[p * 32 : (p + 1) * 32, :]
-        lo += jnp.where(p < e, part, 0.0)
-        hi += jnp.where(p > e, part, 0.0)
+    low_rows, high_rows = [], []
+    for q in range(GX):
+        lo = jnp.zeros((8, 128), F32)
+        hi = jnp.zeros((8, 128), F32)
+        for p in range(DZ):
+            part = r_ref[q * DZ + p]
+            lo += jnp.where(p < e, part, 0.0)
+            hi += jnp.where(p > e, part, 0.0)
+        low_rows.append(lo)
+        high_rows.append(hi)
     top = (e // 4) == 1
     at = lax.rem(e, 4)
     power = lambda k: jnp.where(k == 0, 1.0, jnp.where(k == 1, STEP_Z, jnp.where(k == 2, STEP_Z**2, STEP_Z**3)))
     up = jnp.where(top, power(at), 0.0)
     down = jnp.where(top, 0.0, power(3 - at))
-    for load in loads:
-        load.wait()
-    tg, tm = tg_ref[...], tm_ref[...]
+    tg, tm = sums_ref[d], sums_ref[DY + e]
     ga = jnp.broadcast_to(tg[:, 0:1], (16, 128))
     gb = jnp.broadcast_to(tg[:, 1:2], (16, 128))
     for t in range(NX // 128):
         cols = slice(t * 128, (t + 1) * 128)
-        cl[:, cols] = (pre_ref[0, :, cols] + up * x_ref[:, cols]) + (ga * lo[t : t + 1] + gb * lo[16 + t : 17 + t])
-        ch[:, cols] = (pre_ref[1, :, cols] + down * x_ref[:, cols]) + (ga * hi[t : t + 1] + gb * hi[16 + t : 17 + t])
+        q, i = t // 4, t % 4
+        lo, hi = low_rows[q], high_rows[q]
+        cl[:, cols] = (pre_ref[0, :, cols] + up * x_ref[:, cols]) + (ga * lo[i : i + 1] + gb * lo[4 + i : 5 + i])
+        ch[:, cols] = (pre_ref[1, :, cols] + down * x_ref[:, cols]) + (ga * hi[i : i + 1] + gb * hi[4 + i : 5 + i])
     hl = jnp.broadcast_to(tm[:8, 8:9], (8, 128))
     hh = jnp.broadcast_to(tm[:8, 9:10], (8, 128))
     stores = []
     for l in range(LY):
         for t in range(NX // 128):
             cols = slice(t * 128, (t + 1) * 128)
-            o_ref[l, :, cols] = (
-                loc_ref[l, :, cols] + tv_ref[l : l + 1, :] * dz_ref[0, :, cols]
-                + tv_ref[16 + l : 17 + l, :] * dz_ref[1, :, cols]
-                + (hl * cl[l : l + 1, cols] + hh * ch[l : l + 1, cols]))
+            o_ref[l, :, cols] = near_ref[l, :, cols] + (hl * cl[l : l + 1, cols] + hh * ch[l : l + 1, cols])
         if l % 4 == 3:
             i = l // 4
-            stores += start((o_ref.at[pl.ds(l - 3, 4)], o_hbm.at[pl.ds(l - 3, 4)], sems.at[2 + i]))
+            stores += start((o_ref.at[pl.ds(l - 3, 4)], o_hbm.at[pl.ds(l - 3, 4)], sems.at[i]))
     for store in stores:
         store.wait()
 
@@ -407,6 +421,9 @@
     return lax.ppermute(value, axis, [(i, i ^ bit) for i in range(count)])
 
 
+tie = lambda *values: lax.optimization_barrier(values)
+SMALL = (10**5, 5 * 10**5)
+LAYER = [[(z * GX + x) * DZ + e for x in range(GX) for e in range(DZ)] for z in range(GZ)]
 COLUMN = [[z * GX + x for z in range(GZ)] for x in range(GX)]
 
 
@@ -460,41 +477,34 @@
         "local",
         (2 * 10**9, 8 * 10**6),
     )(f, wx, mf, ml)
+    c, sets[1] = tie(c, sets[1])
     x1 = across(c, "gz", DZ, 1)
-    tots = call(group_kernel, [(GZ, LZ, Q)], [VMEM] * 5, [VMEM], [], 4, "group")(*sets, tv)[0]
+    tots = call(group_kernel, [(GZ, LZ, Q)], [VMEM] * 5, [VMEM], [], 4, "group", SMALL)(*sets, tv)[0]
     r1 = lax.all_to_all(tots, "gy", 0, 0, axis_index_groups=COLUMN)
-    *mine, tot, pre = call(
-        spread_kernel, [QUARTER] * 4 + [SUMS_Z] * 2, [VMEM] * 8, [VMEM] * 6, [], 8, "spread"
-    )(*sets, r1, tv, c, x1)
+    tot, pre = call(pair_kernel, [SUMS_Z] * 2, [VMEM] * 2, [VMEM] * 2, [], 4, "pair", SMALL)(c, x1)
+    x2 = across(tot, "gz", DZ, 2)
+    r1, tot, pre = tie(r1, tot, pre)
+    *mine, s = call(
+        spread_kernel, [QUARTER] * 4 + [(GX, 64, 128)], [VMEM] * 7, [VMEM] * 5, [], 4, "spread", SMALL
+    )(*sets, r1, tv, SUMS)
+    r3 = lax.all_to_all(s.reshape(GX * DZ, 8, 128), ("gy", "gz"), 0, 0, axis_index_groups=LAYER)
     sets = [mine[0]] + [across(mine[i], "gy", DY, i) for i in (1, 2, 3)]
-    x2 = across(tot, "gz", DZ, 2)
-    dz, s, send, pre = call(
-        mixed_kernel,
-        [(2, LZ, NX), (256, 128), (LY, NX), SUMS_Z],
-        [VMEM] * 7 + [HBM],
-        [VMEM] * 4,
-        [pltpu.VMEM((GX, 2, LZ, Q), F32), pltpu.VMEM((16, 128), F32), dma],
-        8,
-        "mixed",
-    )(*sets, tot, x2, pre, SUMS)
+    x2, sets[0] = tie(x2, sets[0])
+    send, pre = call(quad_kernel, [(LY, NX), SUMS_Z], [VMEM] * 3, [VMEM] * 2, [], 4, "quad", SMALL)(tot, x2, pre)
     x3 = across(send, "gz", DZ, 4)
-    r3 = lax.all_to_all(s.reshape(DZ, 32, 128), "gz", 0, 0)
+    dz = call(
+        own_kernel, [(2, LZ, NX)], [VMEM] * 5, [VMEM], [pltpu.VMEM((GX, 2, LZ, Q), F32)], 8, "own", SMALL
+    )(*sets, SUMS)[0]
+    near = call(near_kernel, [FULL], [VMEM] * 3, [VMEM], [], 8, "near", (10**6, 2 * 10**6))(loc, dz, tv)[0]
     return call(
         final_kernel,
         [FULL],
-        [VMEM] * 5 + [HBM, VMEM],
+        [VMEM] * 5,
         [HBM],
-        [
-            pltpu.VMEM((LY, NX), F32),
-            pltpu.VMEM((LY, NX), F32),
-            pltpu.VMEM(FULL, F32),
-            pltpu.VMEM((16, 128), F32),
-            pltpu.VMEM((16, 128), F32),
-            dma((6,)),
-        ],
+        [pltpu.VMEM((LY, NX), F32), pltpu.VMEM((LY, NX), F32), pltpu.VMEM(FULL, F32), dma((4,))],
         16,
         "final",
-    )(loc, dz, pre, x3, r3.reshape(256, 128), SUMS, tv)[0]
+    )(near, pre, x3, r3, SUMS)[0]
 
 
 def solution(mesh):

time: 66.7 us -> 63.5 us (0.952)
  waiting for transfers between devices: 12.4 us -> 4.74 us
  blocking collectives: 13.9 us -> 16.5 us
  starting transfers between devices: 30.3 us -> 31.6 us
    all_to_all x1, waiting for transfers between devices: 7.8 us -> 0.01 us  [on_device(): lax.all_to_all(s.reshape(GX * DZ, 8, 128), ('gy', 'gz'), 0, 0, axis_index...]
    ppermute x9, starting transfers between devices: 15.3 us -> 17.9 us  [across(): return lax.ppermute(value, axis, [(i, i ^ bit) for i in range(count)])]
    all_to_all x1, blocking collectives: 13.9 us -> 16.5 us  [on_device(): r1 = lax.all_to_all(tots, 'gy', 0, 0, axis_index_groups=COLUMN)]
    all_to_all x1, starting transfers between devices: 8.26 us -> 6.9 us  [on_device(): lax.all_to_all(s.reshape(GX * DZ, 8, 128), ('gy', 'gz'), 0, 0, axis_index...]
    pallas_call x4 -> x7, Pallas kernels: 2.36 us -> 2.46 us  [the longest x1 1.16 us: on_device(): call(final_kernel, [FULL], [VMEM] * 5, [HBM], [pltpu.VMEM((LY, NX), F32),...]
  transfers between devices with their start and end apart: 14 -> 14, of which waited for: 4 -> 4; matrix products, arithmetic and copies ran while one was open for 0% -> 0% of each run, Pallas kernels for 5% -> 6%
where the time goes in v4:
time: 63.5 us; the launch traced here: 62.7 us
  starting transfers between devices  31.6 us (50%)
  blocking collectives  16.5 us (26%)
  Pallas kernels  6.13 us (10%)
  waiting for transfers between devices  4.74 us (7%)
  local copies, waits for them, and re-layouts  3.58 us (6%)
    ppermute x9, starting transfers between devices, across(): return lax.ppermute(value, axis, [(i, i ^ bit) for i in range(count)])  17.9 us
    all_to_all x1, blocking collectives, on_device(): r1 = lax.all_to_all(tots, 'gy', 0, 0, axis_index_groups=COLUMN)  16.5 us
    all_to_all x1, starting transfers between devices, on_device(): lax.all_to_all(s.reshape(GX * DZ, 8, 128), ('gy', 'gz'), 0, 0, axis_index...  6.9 us
    ppermute x9, waiting for transfers between devices, across(): return lax.ppermute(value, axis, [(i, i ^ bit) for i in range(count)])  4.73 us
    unnamed x12, local copies, waits for them, and re-layouts  3.58 us
    ppermute x1, starting transfers between devices, on_device(): z1 = lax.ppermute(z1, 'gz', pairs(DZ, False))  3.33 us
    ppermute x1, starting transfers between devices, on_device(): z2 = lax.ppermute(z2, 'gz', pairs(DZ, True))  1.91 us
    pallas_call x1, Pallas kernels, on_device(): call(local_kernel, [FULL, SUMS_Z], [VMEM] * 4, [VMEM] * 2, [pltpu.VMEM((N...  1.59 us
  transfers between devices with their start and end apart: 14, of which 4 were waited for; matrix products, arithmetic and copies ran while one was open for 0% of the time, Pallas kernels for 6%

profile of v4, /device:TPU:1, one launch (start us, length us, event | category | flops | bytes accessed | tf_op | source)
XLA Modules:
  0.0 62.7 jit_solution(13695784287869830032)
XLA Ops:
  0.0 0.0 copy-start.2
  0.0 1.2 %copy-done.2 = f32[16,8,2048]{2,1,0:T(8,128)S(1)} copy-done((f32[16,8,2048]{2,1,0:T(8,128)S(1)}, f32[16,8,2048]{2,1,0:T(8,128)}, u32[]{:S(2)}) %copy-start.2) | copy-done | bytes 1048600
  1.2 0.0 copy-start.3
  1.2 0.1 faces.1
  1.3 3.3 %collective-permute-start.2 = (f32[16,2048]{1,0:T(8,128)S(1)}, f32[16,2048]{1,0:T(8,128)S(1)}, u32[]{:S(2)}, u32[]{:S(2)}) collective-permute-start(f32[16,2048]{1,0:T(8,128)S(1)} %get-tuple-element.40), channel_id=1, source_target_pairs={{0,1},{1,0},{2,3},{3,2},{4,5},{5,4},{6,7},{7,6},{8,9},{9,8},{10,11... | collective-permute-start | bytes 393224 | tf_op jit(solution)/shard_map/ppermute | solution.py:438
  4.6 1.9 %collective-permute-start.3 = (f32[16,2048]{1,0:T(8,128)S(1)}, f32[16,2048]{1,0:T(8,128)S(1)}, u32[]{:S(2)}, u32[]{:S(2)}) collective-permute-start(f32[16,2048]{1,0:T(8,128)S(1)} %get-tuple-element.41), channel_id=1, source_target_pairs={{1,2},{2,1},{3,4},{4,3},{5,6},{6,5},{9,10},{10,9},{11,12},{12,11},... | collective-permute-start | bytes 393224 | tf_op jit(solution)/shard_map/ppermute | solution.py:439
  6.6 0.9 %collective-permute-start = (f32[8,2048]{1,0:T(8,128)S(1)}, f32[8,2048]{1,0:T(8,128)S(1)}, u32[]{:S(2)}, u32[]{:S(2)}) collective-permute-start(f32[8,2048]{1,0:T(8,128)S(1)} %get-tuple-element.38), channel_id=1, source_target_pairs={{0,8},{8,0},{16,24},{24,16},{32,40},{40,32},{48,56},{56,48},{64,72... | collective-permute-start | bytes 196616 | tf_op jit(solution)/shard_map/ppermute | solution.py:436
  7.5 0.7 %collective-permute-start.1 = (f32[8,2048]{1,0:T(8,128)S(1)}, f32[8,2048]{1,0:T(8,128)S(1)}, u32[]{:S(2)}, u32[]{:S(2)}) collective-permute-start(f32[8,2048]{1,0:T(8,128)S(1)} %get-tuple-element.39), channel_id=1, source_target_pairs={{8,16},{16,8},{24,32},{32,24},{40,48},{48,40},{56,64},{64,56},{72,... | collective-permute-start | bytes 196616 | tf_op jit(solution)/shard_map/ppermute | solution.py:437
  8.1 0.0 copy-done.3
  8.1 0.0 copy-start
  8.1 1.4 %copy-done = bf16[3,16,8,2048]{3,2,1,0:T(8,128)(2,1)S(1)} copy-done((bf16[3,16,8,2048]{3,2,1,0:T(8,128)(2,1)S(1)}, bf16[3,16,8,2048]{3,2,1,0:T(8,128)(2,1)}, u32[]{:S(2)}) %copy-start) | copy-done | bytes 1572888
  9.5 0.0 copy-start.5
  9.5 0.7 %copy-done.5 = f32[32,128]{1,0:T(8,128)S(1)} copy-done((f32[32,128]{1,0:T(8,128)S(1)}, f32[32,128]{1,0:T(8,128)}, u32[]{:S(2)}) %copy-start.5) | copy-done | bytes 16408
  10.3 0.0 copy-start.1
  10.3 1.1 %inner.1 = (f32[16,8,2048]{2,1,0:T(8,128)S(1)}, bf16[160,256]{1,0:T(8,128)(2,1)S(1)}, bf16[160,128]{1,0:T(8,128)(2,1)S(1)}, bf16[2,256,256]{2,1,0:T(8,128)(2,1)S(1)}, f32[128,128]{1,0:T(8,128)S(1)}) custom-call(f32[16,8,2048]{2,1,0:T(8,128)S(1)} %copy-done.3, bf16[3,16,8,2048]{3,2,1,0:T(8,128)(2,1)S(1)} %copy-done, f32[32,128]{1,0:T(8,128)S(1)} %copy-done.5), custom_call_target="tpu_custom_call" | custom-call | flops 10000000 | bytes 8000000 | tf_op jit(solution)/shard_map/inner/pallas_call | solution.py:440
  11.4 0.0 collective-permute-done.y1_ref
  11.4 0.0 collective-permute-done.1.y2_ref
  11.4 0.0 collective-permute-done.2.z1_ref
  11.4 0.0 collective-permute-done.3.z2_ref
  11.4 0.2 copy-done.1
  11.7 0.9 %source.1 = (f32[16,8,2048]{2,1,0:T(8,128)S(1)}, f32[2,8,512]{2,1,0:T(8,128)S(1)}, f32[2,8,512]{2,1,0:T(8,128)S(1)}, f32[2,8,512]{2,1,0:T(8,128)S(1)}, f32[2,8,512]{2,1,0:T(8,128)S(1)}) custom-call(f32[16,8,2048]{2,1,0:T(8,128)S(1)} %get-tuple-element.37.f0_ref, bf16[3,16,8,2048]{3,2,1,0:T(8,128)(2,1)S(1)} %copy-done.1, ...), custom_call_target="tpu_custom_call" | custom-call | tf_op jit(solution)/shard_map/source/pallas_call | solution.py:450
  12.5 3.5 %collective-permute-start.4 = (f32[2,8,512]{2,1,0:T(8,128)S(1)}, f32[2,8,512]{2,1,0:T(8,128)S(1)}, u32[]{:S(2)}, u32[]{:S(2)}) collective-permute-start(f32[2,8,512]{2,1,0:T(8,128)S(1)} %get-tuple-element.49), channel_id=1, source_target_pairs={{0,8},{8,0},{16,24},{24,16},{32,40},{40,32},{48,56},{56,48},{64,72... | collective-permute-start | bytes 98312 | tf_op jit(solution)/shard_map/ppermute | solution.py:421
  16.0 0.0 copy-start.4
  16.0 1.6 %local.1 = (f32[16,8,2048]{2,1,0:T(8,128)S(1)}, f32[2,16,2048]{2,1,0:T(8,128)S(1)}) custom-call(f32[16,8,2048]{2,1,0:T(8,128)S(1)} %get-tuple-element.44.f_ref, bf16[2,256,256]{2,1,0:T(8,128)(2,1)S(1)} %get-tuple-element.42.wx_ref, bf16[160,256]{1,0:T(8,128)(2,1)S(1)} %get-tuple-element.45.mf_ref, bf16[160,128]{1,0:T(8,128)(2,1)S(1)} %get-tuple-element.46.ml_ref), custom_call_target="tpu_custom_call" | custom-call | flops 2000000000 | bytes 8000000 | tf_op jit(solution)/shard_map/local/pallas_call | solution.py:465
  17.6 0.0 collective-permute-done.4.b_ref
  17.6 0.1 collective-permute-start.5
  17.7 3.2 %collective-permute-start.7 = (f32[2,8,512]{2,1,0:T(8,128)S(1)}, f32[2,8,512]{2,1,0:T(8,128)S(1)}, u32[]{:S(2)}, u32[]{:S(2)}) collective-permute-start(f32[2,8,512]{2,1,0:T(8,128)S(1)} %get-tuple-element.54), channel_id=1, source_target_pairs={{0,16},{8,24},{16,0},{24,8},{32,48},{40,56},{48,32},{56,40},{64,80... | collective-permute-start | bytes 98312 | tf_op jit(solution)/shard_map/ppermute | solution.py:421
  20.9 0.3 collective-permute-start.8
  21.2 0.0 collective-permute-done.5.x_ref
  21.2 0.1 pair.1
  21.2 2.8 %collective-permute-start.6 = (f32[2,16,2048]{2,1,0:T(8,128)S(1)}, f32[2,16,2048]{2,1,0:T(8,128)S(1)}, u32[]{:S(2)}, u32[]{:S(2)}) collective-permute-start(f32[2,16,2048]{2,1,0:T(8,128)S(1)} %get-tuple-element.63.tot_ref), channel_id=1, source_target_pairs={{0,2},{1,3},{2,0},{3,1},{4,6},{5,7},{6,4},{7,5},{8,10},{9,11},{10,... | collective-permute-start | bytes 786440 | tf_op jit(solution)/shard_map/ppermute | solution.py:421
  24.1 0.0 collective-permute-done.7.c_ref
  24.1 0.8 %collective-permute-done.8.d_ref = f32[2,8,512]{2,1,0:T(8,128)S(1)} collective-permute-done((f32[2,8,512]{2,1,0:T(8,128)S(1)}, f32[2,8,512]{2,1,0:T(8,128)S(1)}, u32[]{:S(2)}, u32[]{:S(2)}) %collective-permute-start.8) | collective-permute-done | bytes 32800 | tf_op jit(solution)/shard_map/ppermute | solution.py:421
  24.9 16.5 %all_to_all.10.r_ref = f32[8,8,512]{2,1,0:T(8,128)S(1)} all-to-all(f32[8,8,512]{2,1,0:T(8,128)S(1)} %group.1), channel_id=1, replica_groups={{0,32,64,96,128,160,192,224},{8,40,72,104,136,168,200,232},{16,48,80,11..., dimensions={0} | all-to-all | bytes 262144 | tf_op jit(solution)/shard_map/all_to_all | solution.py:483
  41.3 0.0 copy-done.4
  41.3 0.9 %spread.1 = (f32[2,8,512]{2,1,0:T(8,128)S(1)}, f32[2,8,512]{2,1,0:T(8,128)S(1)}, f32[2,8,512]{2,1,0:T(8,128)S(1)}, f32[2,8,512]{2,1,0:T(8,128)S(1)}, f32[4,64,128]{2,1,0:T(8,128)}) custom-call(f32[2,8,512]{2,1,0:T(8,128)S(1)} %get-tuple-element.52.a_ref, f32[2,8,512]{2,1,0:T(8,128)S(1)} %collective-permute-done.4.b_ref, ...), custom_call_target="tpu_custom_call" | custom-call | flops 100000 | bytes 500000 | tf_op jit(solution)/shard_map/spread/pallas_call | solution.py:487
  42.2 0.0 collective-permute-done.6.x_ref
  42.2 0.1 quad.1
  42.3 4.1 %collective-permute-start.12 = (f32[16,2048]{1,0:T(8,128)S(1)}, f32[16,2048]{1,0:T(8,128)S(1)}, u32[]{:S(2)}, u32[]{:S(2)}) collective-permute-start(f32[16,2048]{1,0:T(8,128)S(1)} %get-tuple-element.67), channel_id=1, source_target_pairs={{0,4},{1,5},{2,6},{3,7},{4,0},{5,1},{6,2},{7,3},{8,12},{9,13},{10,... | collective-permute-start | bytes 393224 | tf_op jit(solution)/shard_map/ppermute | solution.py:421
  46.4 6.9 %all-to-all-start.1 = ((f32[32,8,128]{2,1,0:T(8,128)}), f32[32,8,128]{2,1,0:T(8,128)S(1)}, u32[]{:S(2)}, u32[]{:S(2)}) async-start(f32[32,8,128]{2,1,0:T(8,128)} %bitcast), calls=%async_computation.1 | async-start | bytes 262144 | tf_op jit(solution)/shard_map/all_to_all | solution.py:490
  53.3 1.5 %collective-permute-start.9 = (f32[2,8,512]{2,1,0:T(8,128)S(1)}, f32[2,8,512]{2,1,0:T(8,128)S(1)}, u32[]{:S(2)}, u32[]{:S(2)}) collective-permute-start(f32[2,8,512]{2,1,0:T(8,128)S(1)} %get-tuple-element.60), channel_id=1, source_target_pairs={{0,8},{8,0},{16,24},{24,16},{32,40},{40,32},{48,56},{56,48},{64,72... | collective-permute-start | bytes 98312 | tf_op jit(solution)/shard_map/ppermute | solution.py:421
  54.8 2.4 %collective-permute-start.10 = (f32[2,8,512]{2,1,0:T(8,128)S(1)}, f32[2,8,512]{2,1,0:T(8,128)S(1)}, u32[]{:S(2)}, u32[]{:S(2)}) collective-permute-start(f32[2,8,512]{2,1,0:T(8,128)S(1)} %get-tuple-element.61), channel_id=1, source_target_pairs={{0,16},{8,24},{16,0},{24,8},{32,48},{40,56},{48,32},{56,40},{64,80... | collective-permute-start | bytes 98312 | tf_op jit(solution)/shard_map/ppermute | solution.py:421
  57.2 0.1 collective-permute-start.11
  57.3 0.4 collective-permute-done.9.p1_ref
  57.7 2.2 %collective-permute-done.10.p2_ref = f32[2,8,512]{2,1,0:T(8,128)S(1)} collective-permute-done((f32[2,8,512]{2,1,0:T(8,128)S(1)}, f32[2,8,512]{2,1,0:T(8,128)S(1)}, u32[]{:S(2)}, u32[]{:S(2)}) %collective-permute-start.10) | collective-permute-done | bytes 32800 | tf_op jit(solution)/shard_map/ppermute | solution.py:421
  59.9 1.3 %collective-permute-done.11.p3_ref = f32[2,8,512]{2,1,0:T(8,128)S(1)} collective-permute-done((f32[2,8,512]{2,1,0:T(8,128)S(1)}, f32[2,8,512]{2,1,0:T(8,128)S(1)}, u32[]{:S(2)}, u32[]{:S(2)}) %collective-permute-start.11) | collective-permute-done | bytes 32800 | tf_op jit(solution)/shard_map/ppermute | solution.py:421
  61.2 0.1 own.1.dz_ref
  61.4 0.1 near.1.near_ref
  61.5 0.0 all-to-all-done.1.r_ref
  61.5 0.0 collective-permute-done.12.x_ref
  61.5 1.2 %final.1 = f32[16,8,2048]{2,1,0:T(8,128)} custom-call(f32[16,8,2048]{2,1,0:T(8,128)S(1)} %near.1.near_ref, f32[2,16,2048]{2,1,0:T(8,128)S(1)} %get-tuple-element.66.pre_ref, f32[16,2048]{1,0:T(8,128)S(1)} %collective-permute-done.12.x_ref, f32[32,8,128]{2,1,0:T(8,128)S(1)} %all-to-all-done.1.r_ref, f32[40,16,128]{2,1,0:T(8,128)S(1)} %copy-done.4), custom_call_target="tpu_custom_call" | custom-call | tf_op jit(solution)/shard_map/final/pallas_call | solution.py:499
  (1 shorter events, 0.0 us)
Async XLA Ops:
  0.0 1.2 %copy-start.2 = (f32[16,8,2048]{2,1,0:T(8,128)S(1)}, f32[16,8,2048]{2,1,0:T(8,128)}, u32[]{:S(2)}) copy-start(f32[16,8,2048]{2,1,0:T(8,128)} %t_ref.3) | copy-start | bytes 3145732
  1.2 6.9 %copy-start.3 = (f32[16,8,2048]{2,1,0:T(8,128)S(1)}, f32[16,8,2048]{2,1,0:T(8,128)}, u32[]{:S(2)}) copy-start(f32[16,8,2048]{2,1,0:T(8,128)} %t_ref.3) | copy-start | bytes 3145732
  1.3 10.1 %collective-permute-start.2 = (f32[16,2048]{1,0:T(8,128)S(1)}, f32[16,2048]{1,0:T(8,128)S(1)}, u32[]{:S(2)}, u32[]{:S(2)}) collective-permute-start(f32[16,2048]{1,0:T(8,128)S(1)} %get-tuple-element.40), channel_id=1, source_target_pairs={{0,1},{1,0},{2,3},{3,2},{4,5},{5,4},{6,7},{7,6},{8,9},{9,8},{10,11... | collective-permute-start | bytes 393224 | tf_op jit(solution)/shard_map/ppermute | solution.py:438
  4.6 6.8 %collective-permute-start.3 = (f32[16,2048]{1,0:T(8,128)S(1)}, f32[16,2048]{1,0:T(8,128)S(1)}, u32[]{:S(2)}, u32[]{:S(2)}) collective-permute-start(f32[16,2048]{1,0:T(8,128)S(1)} %get-tuple-element.41), channel_id=1, source_target_pairs={{1,2},{2,1},{3,4},{4,3},{5,6},{6,5},{9,10},{10,9},{11,12},{12,11},... | collective-permute-start | bytes 393224 | tf_op jit(solution)/shard_map/ppermute | solution.py:439
  6.6 4.8 %collective-permute-start = (f32[8,2048]{1,0:T(8,128)S(1)}, f32[8,2048]{1,0:T(8,128)S(1)}, u32[]{:S(2)}, u32[]{:S(2)}) collective-permute-start(f32[8,2048]{1,0:T(8,128)S(1)} %get-tuple-element.38), channel_id=1, source_target_pairs={{0,8},{8,0},{16,24},{24,16},{32,40},{40,32},{48,56},{56,48},{64,72... | collective-permute-start | bytes 196616 | tf_op jit(solution)/shard_map/ppermute | solution.py:436
  7.5 4.0 %collective-permute-start.1 = (f32[8,2048]{1,0:T(8,128)S(1)}, f32[8,2048]{1,0:T(8,128)S(1)}, u32[]{:S(2)}, u32[]{:S(2)}) collective-permute-start(f32[8,2048]{1,0:T(8,128)S(1)} %get-tuple-element.39), channel_id=1, source_target_pairs={{8,16},{16,8},{24,32},{32,24},{40,48},{48,40},{56,64},{64,56},{72,... | collective-permute-start | bytes 196616 | tf_op jit(solution)/shard_map/ppermute | solution.py:437
  8.1 1.4 %copy-start = (bf16[3,16,8,2048]{3,2,1,0:T(8,128)(2,1)S(1)}, bf16[3,16,8,2048]{3,2,1,0:T(8,128)(2,1)}, u32[]{:S(2)}) copy-start(bf16[3,16,8,2048]{3,2,1,0:T(8,128)(2,1)} %v_ref.3) | copy-start | bytes 4718596
  9.5 0.7 %copy-start.5 = (f32[32,128]{1,0:T(8,128)S(1)}, f32[32,128]{1,0:T(8,128)}, u32[]{:S(2)}) copy-start(f32[32,128]{1,0:T(8,128)} %constant.4.clone.scal_ref) | copy-start | bytes 49156
  10.3 1.4 %copy-start.1 = (bf16[3,16,8,2048]{3,2,1,0:T(8,128)(2,1)S(1)}, bf16[3,16,8,2048]{3,2,1,0:T(8,128)(2,1)}, u32[]{:S(2)}) copy-start(bf16[3,16,8,2048]{3,2,1,0:T(8,128)(2,1)} %v_ref.3) | copy-start | bytes 4718596
  12.5 5.1 %collective-permute-start.4 = (f32[2,8,512]{2,1,0:T(8,128)S(1)}, f32[2,8,512]{2,1,0:T(8,128)S(1)}, u32[]{:S(2)}, u32[]{:S(2)}) collective-permute-start(f32[2,8,512]{2,1,0:T(8,128)S(1)} %get-tuple-element.49), channel_id=1, source_target_pairs={{0,8},{8,0},{16,24},{24,16},{32,40},{40,32},{48,56},{56,48},{64,72... | collective-permute-start | bytes 98312 | tf_op jit(solution)/shard_map/ppermute | solution.py:421
  16.0 25.3 %copy-start.4 = (f32[40,16,128]{2,1,0:T(8,128)S(1)}, f32[40,16,128]{2,1,0:T(8,128)}, u32[]{:S(2)}) copy-start(f32[40,16,128]{2,1,0:T(8,128)} %constant.5.clone.sums_ref) | copy-start | bytes 983044
  17.6 3.6 %collective-permute-start.5 = (f32[2,16,2048]{2,1,0:T(8,128)S(1)}, f32[2,16,2048]{2,1,0:T(8,128)S(1)}, u32[]{:S(2)}, u32[]{:S(2)}) collective-permute-start(f32[2,16,2048]{2,1,0:T(8,128)S(1)} %get-tuple-element.50.cs_ref), channel_id=1, source_target_pairs={{0,1},{1,0},{2,3},{3,2},{4,5},{5,4},{6,7},{7,6},{8,9},{9,8},{10,11... | collective-permute-start | bytes 786440 | tf_op jit(solution)/shard_map/ppermute | solution.py:421
  17.7 6.3 %collective-permute-start.7 = (f32[2,8,512]{2,1,0:T(8,128)S(1)}, f32[2,8,512]{2,1,0:T(8,128)S(1)}, u32[]{:S(2)}, u32[]{:S(2)}) collective-permute-start(f32[2,8,512]{2,1,0:T(8,128)S(1)} %get-tuple-element.54), channel_id=1, source_target_pairs={{0,16},{8,24},{16,0},{24,8},{32,48},{40,56},{48,32},{56,40},{64,80... | collective-permute-start | bytes 98312 | tf_op jit(solution)/shard_map/ppermute | solution.py:421
  20.9 4.0 %collective-permute-start.8 = (f32[2,8,512]{2,1,0:T(8,128)S(1)}, f32[2,8,512]{2,1,0:T(8,128)S(1)}, u32[]{:S(2)}, u32[]{:S(2)}) collective-permute-start(f32[2,8,512]{2,1,0:T(8,128)S(1)} %get-tuple-element.55), channel_id=1, source_target_pairs={{0,24},{8,16},{16,8},{24,0},{32,56},{40,48},{48,40},{56,32},{64,88... | collective-permute-start | bytes 98312 | tf_op jit(solution)/shard_map/ppermute | solution.py:421
  21.2 21.0 %collective-permute-start.6 = (f32[2,16,2048]{2,1,0:T(8,128)S(1)}, f32[2,16,2048]{2,1,0:T(8,128)S(1)}, u32[]{:S(2)}, u32[]{:S(2)}) collective-permute-start(f32[2,16,2048]{2,1,0:T(8,128)S(1)} %get-tuple-element.63.tot_ref), channel_id=1, source_target_pairs={{0,2},{1,3},{2,0},{3,1},{4,6},{5,7},{6,4},{7,5},{8,10},{9,11},{10,... | collective-permute-start | bytes 786440 | tf_op jit(solution)/shard_map/ppermute | solution.py:421
  42.3 19.2 %collective-permute-start.12 = (f32[16,2048]{1,0:T(8,128)S(1)}, f32[16,2048]{1,0:T(8,128)S(1)}, u32[]{:S(2)}, u32[]{:S(2)}) collective-permute-start(f32[16,2048]{1,0:T(8,128)S(1)} %get-tuple-element.67), channel_id=1, source_target_pairs={{0,4},{1,5},{2,6},{3,7},{4,0},{5,1},{6,2},{7,3},{8,12},{9,13},{10,... | collective-permute-start | bytes 393224 | tf_op jit(solution)/shard_map/ppermute | solution.py:421
  46.4 15.1 %all-to-all-start.1 = ((f32[32,8,128]{2,1,0:T(8,128)}), f32[32,8,128]{2,1,0:T(8,128)S(1)}, u32[]{:S(2)}, u32[]{:S(2)}) async-start(f32[32,8,128]{2,1,0:T(8,128)} %bitcast), calls=%async_computation.1 | async-start | bytes 262144 | tf_op jit(solution)/shard_map/all_to_all | solution.py:490
  53.3 4.4 %collective-permute-start.9 = (f32[2,8,512]{2,1,0:T(8,128)S(1)}, f32[2,8,512]{2,1,0:T(8,128)S(1)}, u32[]{:S(2)}, u32[]{:S(2)}) collective-permute-start(f32[2,8,512]{2,1,0:T(8,128)S(1)} %get-tuple-element.60), channel_id=1, source_target_pairs={{0,8},{8,0},{16,24},{24,16},{32,40},{40,32},{48,56},{56,48},{64,72... | collective-permute-start | bytes 98312 | tf_op jit(solution)/shard_map/ppermute | solution.py:421
  54.8 5.1 %collective-permute-start.10 = (f32[2,8,512]{2,1,0:T(8,128)S(1)}, f32[2,8,512]{2,1,0:T(8,128)S(1)}, u32[]{:S(2)}, u32[]{:S(2)}) collective-permute-start(f32[2,8,512]{2,1,0:T(8,128)S(1)} %get-tuple-element.61), channel_id=1, source_target_pairs={{0,16},{8,24},{16,0},{24,8},{32,48},{40,56},{48,32},{56,40},{64,80... | collective-permute-start | bytes 98312 | tf_op jit(solution)/shard_map/ppermute | solution.py:421
  57.2 4.0 %collective-permute-start.11 = (f32[2,8,512]{2,1,0:T(8,128)S(1)}, f32[2,8,512]{2,1,0:T(8,128)S(1)}, u32[]{:S(2)}, u32[]{:S(2)}) collective-permute-start(f32[2,8,512]{2,1,0:T(8,128)S(1)} %get-tuple-element.62), channel_id=1, source_target_pairs={{0,24},{8,16},{16,8},{24,0},{32,56},{40,48},{48,40},{56,32},{64,88... | collective-permute-start | bytes 98312 | tf_op jit(solution)/shard_map/ppermute | solution.py:421

commit v5 on v4

--- a/solution.py
+++ b/solution.py
@@ -23,75 +23,10 @@
     return 1.0 + half - np.sqrt(half * (2.0 + half))
 
 
-def line_factors(count, ratio):
-    q = decay(ratio)
-    i = np.arange(count)
-    low = 1.0 - q ** (2.0 * (i + 1))
-    high = 1.0 - q ** (2.0 * (count - i))
-    denom = ratio * (1.0 - q * q) * (1.0 - q ** (2.0 * count + 2))
-    return q, low, high, denom
-
-
-def split_line(count, ratio, parts):
-    q, low, high, denom = line_factors(count, ratio)
-    size = count // parts
-    low, high = low.reshape(parts, size), high.reshape(parts, size)
-    m = np.arange(size)
-    small = np.minimum(m[:, None], m[None])
-    large = np.maximum(m[:, None], m[None])
-    block = q ** (large - small + 1.0) * low[:, small] * high[:, large] / denom
-    up = q ** (size - 1.0 - m) * low
-    down = q ** (1.0 * m) * high
-    from_low = q ** (m + 2.0) * high / denom
-    from_high = q ** (size + 1.0 - m) * low / denom
-    return block, up, down, from_low, from_high, q**size
-
-
 QX, QY, QZ = decay(RX), decay(RY), decay(RZ)
 
 
-def tables():
-    block_y, up_y, down_y, gl_y, gh_y, step_y = split_line(NY, RY, DY)
-    block_z, up_z, down_z, gl_z, gh_z, step_z = split_line(NZ, RZ, DZ)
-    sums = np.zeros((DY + DZ, 16, 128))
-    tm = sums[DY:]
-    tm[:, :8, :8] = block_z
-    for e in range(DZ):
-        for p in range(DZ):
-            if p > e:
-                tm[e, 8 + p, :8] = up_z[e] * step_z ** (p - e - 1)
-            if p < e:
-                tm[e, 8 + p, :8] = down_z[e] * step_z ** (e - p - 1)
-    tm[:, :8, 8] = gl_z
-    tm[:, :8, 9] = gh_z
-    sums[:DY, :, 0] = gl_y
-    sums[:DY, :, 1] = gh_y
-    scal = np.zeros((DY, 128))
-    scal[:, :16] = gl_y
-    scal[:, 16:32] = gh_y
-    scal[:, 32:48] = up_y
-    scal[:, 48:64] = down_y
-    group = step_y**GX
-    for d in range(DY):
-        z, x = d // GX, d % GX
-        for i in range(GX):
-            xi = x ^ i
-            scal[d, 64 + i] = step_y ** (GX - 1 - xi)
-            scal[d, 68 + i] = step_y**xi
-            for j in range(GX):
-                xj = x ^ j
-                if xj < xi:
-                    scal[d, 80 + 4 * i + j] = step_y ** (xi - xj - 1)
-                if xj > xi:
-                    scal[d, 96 + 4 * i + j] = step_y ** (xj - xi - 1)
-        for p in range(GZ):
-            if p != z:
-                scal[d, 72 + p] = group ** (abs(p - z) - 1)
-    f32 = lambda a: a.astype(np.float32)
-    return f32(sums), f32(scal), float(step_z)
-
-
-SUMS, SCAL, STEP_Z = tables()
+STEP_Z = float(QZ**LZ)
 ROWS = LY * LZ
 
 
@@ -142,7 +77,7 @@
         z2_ref[y : y + 1, :] = jnp.where(odd_z, top, bottom)
 
 
-def inner_kernel(t_ref, v_ref, scal_ref, f_ref, mf_ref, ml_ref, wx_ref, tv_ref):
+def inner_kernel(t_ref, v_ref, f_ref, mf_ref, ml_ref, wx_ref, tv_ref, tz_ref):
     d, e = lax.axis_index("gy"), lax.axis_index("gz")
     zi = lax.broadcasted_iota(jnp.int32, (LZ, NX), 0)
     xi = lax.broadcasted_iota(jnp.int32, (LZ, NX), 1)
@@ -163,10 +98,6 @@
     j = lax.broadcasted_iota(jnp.int32, (XB, XB), 1)
     w = power(QX, (jnp.abs(i - j) + 1).astype(F32)) * (1.0 / (RX * (1 - QX * QX)))
     wx_ref[0], wx_ref[1] = halves(w)
-    row = scal_ref[pl.ds(d, 1), :]
-    r = lax.broadcasted_iota(jnp.int32, (128, 128), 0)
-    c = lax.broadcasted_iota(jnp.int32, (128, 128), 1)
-    tv_ref[...] = jnp.broadcast_to(jnp.sum(jnp.where(r == c, row, 0.0), axis=1, keepdims=True), (128, 128))
     lane = lax.broadcasted_iota(jnp.int32, (16, 128), 1)
     sub = lax.broadcasted_iota(jnp.int32, (16, 128), 0)
 
@@ -182,6 +113,31 @@
     mz = block(QZ, RZ, NZ, e * LZ, sub[:8], w8)
     up = power(QZ, (LZ - 1 - w8).astype(F32)) * (1.0 - power(QZ, 2.0 * (w8 + e * LZ + 1).astype(F32)))
     down = power(QZ, w8.astype(F32)) * (1.0 - power(QZ, 2.0 * (NZ - e * LZ - w8).astype(F32)))
+    wide, x, z = sub.astype(F32), lax.rem(d, GX), d // GX
+    at = (sub + d * LY).astype(F32)
+    low, high = 1.0 - power(QY, 2.0 * at + 2.0), 1.0 - power(QY, 2.0 * (NY - at))
+    scale = 1.0 / (RY * (1 - QY * QY) * (1 - QY ** (2.0 * NY + 2)))
+    tv_ref[0:16] = power(QY, wide + 2.0) * high * scale
+    tv_ref[16:32] = power(QY, LY + 1.0 - wide) * low * scale
+    tv_ref[32:48] = power(QY, LY - 1.0 - wide) * low
+    tv_ref[48:64] = power(QY, wide) * high
+    s8 = sub[:8]
+    xi = (s8 & (GX - 1)) ^ x
+    tv_ref[64:72] = power(QY, (LY * jnp.where(s8 < GX, GX - 1 - xi, xi)).astype(F32))
+    gap = jnp.abs(s8 - z)
+    tv_ref[72:80] = jnp.where(gap == 0, 0.0, power(QY, (LY * GX * (gap - 1)).astype(F32)))
+    ahead = ((sub >> 2) ^ x) - ((sub & (GX - 1)) ^ x)
+    tv_ref[80:96] = jnp.where(ahead > 0, power(QY, (LY * (ahead - 1)).astype(F32)), 0.0)
+    tv_ref[96:112] = jnp.where(ahead < 0, power(QY, (LY * (-ahead - 1)).astype(F32)), 0.0)
+    tv_ref[112:128] = jnp.zeros((16, 128), F32)
+    gap = jnp.abs(s8 - e)
+    reach = power(QZ, (LZ * (gap - 1)).astype(F32))
+    tz_ref[0:8] = mz
+    tz_ref[8:16] = jnp.where(s8 > e, up * reach, jnp.where(s8 < e, down * reach, 0.0))
+    wide, at = s8.astype(F32), (s8 + e * LZ).astype(F32)
+    scale = 1.0 / (RZ * (1 - QZ * QZ) * (1 - QZ ** (2.0 * NZ + 2)))
+    tz_ref[16:24] = power(QZ, wide + 2.0) * (1.0 - power(QZ, 2.0 * (NZ - at))) * scale
+    tz_ref[24:32] = power(QZ, LZ + 1.0 - wide) * (1.0 - power(QZ, 2.0 * at + 2.0)) * scale
     for l in range(LY // 2):
         pair = jnp.concatenate([my[2 * l : 2 * l + 1] * mz, my[2 * l + 1 : 2 * l + 2] * mz], axis=0)
         high, low = halves(pair)
@@ -267,9 +223,8 @@
             o_ref[p, :, cols] = tv_ref[72 + p : 73 + p, :] * jnp.where(p > z, tot[0], tot[1])
 
 
-def weights(sums_ref, first):
-    tm = sums_ref[DY + lax.axis_index("gz")]
-    return [jnp.broadcast_to(tm[first : first + 8, w : w + 1], (8, 128)) for w in range(8)]
+def weights(tz_ref, first):
+    return [jnp.broadcast_to(tz_ref[first : first + 8, w : w + 1], (8, 128)) for w in range(8)]
 
 
 def weighted(rows, p):
@@ -279,10 +234,10 @@
     return total
 
 
-def spread_kernel(a_ref, b_ref, c_ref, d_ref, r_ref, tv_ref, sums_ref, own_ref, s1_ref, s2_ref, s3_ref, o_ref):
+def spread_kernel(a_ref, b_ref, c_ref, d_ref, r_ref, tv_ref, tz_ref, own_ref, s1_ref, s2_ref, s3_ref, o_ref):
     d = lax.axis_index("gy")
     z, x = d // GX, lax.rem(d, GX)
-    out = weights(sums_ref, 8)
+    out = weights(tz_ref, 8)
     parts = (a_ref, b_ref, c_ref, d_ref)
     outs = (own_ref, s1_ref, s2_ref, s3_ref)
     for t in range(Q // 128):
@@ -329,11 +284,11 @@
     pre2_ref[1] = pre_ref[1] + jnp.where(upper, 0.0, high * x_ref[1])
 
 
-def own_kernel(p0_ref, p1_ref, p2_ref, p3_ref, sums_ref, dz_ref, p4):
+def own_kernel(p0_ref, p1_ref, p2_ref, p3_ref, tz_ref, dz_ref, p4):
     x = lax.rem(lax.axis_index("gy"), GX)
     for i, ref in enumerate((p0_ref, p1_ref, p2_ref, p3_ref)):
         p4[lax.bitwise_xor(x, i)] = ref[...]
-    own = weights(sums_ref, 0)
+    own = weights(tz_ref, 0)
     for k in range(2):
         for t in range(16):
             p = p4[t // 4, k, :, (t % 4) * 128 : (t % 4 + 1) * 128]
@@ -348,8 +303,8 @@
                                  + tv_ref[16 + l : 17 + l, :] * dz_ref[1, :, cols])
 
 
-def final_kernel(near_ref, pre_ref, x_ref, r_ref, sums_ref, o_hbm, cl, ch, o_ref, sems):
-    d, e = lax.axis_index("gy"), lax.axis_index("gz")
+def final_kernel(near_ref, pre_ref, x_ref, r_ref, tz_ref, tv_ref, o_hbm, cl, ch, o_ref, sems):
+    e = lax.axis_index("gz")
     low_rows, high_rows = [], []
     for q in range(GX):
         lo = jnp.zeros((8, 128), F32)
@@ -365,17 +320,14 @@
     power = lambda k: jnp.where(k == 0, 1.0, jnp.where(k == 1, STEP_Z, jnp.where(k == 2, STEP_Z**2, STEP_Z**3)))
     up = jnp.where(top, power(at), 0.0)
     down = jnp.where(top, 0.0, power(3 - at))
-    tg, tm = sums_ref[d], sums_ref[DY + e]
-    ga = jnp.broadcast_to(tg[:, 0:1], (16, 128))
-    gb = jnp.broadcast_to(tg[:, 1:2], (16, 128))
+    ga, gb = tv_ref[0:16], tv_ref[16:32]
     for t in range(NX // 128):
         cols = slice(t * 128, (t + 1) * 128)
         q, i = t // 4, t % 4
         lo, hi = low_rows[q], high_rows[q]
         cl[:, cols] = (pre_ref[0, :, cols] + up * x_ref[:, cols]) + (ga * lo[i : i + 1] + gb * lo[4 + i : 5 + i])
         ch[:, cols] = (pre_ref[1, :, cols] + down * x_ref[:, cols]) + (ga * hi[i : i + 1] + gb * hi[4 + i : 5 + i])
-    hl = jnp.broadcast_to(tm[:8, 8:9], (8, 128))
-    hh = jnp.broadcast_to(tm[:8, 9:10], (8, 128))
+    hl, hh = tz_ref[16:24], tz_ref[24:32]
     stores = []
     for l in range(LY):
         for t in range(NX // 128):
@@ -437,16 +389,16 @@
     y2 = lax.ppermute(y2, "gy", pairs(DY, True))
     z1 = lax.ppermute(z1, "gz", pairs(DZ, False))
     z2 = lax.ppermute(z2, "gz", pairs(DZ, True))
-    f, mf, ml, wx, tv = call(
+    f, mf, ml, wx, tv, tz = call(
         inner_kernel,
-        [FULL, bf(ROWS + 32, 256), bf(ROWS + 32, 128), bf(2, XB, XB), (128, 128)],
-        [VMEM] * 3,
-        [VMEM] * 5,
+        [FULL, bf(ROWS + 32, 256), bf(ROWS + 32, 128), bf(2, XB, XB), (128, 128), (32, 128)],
+        [VMEM] * 2,
+        [VMEM] * 6,
         [],
         16,
         "inner",
         (10**7, 8 * 10**6),
-    )(temp, vel, SCAL)
+    )(temp, vel)
     f, *mine = call(
         source_kernel,
         [FULL] + [QUARTER] * 4,
@@ -486,7 +438,7 @@
     r1, tot, pre = tie(r1, tot, pre)
     *mine, s = call(
         spread_kernel, [QUARTER] * 4 + [(GX, 64, 128)], [VMEM] * 7, [VMEM] * 5, [], 4, "spread", SMALL
-    )(*sets, r1, tv, SUMS)
+    )(*sets, r1, tv, tz)
     r3 = lax.all_to_all(s.reshape(GX * DZ, 8, 128), ("gy", "gz"), 0, 0, axis_index_groups=LAYER)
     sets = [mine[0]] + [across(mine[i], "gy", DY, i) for i in (1, 2, 3)]
     x2, sets[0] = tie(x2, sets[0])
@@ -494,17 +446,17 @@
     x3 = across(send, "gz", DZ, 4)
     dz = call(
         own_kernel, [(2, LZ, NX)], [VMEM] * 5, [VMEM], [pltpu.VMEM((GX, 2, LZ, Q), F32)], 8, "own", SMALL
-    )(*sets, SUMS)[0]
+    )(*sets, tz)[0]
     near = call(near_kernel, [FULL], [VMEM] * 3, [VMEM], [], 8, "near", (10**6, 2 * 10**6))(loc, dz, tv)[0]
     return call(
         final_kernel,
         [FULL],
-        [VMEM] * 5,
+        [VMEM] * 6,
         [HBM],
         [pltpu.VMEM((LY, NX), F32), pltpu.VMEM((LY, NX), F32), pltpu.VMEM(FULL, F32), dma((4,))],
         16,
         "final",
-    )(near, pre, x3, r3, SUMS)[0]
+    )(near, pre, x3, r3, tz, tv)[0]
 
 
 def solution(mesh):

time: 63.5 us -> 63.4 us (level)
  local copies, waits for them, and re-layouts: 3.58 us -> 2.65 us
  starting transfers between devices: 31.6 us -> 32.3 us
    unnamed x12 -> x8, local copies, waits for them, and re-layouts: 3.58 us -> 2.65 us
    ppermute x9, starting transfers between devices: 17.9 us -> 18.7 us  [across(): return lax.ppermute(value, axis, [(i, i ^ bit) for i in range(count)])]
  transfers between devices with their start and end apart: 14 -> 14, of which waited for: 4 -> 5; matrix products, arithmetic and copies ran while one was open for 0% -> 0% of each run, Pallas kernels for 6% -> 6%
where the time goes in v5:
time: 63.4 us; the launch traced here: 62.6 us
  starting transfers between devices  32.3 us (51%)
  blocking collectives  17 us (27%)
  Pallas kernels  6.12 us (10%)
  waiting for transfers between devices  4.36 us (7%)
  local copies, waits for them, and re-layouts  2.65 us (4%)
    ppermute x9, starting transfers between devices, across(): return lax.ppermute(value, axis, [(i, i ^ bit) for i in range(count)])  18.7 us
    all_to_all x1, blocking collectives, on_device(): r1 = lax.all_to_all(tots, 'gy', 0, 0, axis_index_groups=COLUMN)  17 us
    all_to_all x1, starting transfers between devices, on_device(): lax.all_to_all(s.reshape(GX * DZ, 8, 128), ('gy', 'gz'), 0, 0, axis_index...  6.89 us
    ppermute x9, waiting for transfers between devices, across(): return lax.ppermute(value, axis, [(i, i ^ bit) for i in range(count)])  4.18 us
    ppermute x1, starting transfers between devices, on_device(): z1 = lax.ppermute(z1, 'gz', pairs(DZ, False))  3.33 us
    unnamed x8, local copies, waits for them, and re-layouts  2.65 us
    ppermute x1, starting transfers between devices, on_device(): z2 = lax.ppermute(z2, 'gz', pairs(DZ, True))  1.91 us
    pallas_call x1, Pallas kernels, on_device(): call(local_kernel, [FULL, SUMS_Z], [VMEM] * 4, [VMEM] * 2, [pltpu.VMEM((N...  1.59 us
  transfers between devices with their start and end apart: 14, of which 5 were waited for; matrix products, arithmetic and copies ran while one was open for 0% of the time, Pallas kernels for 6%

profile of v5, /device:TPU:1, one launch (start us, length us, event | category | flops | bytes accessed | tf_op | source)
XLA Modules:
  0.0 62.6 jit_solution(6917633039827759715)
XLA Ops:
  0.0 0.0 copy-start.2
  0.0 1.2 %copy-done.2 = f32[16,8,2048]{2,1,0:T(8,128)S(1)} copy-done((f32[16,8,2048]{2,1,0:T(8,128)S(1)}, f32[16,8,2048]{2,1,0:T(8,128)}, u32[]{:S(2)}) %copy-start.2) | copy-done | bytes 1048600
  1.2 0.0 copy-start.3
  1.2 0.1 faces.1
  1.3 3.3 %collective-permute-start.2 = (f32[16,2048]{1,0:T(8,128)S(1)}, f32[16,2048]{1,0:T(8,128)S(1)}, u32[]{:S(2)}, u32[]{:S(2)}) collective-permute-start(f32[16,2048]{1,0:T(8,128)S(1)} %get-tuple-element.41), channel_id=1, source_target_pairs={{0,1},{1,0},{2,3},{3,2},{4,5},{5,4},{6,7},{7,6},{8,9},{9,8},{10,11... | collective-permute-start | bytes 393224 | tf_op jit(solution)/shard_map/ppermute | solution.py:390
  4.6 1.9 %collective-permute-start.3 = (f32[16,2048]{1,0:T(8,128)S(1)}, f32[16,2048]{1,0:T(8,128)S(1)}, u32[]{:S(2)}, u32[]{:S(2)}) collective-permute-start(f32[16,2048]{1,0:T(8,128)S(1)} %get-tuple-element.42), channel_id=1, source_target_pairs={{1,2},{2,1},{3,4},{4,3},{5,6},{6,5},{9,10},{10,9},{11,12},{12,11},... | collective-permute-start | bytes 393224 | tf_op jit(solution)/shard_map/ppermute | solution.py:391
  6.6 0.9 %collective-permute-start = (f32[8,2048]{1,0:T(8,128)S(1)}, f32[8,2048]{1,0:T(8,128)S(1)}, u32[]{:S(2)}, u32[]{:S(2)}) collective-permute-start(f32[8,2048]{1,0:T(8,128)S(1)} %get-tuple-element.39), channel_id=1, source_target_pairs={{0,8},{8,0},{16,24},{24,16},{32,40},{40,32},{48,56},{56,48},{64,72... | collective-permute-start | bytes 196616 | tf_op jit(solution)/shard_map/ppermute | solution.py:388
  7.5 0.7 %collective-permute-start.1 = (f32[8,2048]{1,0:T(8,128)S(1)}, f32[8,2048]{1,0:T(8,128)S(1)}, u32[]{:S(2)}, u32[]{:S(2)}) collective-permute-start(f32[8,2048]{1,0:T(8,128)S(1)} %get-tuple-element.40), channel_id=1, source_target_pairs={{8,16},{16,8},{24,32},{32,24},{40,48},{48,40},{56,64},{64,56},{72,... | collective-permute-start | bytes 196616 | tf_op jit(solution)/shard_map/ppermute | solution.py:389
  8.1 0.0 copy-done.3
  8.1 0.0 copy-start
  8.1 1.4 %copy-done = bf16[3,16,8,2048]{3,2,1,0:T(8,128)(2,1)S(1)} copy-done((bf16[3,16,8,2048]{3,2,1,0:T(8,128)(2,1)S(1)}, bf16[3,16,8,2048]{3,2,1,0:T(8,128)(2,1)}, u32[]{:S(2)}) %copy-start) | copy-done | bytes 1572888
  9.5 0.0 copy-start.1
  9.5 1.2 %inner.1 = (f32[16,8,2048]{2,1,0:T(8,128)S(1)}, bf16[160,256]{1,0:T(8,128)(2,1)S(1)}, bf16[160,128]{1,0:T(8,128)(2,1)S(1)}, bf16[2,256,256]{2,1,0:T(8,128)(2,1)S...) custom-call(f32[16,8,2048]{2,1,0:T(8,128)S(1)} %copy-done.3, bf16[3,16,8,2048]{3,2,1,0:T(8,128)(2,1)S(1)} %copy-done), custom_call_target="tpu_custom_call" | custom-call | flops 10000000 | bytes 8000000 | tf_op jit(solution)/shard_map/inner/pallas_call | solution.py:392
  10.7 0.0 collective-permute-done.y1_ref
  10.7 0.0 collective-permute-done.1.y2_ref
  10.7 0.0 collective-permute-done.2.z1_ref
  10.8 0.2 collective-permute-done.3.z2_ref
  10.9 0.0 copy-done.1
  10.9 0.9 %source.1 = (f32[16,8,2048]{2,1,0:T(8,128)S(1)}, f32[2,8,512]{2,1,0:T(8,128)S(1)}, f32[2,8,512]{2,1,0:T(8,128)S(1)}, f32[2,8,512]{2,1,0:T(8,128)S(1)}, f32[2,8,512]{2,1,0:T(8,128)S(1)}) custom-call(f32[16,8,2048]{2,1,0:T(8,128)S(1)} %get-tuple-element.38.f0_ref, bf16[3,16,8,2048]{3,2,1,0:T(8,128)(2,1)S(1)} %copy-done.1, ...), custom_call_target="tpu_custom_call" | custom-call | tf_op jit(solution)/shard_map/source/pallas_call | solution.py:402
  11.8 3.5 %collective-permute-start.4 = (f32[2,8,512]{2,1,0:T(8,128)S(1)}, f32[2,8,512]{2,1,0:T(8,128)S(1)}, u32[]{:S(2)}, u32[]{:S(2)}) collective-permute-start(f32[2,8,512]{2,1,0:T(8,128)S(1)} %get-tuple-element.50), channel_id=1, source_target_pairs={{0,8},{8,0},{16,24},{24,16},{32,40},{40,32},{48,56},{56,48},{64,72... | collective-permute-start | bytes 98312 | tf_op jit(solution)/shard_map/ppermute | solution.py:373
  15.3 1.6 %local.1 = (f32[16,8,2048]{2,1,0:T(8,128)S(1)}, f32[2,16,2048]{2,1,0:T(8,128)S(1)}) custom-call(f32[16,8,2048]{2,1,0:T(8,128)S(1)} %get-tuple-element.45.f_ref, bf16[2,256,256]{2,1,0:T(8,128)(2,1)S(1)} %get-tuple-element.43.wx_ref, bf16[160,256]{1,0:T(8,128)(2,1)S(1)} %get-tuple-element.46.mf_ref, bf16[160,128]{1,0:T(8,128)(2,1)S(1)} %get-tuple-element.47.ml_ref), custom_call_target="tpu_custom_call" | custom-call | flops 2000000000 | bytes 8000000 | tf_op jit(solution)/shard_map/local/pallas_call | solution.py:417
  16.9 0.0 collective-permute-done.4.b_ref
  16.9 0.3 collective-permute-start.5
  17.1 3.2 %collective-permute-start.7 = (f32[2,8,512]{2,1,0:T(8,128)S(1)}, f32[2,8,512]{2,1,0:T(8,128)S(1)}, u32[]{:S(2)}, u32[]{:S(2)}) collective-permute-start(f32[2,8,512]{2,1,0:T(8,128)S(1)} %get-tuple-element.55), channel_id=1, source_target_pairs={{0,16},{8,24},{16,0},{24,8},{32,48},{40,56},{48,32},{56,40},{64,80... | collective-permute-start | bytes 98312 | tf_op jit(solution)/shard_map/ppermute | solution.py:373
  20.3 1.2 %collective-permute-start.8 = (f32[2,8,512]{2,1,0:T(8,128)S(1)}, f32[2,8,512]{2,1,0:T(8,128)S(1)}, u32[]{:S(2)}, u32[]{:S(2)}) collective-permute-start(f32[2,8,512]{2,1,0:T(8,128)S(1)} %get-tuple-element.56), channel_id=1, source_target_pairs={{0,24},{8,16},{16,8},{24,0},{32,56},{40,48},{48,40},{56,32},{64,88... | collective-permute-start | bytes 98312 | tf_op jit(solution)/shard_map/ppermute | solution.py:373
  21.5 0.0 collective-permute-done.5.x_ref
  21.5 0.1 pair.1
  21.6 2.5 %collective-permute-start.6 = (f32[2,16,2048]{2,1,0:T(8,128)S(1)}, f32[2,16,2048]{2,1,0:T(8,128)S(1)}, u32[]{:S(2)}, u32[]{:S(2)}) collective-permute-start(f32[2,16,2048]{2,1,0:T(8,128)S(1)} %get-tuple-element.65.tot_ref), channel_id=1, source_target_pairs={{0,2},{1,3},{2,0},{3,1},{4,6},{5,7},{6,4},{7,5},{8,10},{9,11},{10,... | collective-permute-start | bytes 786440 | tf_op jit(solution)/shard_map/ppermute | solution.py:373
  24.1 0.0 collective-permute-done.7.c_ref
  24.1 0.3 collective-permute-done.8.d_ref
  24.3 17.0 %all_to_all.10.r_ref = f32[8,8,512]{2,1,0:T(8,128)S(1)} all-to-all(f32[8,8,512]{2,1,0:T(8,128)S(1)} %group.1), channel_id=1, replica_groups={{0,32,64,96,128,160,192,224},{8,40,72,104,136,168,200,232},{16,48,80,11..., dimensions={0} | all-to-all | bytes 262144 | tf_op jit(solution)/shard_map/all_to_all | solution.py:435
  41.3 0.8 %spread.1 = (f32[2,8,512]{2,1,0:T(8,128)S(1)}, f32[2,8,512]{2,1,0:T(8,128)S(1)}, f32[2,8,512]{2,1,0:T(8,128)S(1)}, f32[2,8,512]{2,1,0:T(8,128)S(1)}, f32[4,64,128]{2,1,0:T(8,128)}) custom-call(f32[2,8,512]{2,1,0:T(8,128)S(1)} %get-tuple-element.53.a_ref, f32[2,8,512]{2,1,0:T(8,128)S(1)} %collective-permute-done.4.b_ref, ...), custom_call_target="tpu_custom_call" | custom-call | flops 100000 | bytes 500000 | tf_op jit(solution)/shard_map/spread/pallas_call | solution.py:439
  42.2 0.0 collective-permute-done.6.x_ref
  42.2 0.1 quad.1
  42.3 4.1 %collective-permute-start.12 = (f32[16,2048]{1,0:T(8,128)S(1)}, f32[16,2048]{1,0:T(8,128)S(1)}, u32[]{:S(2)}, u32[]{:S(2)}) collective-permute-start(f32[16,2048]{1,0:T(8,128)S(1)} %get-tuple-element.69), channel_id=1, source_target_pairs={{0,4},{1,5},{2,6},{3,7},{4,0},{5,1},{6,2},{7,3},{8,12},{9,13},{10,... | collective-permute-start | bytes 393224 | tf_op jit(solution)/shard_map/ppermute | solution.py:373
  46.4 6.9 %all-to-all-start.1 = ((f32[32,8,128]{2,1,0:T(8,128)}), f32[32,8,128]{2,1,0:T(8,128)S(1)}, u32[]{:S(2)}, u32[]{:S(2)}) async-start(f32[32,8,128]{2,1,0:T(8,128)} %bitcast), calls=%async_computation.1 | async-start | bytes 262144 | tf_op jit(solution)/shard_map/all_to_all | solution.py:442
  53.3 1.5 %collective-permute-start.9 = (f32[2,8,512]{2,1,0:T(8,128)S(1)}, f32[2,8,512]{2,1,0:T(8,128)S(1)}, u32[]{:S(2)}, u32[]{:S(2)}) collective-permute-start(f32[2,8,512]{2,1,0:T(8,128)S(1)} %get-tuple-element.62), channel_id=1, source_target_pairs={{0,8},{8,0},{16,24},{24,16},{32,40},{40,32},{48,56},{56,48},{64,72... | collective-permute-start | bytes 98312 | tf_op jit(solution)/shard_map/ppermute | solution.py:373
  54.8 2.4 %collective-permute-start.10 = (f32[2,8,512]{2,1,0:T(8,128)S(1)}, f32[2,8,512]{2,1,0:T(8,128)S(1)}, u32[]{:S(2)}, u32[]{:S(2)}) collective-permute-start(f32[2,8,512]{2,1,0:T(8,128)S(1)} %get-tuple-element.63), channel_id=1, source_target_pairs={{0,16},{8,24},{16,0},{24,8},{32,48},{40,56},{48,32},{56,40},{64,80... | collective-permute-start | bytes 98312 | tf_op jit(solution)/shard_map/ppermute | solution.py:373
  57.2 0.1 collective-permute-start.11
  57.3 0.4 collective-permute-done.9.p1_ref
  57.7 2.2 %collective-permute-done.10.p2_ref = f32[2,8,512]{2,1,0:T(8,128)S(1)} collective-permute-done((f32[2,8,512]{2,1,0:T(8,128)S(1)}, f32[2,8,512]{2,1,0:T(8,128)S(1)}, u32[]{:S(2)}, u32[]{:S(2)}) %collective-permute-start.10) | collective-permute-done | bytes 32800 | tf_op jit(solution)/shard_map/ppermute | solution.py:373
  59.9 1.3 %collective-permute-done.11.p3_ref = f32[2,8,512]{2,1,0:T(8,128)S(1)} collective-permute-done((f32[2,8,512]{2,1,0:T(8,128)S(1)}, f32[2,8,512]{2,1,0:T(8,128)S(1)}, u32[]{:S(2)}, u32[]{:S(2)}) %collective-permute-start.11) | collective-permute-done | bytes 32800 | tf_op jit(solution)/shard_map/ppermute | solution.py:373
  61.2 0.1 own.1.dz_ref
  61.3 0.1 near.1.near_ref
  61.5 0.0 all-to-all-done.1.r_ref
  61.5 0.0 collective-permute-done.12.x_ref
  61.5 1.1 %final.1 = f32[16,8,2048]{2,1,0:T(8,128)} custom-call(f32[16,8,2048]{2,1,0:T(8,128)S(1)} %near.1.near_ref, f32[2,16,2048]{2,1,0:T(8,128)S(1)} %get-tuple-element.68.pre_ref, f32[16,2048]{1,0:T(8,128)S(1)} %collective-permute-done.12.x_ref, f32[32,8,128]{2,1,0:T(8,128)S(1)} %all-to-all-done.1.r_ref, f32[32,128]{1,0:T(8,128)S(1)} %get-tuple-element.59.tz_ref, ...), custom_call_target="tpu_custom_call" | custom-call | tf_op jit(solution)/shard_map/final/pallas_call | solution.py:451
  (1 shorter events, 0.0 us)
Async XLA Ops:
  0.0 1.2 %copy-start.2 = (f32[16,8,2048]{2,1,0:T(8,128)S(1)}, f32[16,8,2048]{2,1,0:T(8,128)}, u32[]{:S(2)}) copy-start(f32[16,8,2048]{2,1,0:T(8,128)} %t_ref.3) | copy-start | bytes 3145732
  1.2 6.9 %copy-start.3 = (f32[16,8,2048]{2,1,0:T(8,128)S(1)}, f32[16,8,2048]{2,1,0:T(8,128)}, u32[]{:S(2)}) copy-start(f32[16,8,2048]{2,1,0:T(8,128)} %t_ref.3) | copy-start | bytes 3145732
  1.3 9.4 %collective-permute-start.2 = (f32[16,2048]{1,0:T(8,128)S(1)}, f32[16,2048]{1,0:T(8,128)S(1)}, u32[]{:S(2)}, u32[]{:S(2)}) collective-permute-start(f32[16,2048]{1,0:T(8,128)S(1)} %get-tuple-element.41), channel_id=1, source_target_pairs={{0,1},{1,0},{2,3},{3,2},{4,5},{5,4},{6,7},{7,6},{8,9},{9,8},{10,11... | collective-permute-start | bytes 393224 | tf_op jit(solution)/shard_map/ppermute | solution.py:390
  4.6 6.3 %collective-permute-start.3 = (f32[16,2048]{1,0:T(8,128)S(1)}, f32[16,2048]{1,0:T(8,128)S(1)}, u32[]{:S(2)}, u32[]{:S(2)}) collective-permute-start(f32[16,2048]{1,0:T(8,128)S(1)} %get-tuple-element.42), channel_id=1, source_target_pairs={{1,2},{2,1},{3,4},{4,3},{5,6},{6,5},{9,10},{10,9},{11,12},{12,11},... | collective-permute-start | bytes 393224 | tf_op jit(solution)/shard_map/ppermute | solution.py:391
  6.6 4.2 %collective-permute-start = (f32[8,2048]{1,0:T(8,128)S(1)}, f32[8,2048]{1,0:T(8,128)S(1)}, u32[]{:S(2)}, u32[]{:S(2)}) collective-permute-start(f32[8,2048]{1,0:T(8,128)S(1)} %get-tuple-element.39), channel_id=1, source_target_pairs={{0,8},{8,0},{16,24},{24,16},{32,40},{40,32},{48,56},{56,48},{64,72... | collective-permute-start | bytes 196616 | tf_op jit(solution)/shard_map/ppermute | solution.py:388
  7.5 3.3 %collective-permute-start.1 = (f32[8,2048]{1,0:T(8,128)S(1)}, f32[8,2048]{1,0:T(8,128)S(1)}, u32[]{:S(2)}, u32[]{:S(2)}) collective-permute-start(f32[8,2048]{1,0:T(8,128)S(1)} %get-tuple-element.40), channel_id=1, source_target_pairs={{8,16},{16,8},{24,32},{32,24},{40,48},{48,40},{56,64},{64,56},{72,... | collective-permute-start | bytes 196616 | tf_op jit(solution)/shard_map/ppermute | solution.py:389
  8.1 1.4 %copy-start = (bf16[3,16,8,2048]{3,2,1,0:T(8,128)(2,1)S(1)}, bf16[3,16,8,2048]{3,2,1,0:T(8,128)(2,1)}, u32[]{:S(2)}) copy-start(bf16[3,16,8,2048]{3,2,1,0:T(8,128)(2,1)} %v_ref.3) | copy-start | bytes 4718596
  9.5 1.4 %copy-start.1 = (bf16[3,16,8,2048]{3,2,1,0:T(8,128)(2,1)S(1)}, bf16[3,16,8,2048]{3,2,1,0:T(8,128)(2,1)}, u32[]{:S(2)}) copy-start(bf16[3,16,8,2048]{3,2,1,0:T(8,128)(2,1)} %v_ref.3) | copy-start | bytes 4718596
  11.8 5.1 %collective-permute-start.4 = (f32[2,8,512]{2,1,0:T(8,128)S(1)}, f32[2,8,512]{2,1,0:T(8,128)S(1)}, u32[]{:S(2)}, u32[]{:S(2)}) collective-permute-start(f32[2,8,512]{2,1,0:T(8,128)S(1)} %get-tuple-element.50), channel_id=1, source_target_pairs={{0,8},{8,0},{16,24},{24,16},{32,40},{40,32},{48,56},{56,48},{64,72... | collective-permute-start | bytes 98312 | tf_op jit(solution)/shard_map/ppermute | solution.py:373
  16.9 4.6 %collective-permute-start.5 = (f32[2,16,2048]{2,1,0:T(8,128)S(1)}, f32[2,16,2048]{2,1,0:T(8,128)S(1)}, u32[]{:S(2)}, u32[]{:S(2)}) collective-permute-start(f32[2,16,2048]{2,1,0:T(8,128)S(1)} %get-tuple-element.51.cs_ref), channel_id=1, source_target_pairs={{0,1},{1,0},{2,3},{3,2},{4,5},{5,4},{6,7},{7,6},{8,9},{9,8},{10,11... | collective-permute-start | bytes 786440 | tf_op jit(solution)/shard_map/ppermute | solution.py:373
  17.1 6.9 %collective-permute-start.7 = (f32[2,8,512]{2,1,0:T(8,128)S(1)}, f32[2,8,512]{2,1,0:T(8,128)S(1)}, u32[]{:S(2)}, u32[]{:S(2)}) collective-permute-start(f32[2,8,512]{2,1,0:T(8,128)S(1)} %get-tuple-element.55), channel_id=1, source_target_pairs={{0,16},{8,24},{16,0},{24,8},{32,48},{40,56},{48,32},{56,40},{64,80... | collective-permute-start | bytes 98312 | tf_op jit(solution)/shard_map/ppermute | solution.py:373
  20.3 4.0 %collective-permute-start.8 = (f32[2,8,512]{2,1,0:T(8,128)S(1)}, f32[2,8,512]{2,1,0:T(8,128)S(1)}, u32[]{:S(2)}, u32[]{:S(2)}) collective-permute-start(f32[2,8,512]{2,1,0:T(8,128)S(1)} %get-tuple-element.56), channel_id=1, source_target_pairs={{0,24},{8,16},{16,8},{24,0},{32,56},{40,48},{48,40},{56,32},{64,88... | collective-permute-start | bytes 98312 | tf_op jit(solution)/shard_map/ppermute | solution.py:373
  21.6 20.6 %collective-permute-start.6 = (f32[2,16,2048]{2,1,0:T(8,128)S(1)}, f32[2,16,2048]{2,1,0:T(8,128)S(1)}, u32[]{:S(2)}, u32[]{:S(2)}) collective-permute-start(f32[2,16,2048]{2,1,0:T(8,128)S(1)} %get-tuple-element.65.tot_ref), channel_id=1, source_target_pairs={{0,2},{1,3},{2,0},{3,1},{4,6},{5,7},{6,4},{7,5},{8,10},{9,11},{10,... | collective-permute-start | bytes 786440 | tf_op jit(solution)/shard_map/ppermute | solution.py:373
  42.3 19.2 %collective-permute-start.12 = (f32[16,2048]{1,0:T(8,128)S(1)}, f32[16,2048]{1,0:T(8,128)S(1)}, u32[]{:S(2)}, u32[]{:S(2)}) collective-permute-start(f32[16,2048]{1,0:T(8,128)S(1)} %get-tuple-element.69), channel_id=1, source_target_pairs={{0,4},{1,5},{2,6},{3,7},{4,0},{5,1},{6,2},{7,3},{8,12},{9,13},{10,... | collective-permute-start | bytes 393224 | tf_op jit(solution)/shard_map/ppermute | solution.py:373
  46.4 15.1 %all-to-all-start.1 = ((f32[32,8,128]{2,1,0:T(8,128)}), f32[32,8,128]{2,1,0:T(8,128)S(1)}, u32[]{:S(2)}, u32[]{:S(2)}) async-start(f32[32,8,128]{2,1,0:T(8,128)} %bitcast), calls=%async_computation.1 | async-start | bytes 262144 | tf_op jit(solution)/shard_map/all_to_all | solution.py:442
  53.3 4.4 %collective-permute-start.9 = (f32[2,8,512]{2,1,0:T(8,128)S(1)}, f32[2,8,512]{2,1,0:T(8,128)S(1)}, u32[]{:S(2)}, u32[]{:S(2)}) collective-permute-start(f32[2,8,512]{2,1,0:T(8,128)S(1)} %get-tuple-element.62), channel_id=1, source_target_pairs={{0,8},{8,0},{16,24},{24,16},{32,40},{40,32},{48,56},{56,48},{64,72... | collective-permute-start | bytes 98312 | tf_op jit(solution)/shard_map/ppermute | solution.py:373
  54.8 5.1 %collective-permute-start.10 = (f32[2,8,512]{2,1,0:T(8,128)S(1)}, f32[2,8,512]{2,1,0:T(8,128)S(1)}, u32[]{:S(2)}, u32[]{:S(2)}) collective-permute-start(f32[2,8,512]{2,1,0:T(8,128)S(1)} %get-tuple-element.63), channel_id=1, source_target_pairs={{0,16},{8,24},{16,0},{24,8},{32,48},{40,56},{48,32},{56,40},{64,80... | collective-permute-start | bytes 98312 | tf_op jit(solution)/shard_map/ppermute | solution.py:373
  57.2 4.0 %collective-permute-start.11 = (f32[2,8,512]{2,1,0:T(8,128)S(1)}, f32[2,8,512]{2,1,0:T(8,128)S(1)}, u32[]{:S(2)}, u32[]{:S(2)}) collective-permute-start(f32[2,8,512]{2,1,0:T(8,128)S(1)} %get-tuple-element.64), channel_id=1, source_target_pairs={{0,24},{8,16},{16,8},{24,0},{32,56},{40,48},{48,40},{56,32},{64,88... | collective-permute-start | bytes 98312 | tf_op jit(solution)/shard_map/ppermute | solution.py:373

commit v6 on v5

--- a/solution.py
+++ b/solution.py
@@ -65,8 +65,11 @@
         put(2 * b + 1, g[b, :, 128:] + after * right)
 
 
-def faces_kernel(t_ref, y1_ref, y2_ref, z1_ref, z2_ref):
+def faces_kernel(t_hbm, y1_ref, y2_ref, z1_ref, z2_ref, t_ref, sems):
     d, e = lax.axis_index("gy"), lax.axis_index("gz")
+    loads = start(*((t_hbm.at[pl.ds(4 * i, 4)], t_ref.at[pl.ds(4 * i, 4)], sems.at[i]) for i in range(LY // 4)))
+    for load in loads:
+        load.wait()
     odd_y, odd_z = (d % 2) == 1, (e % 2) == 1
     first, last = t_ref[0], t_ref[LY - 1]
     y1_ref[...] = jnp.where(odd_y, first, last)
@@ -383,7 +386,7 @@
     dma = pltpu.SemaphoreType.DMA
     bf = lambda *shape: jax.ShapeDtypeStruct(shape, BF16)
     y1, y2, z1, z2 = call(
-        faces_kernel, [(LZ, NX), (LZ, NX), (LY, NX), (LY, NX)], [VMEM], [VMEM] * 4, [], 4, "faces"
+        faces_kernel, [(LZ, NX), (LZ, NX), (LY, NX), (LY, NX)], [HBM], [VMEM] * 4, [pltpu.VMEM(FULL, F32), dma((LY // 4,))], 62, "faces"
     )(temp)
     y1 = lax.ppermute(y1, "gy", pairs(DY, False))
     y2 = lax.ppermute(y2, "gy", pairs(DY, True))

time: 63.4 us -> 64.3 us (1.014)
  Pallas kernels: 6.12 us -> 8.13 us
  local copies, waits for them, and re-layouts: 2.65 us -> 1.41 us
    pallas_call x1, Pallas kernels: 0.08 us -> 2.09 us  [on_device(): call(faces_kernel, [(LZ, NX), (LZ, NX), (LY, NX), (LY, NX)], [HBM], [VMEM...]
    unnamed x8 -> x6, local copies, waits for them, and re-layouts: 2.65 us -> 1.41 us
where the time goes in v6:
time: 64.3 us; the launch traced here: 63.6 us
  starting transfers between devices  32.2 us (50%)
  blocking collectives  17.1 us (27%)
  Pallas kernels  8.13 us (13%)
  waiting for transfers between devices  4.66 us (7%)
  local copies, waits for them, and re-layouts  1.41 us (2%)
    ppermute x9, starting transfers between devices, across(): return lax.ppermute(value, axis, [(i, i ^ bit) for i in range(count)])  18.5 us
    all_to_all x1, blocking collectives, on_device(): r1 = lax.all_to_all(tots, 'gy', 0, 0, axis_index_groups=COLUMN)  17.1 us
    all_to_all x1, starting transfers between devices, on_device(): lax.all_to_all(s.reshape(GX * DZ, 8, 128), ('gy', 'gz'), 0, 0, axis_index...  6.97 us
    ppermute x9, waiting for transfers between devices, across(): return lax.ppermute(value, axis, [(i, i ^ bit) for i in range(count)])  4.13 us
    ppermute x1, starting transfers between devices, on_device(): z1 = lax.ppermute(z1, 'gz', pairs(DZ, False))  3.33 us
    pallas_call x1, Pallas kernels, on_device(): call(faces_kernel, [(LZ, NX), (LZ, NX), (LY, NX), (LY, NX)], [HBM], [VMEM...  2.09 us
    ppermute x1, starting transfers between devices, on_device(): z2 = lax.ppermute(z2, 'gz', pairs(DZ, True))  1.91 us
    pallas_call x1, Pallas kernels, on_device(): call(local_kernel, [FULL, SUMS_Z], [VMEM] * 4, [VMEM] * 2, [pltpu.VMEM((N...  1.59 us
  transfers between devices with their start and end apart: 14, of which 5 were waited for; matrix products, arithmetic and copies ran while one was open for 0% of the time, Pallas kernels for 6%

profile of v6, /device:TPU:1, one launch (start us, length us, event | category | flops | bytes accessed | tf_op | source)
XLA Modules:
  0.0 63.6 jit_solution(11501613436202096411)
XLA Ops:
  0.0 0.0 copy-start.2
  0.0 2.1 %faces.1 = (f32[8,2048]{1,0:T(8,128)}, f32[8,2048]{1,0:T(8,128)}, f32[16,2048]{1,0:T(8,128)}, f32[16,2048]{1,0:T(8,128)}) custom-call(f32[16,8,2048]{2,1,0:T(8,128)} %t_hbm.1), custom_call_target="tpu_custom_call" | custom-call | tf_op jit(solution)/shard_map/faces/pallas_call | solution.py:388
  2.1 3.3 %collective-permute-start.2 = (f32[16,2048]{1,0:T(8,128)}, f32[16,2048]{1,0:T(8,128)S(1)}, u32[]{:S(2)}, u32[]{:S(2)}) collective-permute-start(f32[16,2048]{1,0:T(8,128)} %get-tuple-element.41), channel_id=1, source_target_pairs={{0,1},{1,0},{2,3},{3,2},{4,5},{5,4},{6,7},{7,6},{8,9},{9,8},{10,11... | collective-permute-start | bytes 393224 | tf_op jit(solution)/shard_map/ppermute | solution.py:393
  5.4 1.9 %collective-permute-start.3 = (f32[16,2048]{1,0:T(8,128)}, f32[16,2048]{1,0:T(8,128)S(1)}, u32[]{:S(2)}, u32[]{:S(2)}) collective-permute-start(f32[16,2048]{1,0:T(8,128)} %get-tuple-element.42), channel_id=1, source_target_pairs={{1,2},{2,1},{3,4},{4,3},{5,6},{6,5},{9,10},{10,9},{11,12},{12,11},... | collective-permute-start | bytes 393224 | tf_op jit(solution)/shard_map/ppermute | solution.py:394
  7.3 0.8 %collective-permute-start = (f32[8,2048]{1,0:T(8,128)}, f32[8,2048]{1,0:T(8,128)S(1)}, u32[]{:S(2)}, u32[]{:S(2)}) collective-permute-start(f32[8,2048]{1,0:T(8,128)} %get-tuple-element.39), channel_id=1, source_target_pairs={{0,8},{8,0},{16,24},{24,16},{32,40},{40,32},{48,56},{56,48},{64,72... | collective-permute-start | bytes 196616 | tf_op jit(solution)/shard_map/ppermute | solution.py:391
  8.1 0.7 %collective-permute-start.1 = (f32[8,2048]{1,0:T(8,128)}, f32[8,2048]{1,0:T(8,128)S(1)}, u32[]{:S(2)}, u32[]{:S(2)}) collective-permute-start(f32[8,2048]{1,0:T(8,128)} %get-tuple-element.40), channel_id=1, source_target_pairs={{8,16},{16,8},{24,32},{32,24},{40,48},{48,40},{56,64},{64,56},{72,... | collective-permute-start | bytes 196616 | tf_op jit(solution)/shard_map/ppermute | solution.py:392
  8.8 0.0 copy-done.2
  8.8 0.0 copy-start
  8.8 1.4 %copy-done = bf16[3,16,8,2048]{3,2,1,0:T(8,128)(2,1)S(1)} copy-done((bf16[3,16,8,2048]{3,2,1,0:T(8,128)(2,1)S(1)}, bf16[3,16,8,2048]{3,2,1,0:T(8,128)(2,1)}, u32[]{:S(2)}) %copy-start) | copy-done | bytes 1572888
  10.2 0.0 copy-start.1
  10.2 1.2 %inner.1 = (f32[16,8,2048]{2,1,0:T(8,128)S(1)}, bf16[160,256]{1,0:T(8,128)(2,1)S(1)}, bf16[160,128]{1,0:T(8,128)(2,1)S(1)}, bf16[2,256,256]{2,1,0:T(8,128)(2,1)S...) custom-call(f32[16,8,2048]{2,1,0:T(8,128)S(1)} %copy-done.2, bf16[3,16,8,2048]{3,2,1,0:T(8,128)(2,1)S(1)} %copy-done), custom_call_target="tpu_custom_call" | custom-call | flops 10000000 | bytes 8000000 | tf_op jit(solution)/shard_map/inner/pallas_call | solution.py:395
  11.4 0.0 collective-permute-done.y1_ref
  11.4 0.0 collective-permute-done.1.y2_ref
  11.4 0.0 collective-permute-done.2.z1_ref
  11.4 0.5 collective-permute-done.3.z2_ref
  11.9 0.0 copy-done.1
  11.9 0.9 %source.1 = (f32[16,8,2048]{2,1,0:T(8,128)S(1)}, f32[2,8,512]{2,1,0:T(8,128)S(1)}, f32[2,8,512]{2,1,0:T(8,128)S(1)}, f32[2,8,512]{2,1,0:T(8,128)S(1)}, f32[2,8,512]{2,1,0:T(8,128)S(1)}) custom-call(f32[16,8,2048]{2,1,0:T(8,128)S(1)} %get-tuple-element.38.f0_ref, bf16[3,16,8,2048]{3,2,1,0:T(8,128)(2,1)S(1)} %copy-done.1, ...), custom_call_target="tpu_custom_call" | custom-call | tf_op jit(solution)/shard_map/source/pallas_call | solution.py:405
  12.8 3.1 %collective-permute-start.4 = (f32[2,8,512]{2,1,0:T(8,128)S(1)}, f32[2,8,512]{2,1,0:T(8,128)S(1)}, u32[]{:S(2)}, u32[]{:S(2)}) collective-permute-start(f32[2,8,512]{2,1,0:T(8,128)S(1)} %get-tuple-element.50), channel_id=1, source_target_pairs={{0,8},{8,0},{16,24},{24,16},{32,40},{40,32},{48,56},{56,48},{64,72... | collective-permute-start | bytes 98312 | tf_op jit(solution)/shard_map/ppermute | solution.py:376
  15.9 1.6 %local.1 = (f32[16,8,2048]{2,1,0:T(8,128)S(1)}, f32[2,16,2048]{2,1,0:T(8,128)S(1)}) custom-call(f32[16,8,2048]{2,1,0:T(8,128)S(1)} %get-tuple-element.45.f_ref, bf16[2,256,256]{2,1,0:T(8,128)(2,1)S(1)} %get-tuple-element.43.wx_ref, bf16[160,256]{1,0:T(8,128)(2,1)S(1)} %get-tuple-element.46.mf_ref, bf16[160,128]{1,0:T(8,128)(2,1)S(1)} %get-tuple-element.47.ml_ref), custom_call_target="tpu_custom_call" | custom-call | flops 2000000000 | bytes 8000000 | tf_op jit(solution)/shard_map/local/pallas_call | solution.py:420
  17.5 0.0 collective-permute-done.4.b_ref
  17.5 0.4 collective-permute-start.5
  17.9 3.2 %collective-permute-start.7 = (f32[2,8,512]{2,1,0:T(8,128)S(1)}, f32[2,8,512]{2,1,0:T(8,128)S(1)}, u32[]{:S(2)}, u32[]{:S(2)}) collective-permute-start(f32[2,8,512]{2,1,0:T(8,128)S(1)} %get-tuple-element.55), channel_id=1, source_target_pairs={{0,16},{8,24},{16,0},{24,8},{32,48},{40,56},{48,32},{56,40},{64,80... | collective-permute-start | bytes 98312 | tf_op jit(solution)/shard_map/ppermute | solution.py:376
  21.2 0.9 %collective-permute-start.8 = (f32[2,8,512]{2,1,0:T(8,128)S(1)}, f32[2,8,512]{2,1,0:T(8,128)S(1)}, u32[]{:S(2)}, u32[]{:S(2)}) collective-permute-start(f32[2,8,512]{2,1,0:T(8,128)S(1)} %get-tuple-element.56), channel_id=1, source_target_pairs={{0,24},{8,16},{16,8},{24,0},{32,56},{40,48},{48,40},{56,32},{64,88... | collective-permute-start | bytes 98312 | tf_op jit(solution)/shard_map/ppermute | solution.py:376
  22.1 0.0 collective-permute-done.5.x_ref
  22.1 0.1 pair.1
  22.2 2.8 %collective-permute-start.6 = (f32[2,16,2048]{2,1,0:T(8,128)S(1)}, f32[2,16,2048]{2,1,0:T(8,128)S(1)}, u32[]{:S(2)}, u32[]{:S(2)}) collective-permute-start(f32[2,16,2048]{2,1,0:T(8,128)S(1)} %get-tuple-element.65.tot_ref), channel_id=1, source_target_pairs={{0,2},{1,3},{2,0},{3,1},{4,6},{5,7},{6,4},{7,5},{8,10},{9,11},{10,... | collective-permute-start | bytes 786440 | tf_op jit(solution)/shard_map/ppermute | solution.py:376
  25.0 0.0 collective-permute-done.7.c_ref
  25.0 0.2 collective-permute-done.8.d_ref
  25.2 17.1 %all_to_all.10.r_ref = f32[8,8,512]{2,1,0:T(8,128)S(1)} all-to-all(f32[8,8,512]{2,1,0:T(8,128)S(1)} %group.1), channel_id=1, replica_groups={{0,32,64,96,128,160,192,224},{8,40,72,104,136,168,200,232},{16,48,80,11..., dimensions={0} | all-to-all | bytes 262144 | tf_op jit(solution)/shard_map/all_to_all | solution.py:438
  42.3 0.8 %spread.1 = (f32[2,8,512]{2,1,0:T(8,128)S(1)}, f32[2,8,512]{2,1,0:T(8,128)S(1)}, f32[2,8,512]{2,1,0:T(8,128)S(1)}, f32[2,8,512]{2,1,0:T(8,128)S(1)}, f32[4,64,128]{2,1,0:T(8,128)}) custom-call(f32[2,8,512]{2,1,0:T(8,128)S(1)} %get-tuple-element.53.a_ref, f32[2,8,512]{2,1,0:T(8,128)S(1)} %collective-permute-done.4.b_ref, ...), custom_call_target="tpu_custom_call" | custom-call | flops 100000 | bytes 500000 | tf_op jit(solution)/shard_map/spread/pallas_call | solution.py:442
  43.1 0.0 collective-permute-done.6.x_ref
  43.1 0.1 quad.1
  43.2 4.1 %collective-permute-start.12 = (f32[16,2048]{1,0:T(8,128)S(1)}, f32[16,2048]{1,0:T(8,128)S(1)}, u32[]{:S(2)}, u32[]{:S(2)}) collective-permute-start(f32[16,2048]{1,0:T(8,128)S(1)} %get-tuple-element.69), channel_id=1, source_target_pairs={{0,4},{1,5},{2,6},{3,7},{4,0},{5,1},{6,2},{7,3},{8,12},{9,13},{10,... | collective-permute-start | bytes 393224 | tf_op jit(solution)/shard_map/ppermute | solution.py:376
  47.3 7.0 %all-to-all-start.1 = ((f32[32,8,128]{2,1,0:T(8,128)}), f32[32,8,128]{2,1,0:T(8,128)S(1)}, u32[]{:S(2)}, u32[]{:S(2)}) async-start(f32[32,8,128]{2,1,0:T(8,128)} %bitcast), calls=%async_computation.1 | async-start | bytes 262144 | tf_op jit(solution)/shard_map/all_to_all | solution.py:445
  54.2 1.5 %collective-permute-start.9 = (f32[2,8,512]{2,1,0:T(8,128)S(1)}, f32[2,8,512]{2,1,0:T(8,128)S(1)}, u32[]{:S(2)}, u32[]{:S(2)}) collective-permute-start(f32[2,8,512]{2,1,0:T(8,128)S(1)} %get-tuple-element.62), channel_id=1, source_target_pairs={{0,8},{8,0},{16,24},{24,16},{32,40},{40,32},{48,56},{56,48},{64,72... | collective-permute-start | bytes 98312 | tf_op jit(solution)/shard_map/ppermute | solution.py:376
  55.7 2.4 %collective-permute-start.10 = (f32[2,8,512]{2,1,0:T(8,128)S(1)}, f32[2,8,512]{2,1,0:T(8,128)S(1)}, u32[]{:S(2)}, u32[]{:S(2)}) collective-permute-start(f32[2,8,512]{2,1,0:T(8,128)S(1)} %get-tuple-element.63), channel_id=1, source_target_pairs={{0,16},{8,24},{16,0},{24,8},{32,48},{40,56},{48,32},{56,40},{64,80... | collective-permute-start | bytes 98312 | tf_op jit(solution)/shard_map/ppermute | solution.py:376
  58.2 0.1 collective-permute-start.11
  58.2 0.4 collective-permute-done.9.p1_ref
  58.6 2.2 %collective-permute-done.10.p2_ref = f32[2,8,512]{2,1,0:T(8,128)S(1)} collective-permute-done((f32[2,8,512]{2,1,0:T(8,128)S(1)}, f32[2,8,512]{2,1,0:T(8,128)S(1)}, u32[]{:S(2)}, u32[]{:S(2)}) %collective-permute-start.10) | collective-permute-done | bytes 32800 | tf_op jit(solution)/shard_map/ppermute | solution.py:376
  60.8 1.3 %collective-permute-done.11.p3_ref = f32[2,8,512]{2,1,0:T(8,128)S(1)} collective-permute-done((f32[2,8,512]{2,1,0:T(8,128)S(1)}, f32[2,8,512]{2,1,0:T(8,128)S(1)}, u32[]{:S(2)}, u32[]{:S(2)}) %collective-permute-start.11) | collective-permute-done | bytes 32800 | tf_op jit(solution)/shard_map/ppermute | solution.py:376
  62.1 0.1 own.1.dz_ref
  62.3 0.1 near.1.near_ref
  62.4 0.0 all-to-all-done.1.r_ref
  62.4 0.0 collective-permute-done.12.x_ref
  62.4 1.1 %final.1 = f32[16,8,2048]{2,1,0:T(8,128)} custom-call(f32[16,8,2048]{2,1,0:T(8,128)S(1)} %near.1.near_ref, f32[2,16,2048]{2,1,0:T(8,128)S(1)} %get-tuple-element.68.pre_ref, f32[16,2048]{1,0:T(8,128)S(1)} %collective-permute-done.12.x_ref, f32[32,8,128]{2,1,0:T(8,128)S(1)} %all-to-all-done.1.r_ref, f32[32,128]{1,0:T(8,128)S(1)} %get-tuple-element.59.tz_ref, ...), custom_call_target="tpu_custom_call" | custom-call | tf_op jit(solution)/shard_map/final/pallas_call | solution.py:454
  (1 shorter events, 0.0 us)
Async XLA Ops:
  0.0 8.8 %copy-start.2 = (f32[16,8,2048]{2,1,0:T(8,128)S(1)}, f32[16,8,2048]{2,1,0:T(8,128)}, u32[]{:S(2)}) copy-start(f32[16,8,2048]{2,1,0:T(8,128)} %t_hbm.1) | copy-start | bytes 3145732
  2.1 9.3 %collective-permute-start.2 = (f32[16,2048]{1,0:T(8,128)}, f32[16,2048]{1,0:T(8,128)S(1)}, u32[]{:S(2)}, u32[]{:S(2)}) collective-permute-start(f32[16,2048]{1,0:T(8,128)} %get-tuple-element.41), channel_id=1, source_target_pairs={{0,1},{1,0},{2,3},{3,2},{4,5},{5,4},{6,7},{7,6},{8,9},{9,8},{10,11... | collective-permute-start | bytes 393224 | tf_op jit(solution)/shard_map/ppermute | solution.py:393
  5.4 6.5 %collective-permute-start.3 = (f32[16,2048]{1,0:T(8,128)}, f32[16,2048]{1,0:T(8,128)S(1)}, u32[]{:S(2)}, u32[]{:S(2)}) collective-permute-start(f32[16,2048]{1,0:T(8,128)} %get-tuple-element.42), channel_id=1, source_target_pairs={{1,2},{2,1},{3,4},{4,3},{5,6},{6,5},{9,10},{10,9},{11,12},{12,11},... | collective-permute-start | bytes 393224 | tf_op jit(solution)/shard_map/ppermute | solution.py:394
  7.3 4.0 %collective-permute-start = (f32[8,2048]{1,0:T(8,128)}, f32[8,2048]{1,0:T(8,128)S(1)}, u32[]{:S(2)}, u32[]{:S(2)}) collective-permute-start(f32[8,2048]{1,0:T(8,128)} %get-tuple-element.39), channel_id=1, source_target_pairs={{0,8},{8,0},{16,24},{24,16},{32,40},{40,32},{48,56},{56,48},{64,72... | collective-permute-start | bytes 196616 | tf_op jit(solution)/shard_map/ppermute | solution.py:391
  8.1 3.3 %collective-permute-start.1 = (f32[8,2048]{1,0:T(8,128)}, f32[8,2048]{1,0:T(8,128)S(1)}, u32[]{:S(2)}, u32[]{:S(2)}) collective-permute-start(f32[8,2048]{1,0:T(8,128)} %get-tuple-element.40), channel_id=1, source_target_pairs={{8,16},{16,8},{24,32},{32,24},{40,48},{48,40},{56,64},{64,56},{72,... | collective-permute-start | bytes 196616 | tf_op jit(solution)/shard_map/ppermute | solution.py:392
  8.8 1.4 %copy-start = (bf16[3,16,8,2048]{3,2,1,0:T(8,128)(2,1)S(1)}, bf16[3,16,8,2048]{3,2,1,0:T(8,128)(2,1)}, u32[]{:S(2)}) copy-start(bf16[3,16,8,2048]{3,2,1,0:T(8,128)(2,1)} %v_ref.3) | copy-start | bytes 4718596
  10.2 1.7 %copy-start.1 = (bf16[3,16,8,2048]{3,2,1,0:T(8,128)(2,1)S(1)}, bf16[3,16,8,2048]{3,2,1,0:T(8,128)(2,1)}, u32[]{:S(2)}) copy-start(bf16[3,16,8,2048]{3,2,1,0:T(8,128)(2,1)} %v_ref.3) | copy-start | bytes 4718596
  12.8 4.7 %collective-permute-start.4 = (f32[2,8,512]{2,1,0:T(8,128)S(1)}, f32[2,8,512]{2,1,0:T(8,128)S(1)}, u32[]{:S(2)}, u32[]{:S(2)}) collective-permute-start(f32[2,8,512]{2,1,0:T(8,128)S(1)} %get-tuple-element.50), channel_id=1, source_target_pairs={{0,8},{8,0},{16,24},{24,16},{32,40},{40,32},{48,56},{56,48},{64,72... | collective-permute-start | bytes 98312 | tf_op jit(solution)/shard_map/ppermute | solution.py:376
  17.5 4.6 %collective-permute-start.5 = (f32[2,16,2048]{2,1,0:T(8,128)S(1)}, f32[2,16,2048]{2,1,0:T(8,128)S(1)}, u32[]{:S(2)}, u32[]{:S(2)}) collective-permute-start(f32[2,16,2048]{2,1,0:T(8,128)S(1)} %get-tuple-element.51.cs_ref), channel_id=1, source_target_pairs={{0,1},{1,0},{2,3},{3,2},{4,5},{5,4},{6,7},{7,6},{8,9},{9,8},{10,11... | collective-permute-start | bytes 786440 | tf_op jit(solution)/shard_map/ppermute | solution.py:376
  17.9 7.0 %collective-permute-start.7 = (f32[2,8,512]{2,1,0:T(8,128)S(1)}, f32[2,8,512]{2,1,0:T(8,128)S(1)}, u32[]{:S(2)}, u32[]{:S(2)}) collective-permute-start(f32[2,8,512]{2,1,0:T(8,128)S(1)} %get-tuple-element.55), channel_id=1, source_target_pairs={{0,16},{8,24},{16,0},{24,8},{32,48},{40,56},{48,32},{56,40},{64,80... | collective-permute-start | bytes 98312 | tf_op jit(solution)/shard_map/ppermute | solution.py:376
  21.2 4.0 %collective-permute-start.8 = (f32[2,8,512]{2,1,0:T(8,128)S(1)}, f32[2,8,512]{2,1,0:T(8,128)S(1)}, u32[]{:S(2)}, u32[]{:S(2)}) collective-permute-start(f32[2,8,512]{2,1,0:T(8,128)S(1)} %get-tuple-element.56), channel_id=1, source_target_pairs={{0,24},{8,16},{16,8},{24,0},{32,56},{40,48},{48,40},{56,32},{64,88... | collective-permute-start | bytes 98312 | tf_op jit(solution)/shard_map/ppermute | solution.py:376
  22.2 20.9 %collective-permute-start.6 = (f32[2,16,2048]{2,1,0:T(8,128)S(1)}, f32[2,16,2048]{2,1,0:T(8,128)S(1)}, u32[]{:S(2)}, u32[]{:S(2)}) collective-permute-start(f32[2,16,2048]{2,1,0:T(8,128)S(1)} %get-tuple-element.65.tot_ref), channel_id=1, source_target_pairs={{0,2},{1,3},{2,0},{3,1},{4,6},{5,7},{6,4},{7,5},{8,10},{9,11},{10,... | collective-permute-start | bytes 786440 | tf_op jit(solution)/shard_map/ppermute | solution.py:376
  43.2 19.2 %collective-permute-start.12 = (f32[16,2048]{1,0:T(8,128)S(1)}, f32[16,2048]{1,0:T(8,128)S(1)}, u32[]{:S(2)}, u32[]{:S(2)}) collective-permute-start(f32[16,2048]{1,0:T(8,128)S(1)} %get-tuple-element.69), channel_id=1, source_target_pairs={{0,4},{1,5},{2,6},{3,7},{4,0},{5,1},{6,2},{7,3},{8,12},{9,13},{10,... | collective-permute-start | bytes 393224 | tf_op jit(solution)/shard_map/ppermute | solution.py:376
  47.3 15.2 %all-to-all-start.1 = ((f32[32,8,128]{2,1,0:T(8,128)}), f32[32,8,128]{2,1,0:T(8,128)S(1)}, u32[]{:S(2)}, u32[]{:S(2)}) async-start(f32[32,8,128]{2,1,0:T(8,128)} %bitcast), calls=%async_computation.1 | async-start | bytes 262144 | tf_op jit(solution)/shard_map/all_to_all | solution.py:445
  54.2 4.4 %collective-permute-start.9 = (f32[2,8,512]{2,1,0:T(8,128)S(1)}, f32[2,8,512]{2,1,0:T(8,128)S(1)}, u32[]{:S(2)}, u32[]{:S(2)}) collective-permute-start(f32[2,8,512]{2,1,0:T(8,128)S(1)} %get-tuple-element.62), channel_id=1, source_target_pairs={{0,8},{8,0},{16,24},{24,16},{32,40},{40,32},{48,56},{56,48},{64,72... | collective-permute-start | bytes 98312 | tf_op jit(solution)/shard_map/ppermute | solution.py:376
  55.7 5.1 %collective-permute-start.10 = (f32[2,8,512]{2,1,0:T(8,128)S(1)}, f32[2,8,512]{2,1,0:T(8,128)S(1)}, u32[]{:S(2)}, u32[]{:S(2)}) collective-permute-start(f32[2,8,512]{2,1,0:T(8,128)S(1)} %get-tuple-element.63), channel_id=1, source_target_pairs={{0,16},{8,24},{16,0},{24,8},{32,48},{40,56},{48,32},{56,40},{64,80... | collective-permute-start | bytes 98312 | tf_op jit(solution)/shard_map/ppermute | solution.py:376
  58.2 4.0 %collective-permute-start.11 = (f32[2,8,512]{2,1,0:T(8,128)S(1)}, f32[2,8,512]{2,1,0:T(8,128)S(1)}, u32[]{:S(2)}, u32[]{:S(2)}) collective-permute-start(f32[2,8,512]{2,1,0:T(8,128)S(1)} %get-tuple-element.64), channel_id=1, source_target_pairs={{0,24},{8,16},{16,8},{24,0},{32,56},{40,48},{48,40},{56,32},{64,88... | collective-permute-start | bytes 98312 | tf_op jit(solution)/shard_map/ppermute | solution.py:376
